TPU v7x, 256 devices: a whole 4x4x8 slice. The times are simulated.
256 devices in a mesh: view: 8 (over z_hi, core), gz: 32 (over z_lo, y, x).
Axes of the slice: x: 4, y: 4, z: 8 (z_hi: 4, z_lo: 2; z = z_hi * 2 + z_lo), core: 2. Of those that a mesh axis runs over, the one named last changes fastest.
Arguments:
- estimate: float32 [1536, 128, 128], P('gz'), may hold values from 0.5 to 2
- measured: float32 [8, 1536, 128, 128], P('view', 'gz'), may hold values from 0.3 to 3
- lateral_x: float32 [8, 128, 128], P('view'), may hold values from 0 to 0.5, as said below
- lateral_y: float32 [8, 128, 128], P('view'), may hold values from 0 to 0.5, as said below
- depth_taps: float32 [8, 33], P('view'), may hold values from 0.01 to 0.06
Outputs:
- updated: float32 [1536, 128, 128], P('gz')
Inputs may be any that keep to these rules, and one draw needn't show every extreme that they name: `lateral_x`: nonnegative entries. `lateral_y`: nonnegative entries.
All inputs are finite; a program needn't handle non-finite values.
Results may differ from a plain program's by a relative error of at most 0.0001.
Values sent between devices are 32-bit elements; how exact they have to be, the bound alone decides.
No kernel may reach another device: no remote copies, remote signals or barrier semaphores. Data moves between devices by JAX's collectives and lax.ppermute only.
A program may use at most 64 MiB of HBM per device.

v0:
```python
import jax
import jax.numpy as jnp
from jax import lax
from jax.sharding import PartitionSpec as P

DEPTH = 33
HALF = 16
ITERS = 2


def with_halo(x, sides, width):
    for axis, dim in sides:
        devices, length = (lax.axis_size(axis), x.shape[dim])
        up = [(i, (i + 1) % devices) for i in range(devices - 1)]
        down = [(j, i) for i, j in up]
        last = lax.slice_in_dim(x, length - width, length, axis=dim)
        first = lax.slice_in_dim(x, 0, width, axis=dim)
        before = lax.ppermute(last, axis, up)
        after = lax.ppermute(first, axis, down)
        x = jnp.concatenate([before, x, after], axis=dim)
    return x


def lateral_forward(field, across, along):
    step = jnp.einsum("zxy,ax->zay", field, across, precision=lax.Precision.HIGHEST)
    return jnp.einsum("zay,by->zab", step, along, precision=lax.Precision.HIGHEST)


def lateral_adjoint(field, across, along):
    step = jnp.einsum("zab,ax->zxb", field, across, precision=lax.Precision.HIGHEST)
    return jnp.einsum("zxb,by->zxy", step, along, precision=lax.Precision.HIGHEST)


def depth_blur(padded, taps, count):
    total = jnp.zeros((count,) + padded.shape[1:], jnp.float32)
    for shift in range(DEPTH):
        total = total + taps[shift] * padded[shift : shift + count]
    return total


def depth_adjoint(padded, taps, count):
    total = jnp.zeros((count,) + padded.shape[1:], jnp.float32)
    for shift in range(DEPTH):
        begin = 2 * HALF - shift
        total = total + taps[shift] * padded[begin : begin + count]
    return total


def on_device(estimate, measured, lateral_x, lateral_y, depth_taps):
    count = estimate.shape[0]
    views = lax.axis_size("view")
    recorded = measured[0]
    across = lateral_x[0]
    along = lateral_y[0]
    taps = depth_taps[0]
    updated = estimate
    for update in range(ITERS):
        smooth = lateral_forward(updated, across, along)
        padded = with_halo(smooth, (("gz", 0),), HALF)
        blurred = depth_blur(padded, taps, count)
        ratio_wide = with_halo(recorded / blurred, (("gz", 0),), HALF)
        factor = lateral_adjoint(depth_adjoint(ratio_wide, taps, count), across, along)
        logs = jnp.log(factor)
        updated = updated * jnp.exp(lax.psum(logs, "view") / views)
    return updated


def solution(mesh):
    return jax.shard_map(
        on_device,
        mesh=mesh,
        in_specs=(
            P("gz", None, None),
            P("view", "gz", None, None),
            P("view", None, None),
            P("view", None, None),
            P("view", None),
        ),
        out_specs=P("gz", None, None),
        check_vma=False,
    )
```

profile of v0, /device:TPU:33, one launch (start us, length us, event | category | flops | bytes accessed | tf_op | source)
XLA Modules:
  0.0 513.4 jit_solution(8047043891959387970)
XLA Ops:
  6.5 0.0 copy-start
  6.5 0.0 all-reduce.3.cloned.1.call-start
  6.5 0.8 copy-done
  7.4 4.7 fusion.538
  12.1 0.0 copy-done.4
  12.1 2.7 fusion.454
  14.9 0.0 copy-start.5
  14.9 0.0 copy-start.2
  14.9 0.2 fusion.546
  15.1 3.2 collective-permute-start
  18.3 6.4 %collective-permute-start.1 = (f32[16,128,128]{2,1,0:T(8,128)S(1)}, f32[16,128,128]{2,1,0:T(8,128)S(1)}, u32[]{:S(2)}, u32[]{:S(2)}) collective-permute-start(f32[16,128,128]{2,1,0:T(8,128)S(1)} %get-tuple-element.12), channel_id=1, source_target_pairs={{1,0},{2,1},{3,2},{4,3},{5,4},{6,5},{7,6},{8,7},{9,8},{10,9},{11,1... | collective-permute-start | bytes 3145736 | tf_op jit(solution)/shard_map/ppermute | solution.py:19
  24.7 0.7 fusion.548
  25.5 0.7 fusion.547
  26.2 19.2 %collective-permute-done = f32[16,128,128]{2,1,0:T(8,128)S(1)} collective-permute-done((f32[16,128,128]{2,1,0:T(8,128)S(1)}, f32[16,128,128]{2,1,0:T(8,128)S(1)}, u32[]{:S(2)}, u32[]{:S(2)}) %collective-permute-start) | collective-permute-done | bytes 1048608 | tf_op jit(solution)/shard_map/ppermute | solution.py:18
  45.4 0.9 collective-permute-done.1
  46.2 35.0 %fusion.343 = f32[48,128,128]{2,1,0:T(8,128)S(1)} fusion(f32[48,128,128]{2,1,0:T(8,128)S(1)} %fusion.454, f32[16,128,128]{2,1,0:T(8,128)S(1)} %collective-permute-done.1, f32[16,128,128]{2,1,0:T(8,128)S(1)} %collective-permute-done, f32[1,48,128,128]{3,2,1,0:T(8,128)S(1)} %copy-done.2, f32[]{:T(128)} %bitcast.38, f32[]{:T(128)} %bitcast.37, f32[]{:T(128)} %bitcast.36, ...), kind=kLoop, calls=%fused_computation.523 | loop fusion | flops 77070336 | bytes 11534468 | tf_op jit(solution)/shard_map/div | solution.py:61
  81.3 0.1 fusion.545
  81.4 8.3 %collective-permute-start.2 = (f32[16,128,128]{2,1,0:T(8,128)S(1)}, f32[16,128,128]{2,1,0:T(8,128)S(1)}, u32[]{:S(2)}, u32[]{:S(2)}) collective-permute-start(f32[16,128,128]{2,1,0:T(8,128)S(1)} %get-tuple-element.9), channel_id=1, source_target_pairs={{1,0},{2,1},{3,2},{4,3},{5,4},{6,5},{7,6},{8,7},{9,8},{10,9},{11,1... | collective-permute-start | bytes 3145736 | tf_op jit(solution)/shard_map/ppermute | solution.py:19
  89.7 2.1 collective-permute-start.3
  91.8 18.5 %collective-permute-done.2 = f32[16,128,128]{2,1,0:T(8,128)S(1)} collective-permute-done((f32[16,128,128]{2,1,0:T(8,128)S(1)}, f32[16,128,128]{2,1,0:T(8,128)S(1)}, u32[]{:S(2)}, u32[]{:S(2)}) %collective-permute-start.2) | collective-permute-done | bytes 1048608 | tf_op jit(solution)/shard_map/ppermute | solution.py:19
  110.3 8.1 %collective-permute-done.3 = f32[16,128,128]{2,1,0:T(8,128)S(1)} collective-permute-done((f32[16,128,128]{2,1,0:T(8,128)S(1)}, f32[16,128,128]{2,1,0:T(8,128)S(1)}, u32[]{:S(2)}, u32[]{:S(2)}) %collective-permute-start.3) | collective-permute-done | bytes 1048608 | tf_op jit(solution)/shard_map/ppermute | solution.py:18
  118.4 34.1 %fusion.555 = f32[48,128,128]{2,1,0:T(8,128)S(1)} fusion(f32[48,128,128]{2,1,0:T(8,128)S(1)} %fusion.343, f32[16,128,128]{2,1,0:T(8,128)S(1)} %collective-permute-done.3, f32[16,128,128]{2,1,0:T(8,128)S(1)} %collective-permute-done.2, f32[]{:T(128)} %bitcast.38, f32[]{:T(128)} %bitcast.37, f32[]{:T(128)} %bitcast.36, f32[]{:T(128)} %bitcast.35, ...), kind=kLoop, calls=%fused_computation.429.clone.clone | loop fusion | flops 76283904 | bytes 8388740 | tf_op jit(solution)/shard_map/zab,ax->zxb/dot_general | solution.py:30
  152.4 3.1 fusion.220
  155.5 4.3 fusion.458
  159.8 0.0 all-reduce.3.cloned.1.call-update
  159.8 0.3 all-reduce.5.cloned.1.call-start
  160.1 94.7 %all-reduce.3.cloned.1.call-done = f32[48,128,128]{2,1,0:T(8,128)} async-done(((f32[48,128,128]{2,1,0:T(8,128)}), f32[48,128,128]{2,1,0:T(8,128)}) %all-reduce.3.cloned.1.call-update) | async-done | bytes 3145744 | tf_op jit(solution)/shard_map/psum | solution.py:64
  254.8 5.4 %fusion.530 = f32[48,128,128]{1,2,0:T(8,128)S(1)} fusion(f32[48,128,128]{2,1,0:T(8,128)S(1)} %copy-done.1, f32[48,128,128]{2,1,0:T(8,128)} %all-reduce.3.cloned.1.call-done, f32[1,128,128]{2,1,0:T(8,128)S(1)} %copy-done), kind=kOutput, calls=%fused_computation.712 | convolution fusion | flops 1209532416 | bytes 9502720 | tf_op jit(solution)/shard_map/zxy,ax->zay/dot_general | solution.py:25
  260.2 2.7 fusion.450
  262.9 0.0 copy-start.3
  262.9 0.2 fusion.544
  263.1 3.6 collective-permute-start.4
  266.7 6.0 %collective-permute-start.5 = (f32[16,128,128]{2,1,0:T(8,128)S(1)}, f32[16,128,128]{2,1,0:T(8,128)S(1)}, u32[]{:S(2)}, u32[]{:S(2)}) collective-permute-start(f32[16,128,128]{2,1,0:T(8,128)S(1)} %get-tuple-element.8), channel_id=1, source_target_pairs={{1,0},{2,1},{3,2},{4,3},{5,4},{6,5},{7,6},{8,7},{9,8},{10,9},{11,1... | collective-permute-start | bytes 3145736 | tf_op jit(solution)/shard_map/ppermute | solution.py:19
  272.8 19.0 %collective-permute-done.4 = f32[16,128,128]{2,1,0:T(8,128)S(1)} collective-permute-done((f32[16,128,128]{2,1,0:T(8,128)S(1)}, f32[16,128,128]{2,1,0:T(8,128)S(1)}, u32[]{:S(2)}, u32[]{:S(2)}) %collective-permute-start.4) | collective-permute-done | bytes 1048608 | tf_op jit(solution)/shard_map/ppermute | solution.py:18
  291.8 1.1 collective-permute-done.5
  292.8 0.0 copy-done.3
  292.8 35.2 %fusion.127 = f32[48,128,128]{2,1,0:T(8,128)S(1)} fusion(f32[48,128,128]{2,1,0:T(8,128)S(1)} %fusion.450, f32[16,128,128]{2,1,0:T(8,128)S(1)} %collective-permute-done.5, f32[16,128,128]{2,1,0:T(8,128)S(1)} %collective-permute-done.4, f32[1,48,128,128]{3,2,1,0:T(8,128)S(1)} %copy-done.3, f32[]{:T(128)} %bitcast.38, f32[]{:T(128)} %bitcast.37, f32[]{:T(128)} %bitcast.36, ...), kind=kLoop, calls=%fused_computation.337 | loop fusion | flops 77070336 | bytes 11534468 | tf_op jit(solution)/shard_map/div | solution.py:61
  328.1 0.2 fusion.543
  328.3 8.2 %collective-permute-start.6 = (f32[16,128,128]{2,1,0:T(8,128)S(1)}, f32[16,128,128]{2,1,0:T(8,128)S(1)}, u32[]{:S(2)}, u32[]{:S(2)}) collective-permute-start(f32[16,128,128]{2,1,0:T(8,128)S(1)} %get-tuple-element.5), channel_id=1, source_target_pairs={{1,0},{2,1},{3,2},{4,3},{5,4},{6,5},{7,6},{8,7},{9,8},{10,9},{11,1... | collective-permute-start | bytes 3145736 | tf_op jit(solution)/shard_map/ppermute | solution.py:19
  336.5 2.2 collective-permute-start.7
  338.6 16.8 %collective-permute-done.6 = f32[16,128,128]{2,1,0:T(8,128)S(1)} collective-permute-done((f32[16,128,128]{2,1,0:T(8,128)S(1)}, f32[16,128,128]{2,1,0:T(8,128)S(1)}, u32[]{:S(2)}, u32[]{:S(2)}) %collective-permute-start.6) | collective-permute-done | bytes 1048608 | tf_op jit(solution)/shard_map/ppermute | solution.py:19
  355.4 8.1 %collective-permute-done.7 = f32[16,128,128]{2,1,0:T(8,128)S(1)} collective-permute-done((f32[16,128,128]{2,1,0:T(8,128)S(1)}, f32[16,128,128]{2,1,0:T(8,128)S(1)}, u32[]{:S(2)}, u32[]{:S(2)}) %collective-permute-start.7) | collective-permute-done | bytes 1048608 | tf_op jit(solution)/shard_map/ppermute | solution.py:18
  363.5 34.2 %fusion.553 = f32[48,128,128]{2,1,0:T(8,128)S(1)} fusion(f32[48,128,128]{2,1,0:T(8,128)S(1)} %fusion.127, f32[16,128,128]{2,1,0:T(8,128)S(1)} %collective-permute-done.7, f32[16,128,128]{2,1,0:T(8,128)S(1)} %collective-permute-done.6, f32[]{:T(128)} %bitcast.38, f32[]{:T(128)} %bitcast.37, f32[]{:T(128)} %bitcast.36, f32[]{:T(128)} %bitcast.35, ...), kind=kLoop, calls=%fused_computation.243.clone.clone.1 | loop fusion | flops 76283904 | bytes 8388740 | tf_op jit(solution)/shard_map/zab,ax->zxb/dot_general | solution.py:30
  397.7 3.1 fusion.4
  400.7 4.3 fusion.461
  405.0 0.0 all-reduce.5.cloned.1.call-update
  405.0 95.9 %all-reduce.5.cloned.1.call-done = f32[48,128,128]{2,1,0:T(8,128)} async-done(((f32[48,128,128]{2,1,0:T(8,128)}), f32[48,128,128]{2,1,0:T(8,128)}) %all-reduce.5.cloned.1.call-update) | async-done | bytes 3145744 | tf_op jit(solution)/shard_map/psum | solution.py:64
  501.0 5.6 %exponential_multiply_fusion = f32[48,128,128]{2,1,0:T(8,128)} fusion(f32[48,128,128]{2,1,0:T(8,128)} %all-reduce.5.cloned.1.call-done, f32[48,128,128]{2,1,0:T(8,128)S(1)} %copy-done.1, f32[48,128,128]{2,1,0:T(8,128)} %all-reduce.3.cloned.1.call-done), kind=kLoop, calls=%fused_computation.640 | loop fusion | flops 3145728 | bytes 12582912 | tf_op jit(solution)/shard_map/mul | solution.py:64
  (5 shorter events, 0.0 us)
Async XLA Ops:
  6.5 0.8 copy-start
  6.5 5.6 %copy-start.4 = (f32[1,128,128]{2,1,0:T(8,128)S(1)}, f32[1,128,128]{2,1,0:T(8,128)}, u32[]{:S(2)}) copy-start(f32[1,128,128]{2,1,0:T(8,128)} %param.8) | copy-start | bytes 196612
  6.5 248.2 %all-reduce.3.cloned.1.call-start = ((), (), s32[]{:S(2)}) async-start(), calls=%async_computation | async-start | bytes 6291456 | tf_op jit(solution)/shard_map/psum | solution.py:64
  14.9 9.9 %copy-start.5 = (f32[1,33]{1,0:T(1,128)S(1)}, f32[1,33]{1,0:T(1,128)}, u32[]{:S(2)}) copy-start(f32[1,33]{1,0:T(1,128)} %param.9) | copy-start | bytes 400
  14.9 31.3 %copy-start.2 = (f32[1,48,128,128]{3,2,1,0:T(8,128)S(1)}, f32[1,48,128,128]{3,2,1,0:T(8,128)}, u32[]{:S(2)}) copy-start(f32[1,48,128,128]{3,2,1,0:T(8,128)} %param.6) | copy-start | bytes 9437188
  15.1 30.3 %collective-permute-start = (f32[16,128,128]{2,1,0:T(8,128)S(1)}, f32[16,128,128]{2,1,0:T(8,128)S(1)}, u32[]{:S(2)}, u32[]{:S(2)}) collective-permute-start(f32[16,128,128]{2,1,0:T(8,128)S(1)} %get-tuple-element.11), channel_id=1, source_target_pairs={{0,1},{1,2},{2,3},{3,4},{4,5},{5,6},{6,7},{7,8},{8,9},{9,10},{10,1... | collective-permute-start | bytes 3145736 | tf_op jit(solution)/shard_map/ppermute | solution.py:18
  18.3 27.9 %collective-permute-start.1 = (f32[16,128,128]{2,1,0:T(8,128)S(1)}, f32[16,128,128]{2,1,0:T(8,128)S(1)}, u32[]{:S(2)}, u32[]{:S(2)}) collective-permute-start(f32[16,128,128]{2,1,0:T(8,128)S(1)} %get-tuple-element.12), channel_id=1, source_target_pairs={{1,0},{2,1},{3,2},{4,3},{5,4},{6,5},{7,6},{8,7},{9,8},{10,9},{11,1... | collective-permute-start | bytes 3145736 | tf_op jit(solution)/shard_map/ppermute | solution.py:19
  81.4 28.9 %collective-permute-start.2 = (f32[16,128,128]{2,1,0:T(8,128)S(1)}, f32[16,128,128]{2,1,0:T(8,128)S(1)}, u32[]{:S(2)}, u32[]{:S(2)}) collective-permute-start(f32[16,128,128]{2,1,0:T(8,128)S(1)} %get-tuple-element.9), channel_id=1, source_target_pairs={{1,0},{2,1},{3,2},{4,3},{5,4},{6,5},{7,6},{8,7},{9,8},{10,9},{11,1... | collective-permute-start | bytes 3145736 | tf_op jit(solution)/shard_map/ppermute | solution.py:19
  89.7 28.6 %collective-permute-start.3 = (f32[16,128,128]{2,1,0:T(8,128)S(1)}, f32[16,128,128]{2,1,0:T(8,128)S(1)}, u32[]{:S(2)}, u32[]{:S(2)}) collective-permute-start(f32[16,128,128]{2,1,0:T(8,128)S(1)} %get-tuple-element.10), channel_id=1, source_target_pairs={{0,1},{1,2},{2,3},{3,4},{4,5},{5,6},{6,7},{7,8},{8,9},{9,10},{10,1... | collective-permute-start | bytes 3145736 | tf_op jit(solution)/shard_map/ppermute | solution.py:18
  159.8 95.0 %copy-start.1 = (f32[48,128,128]{2,1,0:T(8,128)S(1)}, f32[48,128,128]{2,1,0:T(8,128)}, u32[]{:S(2)}) copy-start(f32[48,128,128]{2,1,0:T(8,128)} %param.5) | copy-start | bytes 9437188
  159.8 341.2 %all-reduce.5.cloned.1.call-start = ((), (), s32[]{:S(2)}) async-start(), calls=%async_computation.1 | async-start | bytes 6291456 | tf_op jit(solution)/shard_map/psum | solution.py:64
  262.9 29.9 %copy-start.3 = (f32[1,48,128,128]{3,2,1,0:T(8,128)S(1)}, f32[1,48,128,128]{3,2,1,0:T(8,128)}, u32[]{:S(2)}) copy-start(f32[1,48,128,128]{3,2,1,0:T(8,128)} %param.6) | copy-start | bytes 9437188
  263.1 28.6 %collective-permute-start.4 = (f32[16,128,128]{2,1,0:T(8,128)S(1)}, f32[16,128,128]{2,1,0:T(8,128)S(1)}, u32[]{:S(2)}, u32[]{:S(2)}) collective-permute-start(f32[16,128,128]{2,1,0:T(8,128)S(1)} %get-tuple-element.7), channel_id=1, source_target_pairs={{0,1},{1,2},{2,3},{3,4},{4,5},{5,6},{6,7},{7,8},{8,9},{9,10},{10,1... | collective-permute-start | bytes 3145736 | tf_op jit(solution)/shard_map/ppermute | solution.py:18
  266.7 26.1 %collective-permute-start.5 = (f32[16,128,128]{2,1,0:T(8,128)S(1)}, f32[16,128,128]{2,1,0:T(8,128)S(1)}, u32[]{:S(2)}, u32[]{:S(2)}) collective-permute-start(f32[16,128,128]{2,1,0:T(8,128)S(1)} %get-tuple-element.8), channel_id=1, source_target_pairs={{1,0},{2,1},{3,2},{4,3},{5,4},{6,5},{7,6},{8,7},{9,8},{10,9},{11,1... | collective-permute-start | bytes 3145736 | tf_op jit(solution)/shard_map/ppermute | solution.py:19
  328.3 27.1 %collective-permute-start.6 = (f32[16,128,128]{2,1,0:T(8,128)S(1)}, f32[16,128,128]{2,1,0:T(8,128)S(1)}, u32[]{:S(2)}, u32[]{:S(2)}) collective-permute-start(f32[16,128,128]{2,1,0:T(8,128)S(1)} %get-tuple-element.5), channel_id=1, source_target_pairs={{1,0},{2,1},{3,2},{4,3},{5,4},{6,5},{7,6},{8,7},{9,8},{10,9},{11,1... | collective-permute-start | bytes 3145736 | tf_op jit(solution)/shard_map/ppermute | solution.py:19
  336.5 27.0 %collective-permute-start.7 = (f32[16,128,128]{2,1,0:T(8,128)S(1)}, f32[16,128,128]{2,1,0:T(8,128)S(1)}, u32[]{:S(2)}, u32[]{:S(2)}) collective-permute-start(f32[16,128,128]{2,1,0:T(8,128)S(1)} %get-tuple-element.6), channel_id=1, source_target_pairs={{0,1},{1,2},{2,3},{3,4},{4,5},{5,6},{6,7},{7,8},{8,9},{9,10},{10,1... | collective-permute-start | bytes 3145736 | tf_op jit(solution)/shard_map/ppermute | solution.py:18
Sparse Core Ops, SparseCore 0:
  159.9 94.8 all-reduce.2
  405.2 95.7 all-reduce.4
where the time goes:
time: 518 us; the launch traced here: 513 us
  waiting for transfers between devices  282 us (54%)
  other arithmetic  144 us (28%)
  starting transfers between devices  40.3 us (8%)
  matrix products  30.3 us (6%)
  between operations  13.6 us (3%)
    psum x2, waiting for transfers between devices, on_device(): updated = updated * jnp.exp(lax.psum(logs, 'view') / views)  191 us
    div x2, other arithmetic, on_device(): ratio_wide = with_halo(recorded / blurred, (('gz', 0),), HALF)  70.2 us
    dot_general x2, other arithmetic, lateral_adjoint(): jnp.einsum('zab,ax->zxb', field, across, precision=lax.Precision.HIGHEST)  68.2 us
    ppermute x4, waiting for transfers between devices, with_halo(): before = lax.ppermute(last, axis, up)  54.3 us
    ppermute x4, waiting for transfers between devices, with_halo(): after = lax.ppermute(first, axis, down)  37.2 us
    ppermute x4, starting transfers between devices, with_halo(): after = lax.ppermute(first, axis, down)  28.9 us
    ppermute x4, starting transfers between devices, with_halo(): before = lax.ppermute(last, axis, up)  11.1 us
  transfers between devices with their start and end apart: 10, of which 10 were waited for; matrix products, arithmetic and copies ran while one was open for 0% of the time, Pallas kernels for 0%

commit v1 on v0

v1 whole, which is shorter than its diff:
```python
import jax
import jax.numpy as jnp
from jax import lax
from jax.experimental import pallas as pl
from jax.experimental.pallas import tpu as pltpu
from jax.sharding import PartitionSpec as P

DEPTH = 33
HALF = 16
N = 128
SLAB = 48
FAR = 2 * HALF
F32 = jnp.float32
BF16 = jnp.bfloat16
MIB = 1024 * 1024


def split(x):
    hi = x.astype(BF16)
    return hi, (x - hi.astype(F32)).astype(BF16)


def split_matrix(m):
    hi = lax.reduce_precision(m, 8, 7)
    return hi.astype(BF16), lax.reduce_precision(m - hi, 8, 7).astype(BF16)


def left_operand(m):
    hi, lo = split_matrix(m)
    return jnp.concatenate([jnp.concatenate([hi, hi], 1), jnp.concatenate([lo, lo], 1)], 0)


def right_operand(m):
    hi, lo = split_matrix(m)
    return jnp.concatenate([jnp.concatenate([hi, lo], 1), jnp.concatenate([hi, lo], 1)], 0)


def left_product(operand, x):
    hi, lo = split(x)
    out = jnp.dot(operand, jnp.concatenate([hi, lo], 0), preferred_element_type=F32)
    rows = operand.shape[0] // 2
    return out[:rows] + out[rows:]


def right_product(x, operand):
    hi, lo = split(x)
    out = jnp.dot(jnp.concatenate([hi, lo], 1), operand, preferred_element_type=F32)
    cols = operand.shape[1] // 2
    return out[:, :cols] + out[:, cols:]


def two_sided(planes, left, right):
    both = left_product(left, jnp.concatenate(planes, 1))
    rows = jnp.concatenate([both[:, :N], both[:, N:]], 0)
    return right_product(rows, right)


def region_plane(refs, z):
    blocks = []
    for ref in refs:
        if len(ref.shape) == 3:
            blocks.append(ref[z])
        else:
            blocks.extend(ref[p, z] for p in range(ref.shape[0]))
    return jnp.concatenate(blocks, 0) if len(blocks) > 1 else blocks[0]


def lateral_kernel(counts, *refs):
    total = sum(c for c, _ in counts)
    ins, (left_ref, right_ref), outs = refs[:total], refs[total : total + 2], refs[total + 2 :]
    left = left_ref[...]
    right = right_ref[...]
    at = 0
    for (count, planes), out in zip(counts, outs):
        region = ins[at : at + count]
        at += count

        @pl.loop(0, planes // 4)
        def _(i, region=region, out=out):
            for j in range(2):
                z = 4 * i + 2 * j
                res = two_sided([region_plane(region, z), region_plane(region, z + 1)], left, right)
                out[pl.ds(pl.multiple_of(z * N, 2 * N), 2 * N), :] = res


def lateral(regions, left, right):
    counts = []
    ins = []
    for region in regions:
        ref = region[0]
        counts.append((len(region), ref.shape[0] if ref.ndim == 3 else ref.shape[1]))
        ins.extend(region)
    planes = sum(p for _, p in counts)
    return pl.pallas_call(
        lambda *refs: lateral_kernel(counts, *refs),
        out_shape=[jax.ShapeDtypeStruct((p * N, N), F32) for _, p in counts],
        in_specs=[pl.BlockSpec(memory_space=pltpu.VMEM)] * (len(ins) + 2),
        out_specs=[pl.BlockSpec(memory_space=pltpu.VMEM)] * len(counts),
        compiler_params=pltpu.CompilerParams(vmem_limit_bytes=20 * MIB),
        cost_estimate=pl.CostEstimate(flops=planes * 16 * N**3, bytes_accessed=planes * 8 * N * N, transcendentals=0),
        name="lateral",
    )(*ins, left, right)


def middle_kernel(sb, so, sa, mb, mo, ma, tf_ref, ta_ref, left_ref, right_ref, own, other, back):
    tf = tf_ref[...]
    ta = ta_ref[...]

    def rows(refs, a):
        return jnp.concatenate([r[pl.ds(a, r.shape[0] // N, stride=N), :] for r in refs], 0)

    def pair(refs, a):
        return jnp.concatenate([rows(refs, a), rows(refs, a + 1)], 1)

    @pl.loop(0, N // 4)
    def _(i):
        for j in range(2):
            a = 4 * i + 2 * j
            blurred = left_product(tf, pair((sb, so, sa), a))
            recorded = pair((mb, mo, ma), a)
            ratio = jnp.where(recorded > 0, recorded / blurred, 0.0)
            res = left_product(ta, ratio)
            back[pl.ds(a, SLAB, stride=N), :] = res[:, :N]
            back[pl.ds(a + 1, SLAB, stride=N), :] = res[:, N:]

    left = left_ref[...]
    right = right_ref[...]

    @pl.loop(0, SLAB // 4)
    def _(i):
        for j in range(2):
            z = 4 * i + 2 * j
            at = pl.multiple_of(z * N, 2 * N)
            logs = jnp.log(two_sided([back[pl.ds(at, N), :], back[pl.ds(at + N, N), :]], left, right))
            for k in range(2):
                for p in range(8):
                    own[p, z + k] = logs[k * N + 8 * p : k * N + 8 * p + 8]
                    other[p, z + k] = logs[k * N + 64 + 8 * p : k * N + 64 + 8 * p + 8]


def middle(smooth, recorded, tf, ta, left, right):
    ins = [*smooth, *[r.reshape(-1, N) for r in recorded], tf, ta, left, right]
    half = jax.ShapeDtypeStruct((8, SLAB, 8, N), F32)
    return pl.pallas_call(
        middle_kernel,
        out_shape=[half, half],
        in_specs=[pl.BlockSpec(memory_space=pltpu.VMEM)] * len(ins),
        out_specs=[pl.BlockSpec(memory_space=pltpu.VMEM)] * 2,
        scratch_shapes=[pltpu.VMEM((SLAB * N, N), F32)],
        compiler_params=pltpu.CompilerParams(vmem_limit_bytes=28 * MIB),
        cost_estimate=pl.CostEstimate(flops=8 * 10**9, bytes_accessed=15 * MIB, transcendentals=SLAB * N * N),
        name="middle",
    )(*ins)


def place_kernel(starts, *refs):
    out = refs[-1]
    at = 0
    for ref in refs[:-1]:
        for p in range(ref.shape[0]):
            begin = pl.multiple_of(starts[at], 8)
            out[:, pl.ds(begin, 8), :] = ref[p]
            at += 1


def place(starts, pieces):
    return pl.pallas_call(
        place_kernel,
        out_shape=jax.ShapeDtypeStruct((SLAB, N, N), F32),
        in_specs=[pl.BlockSpec(memory_space=pltpu.SMEM)] + [pl.BlockSpec(memory_space=pltpu.VMEM)] * len(pieces),
        out_specs=pl.BlockSpec(memory_space=pltpu.VMEM),
        compiler_params=pltpu.CompilerParams(vmem_limit_bytes=16 * MIB),
        name="place",
    )(starts, *pieces)


def to_core(x):
    return lax.ppermute(x, "view", [(i, i ^ 1) for i in range(8)])


def to_next(x):
    return lax.ppermute(x, "view", [(i, (i + 2) % 8) for i in range(8)])


def to_prev(x):
    return lax.ppermute(x, "view", [(i, (i - 2) % 8) for i in range(8)])


def up(x):
    n = lax.axis_size("gz")
    return lax.ppermute(x, "gz", [(i, i + 1) for i in range(n - 1)])


def down(x):
    n = lax.axis_size("gz")
    return lax.ppermute(x, "gz", [(i + 1, i) for i in range(n - 1)])


def reduce_chunk(other, own):
    total = own + to_core(other)
    from_prev = to_next(total[0:2])
    from_next = to_prev(total[2:4])
    fwd_next = total[4:5] + from_prev[0:1]
    fwd_prev = total[5:6] + from_next[0:1]
    last_a = to_next(fwd_next)
    last_b = to_prev(fwd_prev)
    a = total[6:7] + from_next[1:2] + last_a
    b = total[7:8] + from_prev[1:2] + last_b
    return jnp.concatenate([a, b], 0)


def on_device(estimate, measured, lateral_x, lateral_y, depth_taps):
    view = lax.axis_index("view")
    core = lax.rem(view, 2)
    chip = lax.div(view, 2)
    recorded = measured[0]
    mx = lateral_x[0]
    my = lateral_y[0]
    taps = depth_taps[0]

    half = lax.dynamic_slice_in_dim(estimate, core * 64, 64, axis=1)
    before = up(half[SLAB - FAR :])
    after = down(half[:FAR])
    before, after, recorded = lax.optimization_barrier((before, after, recorded))
    rec_before = up(recorded[SLAB - HALF :])
    rec_after = down(recorded[:HALF])
    before2, after2 = to_core(before), to_core(after)

    nxt, prv, opp = (chip + 1) % 4, (chip + 3) % 4, (chip + 2) % 4
    order = jnp.stack([2 * opp, 2 * nxt + 1, 2 * opp + 1, 2 * prv, 2 * nxt, 2 * prv + 1, 2 * chip, 2 * chip + 1])
    starts = jnp.concatenate([core * 64 + 8 * order, (1 - core) * 64 + 8 * order]).astype(jnp.int32)
    xt = mx.T
    xt_pieces = jnp.concatenate([lax.dynamic_slice_in_dim(xt, starts[p], 8, axis=0) for p in range(16)], 0)
    x_pieces = xt_pieces.T
    x_halves = jnp.roll(mx, core * 64, axis=1)

    diag = jnp.arange(112)[None, :] - jnp.arange(80)[:, None]
    shift = jnp.arange(DEPTH)[:, None, None]
    toeplitz = jnp.sum(jnp.where(diag[None] == shift, taps[:, None, None], 0.0), 0)
    adjoint = jnp.sum(jnp.where(diag[None, :SLAB, :80] == shift, taps[::-1][:, None, None], 0.0), 0)
    tf = left_operand(toeplitz)
    ta = left_operand(adjoint)
    fwd_y = right_operand(my.T)
    adj_y = right_operand(my)
    adj_x = left_operand(xt_pieces)

    def middle_of(smooth):
        return middle(smooth, (rec_before, recorded, rec_after), tf, ta, adj_x, adj_y)

    mine = jnp.stack(
        [lax.dynamic_slice_in_dim(estimate, starts[6 + k], 8, axis=1) for k in range(2)], 0
    )

    (smooth_own,) = lateral([[estimate]], left_operand(mx), fwd_y)
    smooth_b, smooth_a = lateral([[before, before2], [after, after2]], left_operand(x_halves), fwd_y)
    own, other = middle_of((smooth_b, smooth_own, smooth_a))
    mine = mine * jnp.exp(reduce_chunk(other, own) / 8.0)

    prev_c, next_c = to_next(mine), to_prev(mine)
    b0, a0 = up(mine[:, SLAB - FAR :]), down(mine[:, :FAR])
    opp_a, opp_b = to_next(prev_c[0:1]), to_prev(next_c[1:2])
    sides = jnp.concatenate([prev_c, next_c], 0)
    b1, a1 = up(sides[:, SLAB - FAR :]), down(sides[:, :FAR])
    near = jnp.concatenate([mine, sides], 0)
    near2 = to_core(near)
    opp_c = jnp.concatenate([opp_a, opp_b], 0)
    b2, a2 = up(opp_c[:, SLAB - FAR :]), down(opp_c[:, :FAR])
    opp2 = to_core(opp_c)
    ends = jnp.concatenate([b0, b1, a0, a1], 0)
    ends2 = to_core(ends)
    tail = jnp.concatenate([b2, a2], 0)
    tail2 = to_core(tail)

    x_fwd = left_operand(x_pieces)

    def in_order(near, opp_c):
        mine, prv, nxt = near[0:2], near[2:4], near[4:6]
        return [opp_c[0:1], nxt[1:2], opp_c[1:2], prv[0:1], nxt[0:1], prv[1:2], mine]

    (smooth_own,) = lateral([in_order(near, opp_c) + in_order(near2, opp2)], x_fwd, fwd_y)
    smooth_b, smooth_a = lateral(
        [
            in_order(ends[0:6], tail[0:2]) + in_order(ends2[0:6], tail2[0:2]),
            in_order(ends[6:12], tail[2:4]) + in_order(ends2[6:12], tail2[2:4]),
        ],
        x_fwd,
        fwd_y,
    )
    own, other = middle_of((smooth_b, smooth_own, smooth_a))
    mine = mine * jnp.exp(reduce_chunk(other, own) / 8.0)
    prev_c, next_c = to_next(mine), to_prev(mine)
    near = jnp.concatenate([mine, prev_c, next_c], 0)
    near2 = to_core(near)
    opp_c = jnp.concatenate([to_next(prev_c[0:1]), to_prev(next_c[1:2])], 0)
    opp2 = to_core(opp_c)
    return place(starts, in_order(near, opp_c) + in_order(near2, opp2))


def solution(mesh):
    return jax.shard_map(
        on_device,
        mesh=mesh,
        in_specs=(
            P("gz", None, None),
            P("view", "gz", None, None),
            P("view", None, None),
            P("view", None, None),
            P("view", None),
        ),
        out_specs=P("gz", None, None),
        check_vma=False,
    )
```

time: 518 us -> 383 us (0.74)
  waiting for transfers between devices: 282 us -> 117 us
  other arithmetic: 144 us -> 10.9 us
  Pallas kernels: 0 us -> 85.5 us
  starting transfers between devices: 40.3 us -> 93 us
  local copies, waits for them, and re-layouts: 2.99 us -> 43.1 us
  matrix products: 30.3 us -> 0 us
  between operations: 13.6 us -> 31.7 us
    psum x2 -> x0, waiting for transfers between devices: 191 us -> none  [on_device(): updated = updated * jnp.exp(lax.psum(logs, 'view') / views)]
    pallas_call x0 -> x7, Pallas kernels: none -> 85.5 us  [the longest x2 55.9 us: middle(): pl.pallas_call(middle_kernel, out_shape=[half, half], in_specs=[pl.BlockS...]
    div x2 -> x0, other arithmetic: 70.2 us -> none  [on_device(): ratio_wide = with_halo(recorded / blurred, (('gz', 0),), HALF)]
    dot_general x2 -> x0, other arithmetic: 68.2 us -> none  [lateral_adjoint(): jnp.einsum('zab,ax->zxb', field, across, precision=lax.Precision.HIGHEST)]
    ppermute x8 -> x36, starting transfers between devices: 40 us -> 93 us  [the longest x5 33.7 us: down(): return lax.ppermute(x, 'gz', [(i + 1, i) for i in range(n - 1)])]
    dot_general x8 -> x0, matrix products: 30.3 us -> none  [the longest x2 10.2 us: lateral_forward(): jnp.einsum('zxy,ax->zay', field, across, precision=lax.Precision.HIGHEST)]
    ppermute x8 -> x36, waiting for transfers between devices: 91.4 us -> 117 us  [the longest x8 74.4 us: to_next(): return lax.ppermute(x, 'view', [(i, (i + 2) % 8) for i in range(8)])]
    another operation x0 -> x19, local copies, waits for them, and re-layouts: none -> 18.3 us
  transfers between devices with their start and end apart: 10 -> 36, of which waited for: 10 -> 20; matrix products, arithmetic and copies ran while one was open for 0% -> 13% of each run, Pallas kernels for 0% -> 5%
where the time goes in v1:
time: 383 us; the launch traced here: 381 us
  waiting for transfers between devices  117 us (31%)
  starting transfers between devices  93 us (24%)
  Pallas kernels  85.5 us (22%)
  local copies, waits for them, and re-layouts  43.1 us (11%)
  between operations  31.7 us (8%)
  other arithmetic  10.9 us (3%)
    ppermute x8, waiting for transfers between devices, to_next(): return lax.ppermute(x, 'view', [(i, (i + 2) % 8) for i in range(8)])  74.4 us
    pallas_call x2, Pallas kernels, middle(): pl.pallas_call(middle_kernel, out_shape=[half, half], in_specs=[pl.BlockS...  55.9 us
    ppermute x5, starting transfers between devices, down(): return lax.ppermute(x, 'gz', [(i + 1, i) for i in range(n - 1)])  33.7 us
    pallas_call x4, Pallas kernels, lateral(): pl.pallas_call(lambda *refs: lateral_kernel(counts, *refs), out_shape=[ja...  27 us
    ppermute x8, waiting for transfers between devices, to_prev(): return lax.ppermute(x, 'view', [(i, (i - 2) % 8) for i in range(8)])  26.5 us
    another operation x17, local copies, waits for them, and re-layouts  18.2 us
    ppermute x8, starting transfers between devices, to_next(): return lax.ppermute(x, 'view', [(i, (i + 2) % 8) for i in range(8)])  17.9 us
    unnamed x59, local copies, waits for them, and re-layouts  16.7 us
  transfers between devices with their start and end apart: 36, of which 20 were waited for; matrix products, arithmetic and copies ran while one was open for 13% of the time, Pallas kernels for 5%

profile of v1, /device:TPU:33, one launch (start us, length us, event | category | flops | bytes accessed | tf_op | source)
XLA Modules:
  0.0 381.1 jit_solution(9440836079039305034)
XLA Ops:
  0.0 1.7 constant_dynamic-slice_fusion.17
  1.8 3.1 collective-permute-start
  4.9 6.4 %collective-permute-start.1 = (f32[32,64,128]{2,1,0:T(8,128)S(1)}, f32[32,64,128]{2,1,0:T(8,128)}, u32[]{:S(2)}, u32[]{:S(2)}) collective-permute-start(f32[32,64,128]{2,1,0:T(8,128)S(1)} %get-tuple-element.29), channel_id=1, source_target_pairs={{1,0},{2,1},{3,2},{4,3},{5,4},{6,5},{7,6},{8,7},{9,8},{10,9},{11,1... | collective-permute-start | bytes 3145736 | tf_op jit(solution)/shard_map/ppermute | solution.py:196
  86.8 3.2 fusion.24
  89.9 1.9 collective-permute-start.4
  91.8 7.6 %collective-permute-start.5 = (f32[16,128,128]{2,1,0:T(8,128)}, f32[16,128,128]{2,1,0:T(8,128)}, u32[]{:S(2)}, u32[]{:S(2)}) collective-permute-start(f32[16,128,128]{2,1,0:T(8,128)} %get-tuple-element.27), channel_id=1, source_target_pairs={{1,0},{2,1},{3,2},{4,3},{5,4},{6,5},{7,6},{8,7},{9,8},{10,9},{11,1... | collective-permute-start | bytes 3145736 | tf_op jit(solution)/shard_map/ppermute | solution.py:196
  102.0 5.3 %lateral.5.so = f32[6144,128]{1,0:T(8,128)S(1)} custom-call(f32[48,128,128]{2,1,0:T(8,128)S(1)} %copy-done, bf16[256,256]{1,0:T(8,128)(2,1)S(1)} %maximum_maximum_fusion.2.refs_1_, bf16[256,256]{1,0:T(8,128)(2,1)S(1)} %copy.28.refs_5_.refs_2_.refs_29_.refs_15_), custom_call_target="tpu_custom_call" | custom-call | flops 1610612736 | bytes 6291456 | tf_op jit(solution)/shard_map/lateral/pallas_call | solution.py:94
  107.4 9.1 %lateral.4 = (f32[4096,128]{1,0:T(8,128)S(1)}, f32[4096,128]{1,0:T(8,128)S(1)}) custom-call(f32[32,64,128]{2,1,0:T(8,128)S(1)} %copy-done.11, f32[32,64,128]{2,1,0:T(8,128)} %collective-permute-done.2.refs_1_, f32[32,64,128]{2,1,0:T(8,128)} %collective-permute-done.1.refs_2_, f32[32,64,128]{2,1,0:T(8,128)} %collective-permute-done.3.refs_3_, ...), custom_call_target="tpu_custom_call" | custom-call | flops 2147483648 | bytes 8388608 | tf_op jit(solution)/shard_map/lateral/pallas_call | solution.py:94
  116.6 3.7 collective-permute-done.4
  121.1 27.9 %middle.2 = (f32[8,48,8,128]{3,2,1,0:T(8,128)S(1)}, f32[8,48,8,128]{3,2,1,0:T(8,128)S(1)}) custom-call(f32[4096,128]{1,0:T(8,128)S(1)} %get-tuple-element.18.sb, f32[6144,128]{1,0:T(8,128)S(1)} %lateral.5.so, f32[4096,128]{1,0:T(8,128)S(1)} %get-tuple-element.19.sa, f32[2048,128]{1,0:T(8,128)} %bitcast.17.mb, f32[6144,128]{1,0:T(8,128)S(1)} %bitcast.111, ...), custom_call_target="tpu_custom_call" | custom-call | flops 8000000000 | bytes 15728640 | tf_op jit(solution)/shard_map/middle/pallas_call | solution.py:144
  149.1 2.0 collective-permute-start.6
  151.1 3.0 collective-permute-done.6
  154.4 3.1 collective-permute-start.8
  157.5 2.2 collective-permute-start.7
  159.7 13.1 %collective-permute-done.8 = f32[2,48,8,128]{3,2,1,0:T(8,128)S(1)} collective-permute-done((f32[2,48,8,128]{3,2,1,0:T(8,128)S(1)}, f32[2,48,8,128]{3,2,1,0:T(8,128)S(1)}, u32[]{:S(2)}, u32[]{:S(2)}) %collective-permute-start.8) | collective-permute-done | bytes 393248 | tf_op jit(solution)/shard_map/ppermute | solution.py:182
  172.9 3.1 collective-permute-done.7
  176.0 7.2 %collective-permute-done.9 = f32[1,48,8,128]{3,2,1,0:T(8,128)S(1)} collective-permute-done((f32[1,48,8,128]{3,2,1,0:T(8,128)S(1)}, f32[1,48,8,128]{3,2,1,0:T(8,128)S(1)}, u32[]{:S(2)}, u32[]{:S(2)}) %collective-permute-start.9) | collective-permute-done | bytes 196640 | tf_op jit(solution)/shard_map/ppermute | solution.py:182
  183.2 3.3 collective-permute-start.10
  186.6 6.3 %collective-permute-done.10 = f32[1,48,8,128]{3,2,1,0:T(8,128)S(1)} collective-permute-done((f32[1,48,8,128]{3,2,1,0:T(8,128)S(1)}, f32[1,48,8,128]{3,2,1,0:T(8,128)S(1)}, u32[]{:S(2)}, u32[]{:S(2)}) %collective-permute-start.10) | collective-permute-done | bytes 196640 | tf_op jit(solution)/shard_map/ppermute | solution.py:186
  193.0 1.8 collective-permute-start.11
  194.8 2.3 collective-permute-start.13
  198.1 15.3 %collective-permute-done.11 = f32[2,48,8,128]{3,2,1,0:T(8,128)S(1)} collective-permute-done((f32[2,48,8,128]{3,2,1,0:T(8,128)S(1)}, f32[2,48,8,128]{3,2,1,0:T(8,128)S(1)}, u32[]{:S(2)}, u32[]{:S(2)}) %collective-permute-start.11) | collective-permute-done | bytes 393248 | tf_op jit(solution)/shard_map/ppermute | solution.py:182
  213.7 3.6 collective-permute-start.14
  217.5 2.2 collective-permute-start.16
  219.7 7.3 %collective-permute-start.21 = (f32[4,32,8,128]{3,2,1,0:T(8,128)S(1)}, f32[4,32,8,128]{3,2,1,0:T(8,128)S(1)}, u32[]{:S(2)}, u32[]{:S(2)}) collective-permute-start(f32[4,32,8,128]{3,2,1,0:T(8,128)S(1)} %get-tuple-element.59), channel_id=1, source_target_pairs={{1,0},{2,1},{3,2},{4,3},{5,4},{6,5},{7,6},{8,7},{9,8},{10,9},{11,1... | collective-permute-start | bytes 1572872 | tf_op jit(solution)/shard_map/ppermute | solution.py:196
  227.1 1.9 collective-permute-start.15
  229.1 7.6 %collective-permute-start.18 = (f32[2,32,8,128]{3,2,1,0:T(8,128)S(1)}, f32[2,32,8,128]{3,2,1,0:T(8,128)S(1)}, u32[]{:S(2)}, u32[]{:S(2)}) collective-permute-start(f32[2,32,8,128]{3,2,1,0:T(8,128)S(1)} %get-tuple-element.87), channel_id=1, source_target_pairs={{1,0},{2,1},{3,2},{4,3},{5,4},{6,5},{7,6},{8,7},{9,8},{10,9},{11,1... | collective-permute-start | bytes 786440 | tf_op jit(solution)/shard_map/ppermute | solution.py:196
  236.7 1.9 collective-permute-start.17
  238.7 2.8 collective-permute-done.15
  241.5 4.8 %collective-permute-start.20 = (f32[2,32,8,128]{3,2,1,0:T(8,128)S(1)}, f32[2,32,8,128]{3,2,1,0:T(8,128)S(1)}, u32[]{:S(2)}, u32[]{:S(2)}) collective-permute-start(f32[2,32,8,128]{3,2,1,0:T(8,128)S(1)} %get-tuple-element.85), channel_id=1, source_target_pairs={{1,0},{2,1},{3,2},{4,3},{5,4},{6,5},{7,6},{8,7},{9,8},{10,9},{11,1... | collective-permute-start | bytes 786440 | tf_op jit(solution)/shard_map/ppermute | solution.py:196
  246.3 4.0 %collective-permute-start.24 = (f32[6,48,8,128]{3,2,1,0:T(8,128)S(1)}, f32[6,48,8,128]{3,2,1,0:T(8,128)S(1)}, u32[]{:S(2)}, u32[]{:S(2)}) collective-permute-start(f32[6,48,8,128]{3,2,1,0:T(8,128)S(1)} %pad_maximum_fusion.1), channel_id=1, source_target_pairs={{0,32},{32,0},{64,96},{96,64},{128,160},{160,128},{192,224},{224,1... | collective-permute-start | bytes 3538952 | tf_op jit(solution)/shard_map/ppermute | solution.py:178
  250.4 2.1 collective-permute-start.23
  255.8 5.4 %lateral.7.so = f32[6144,128]{1,0:T(8,128)S(1)} custom-call(f32[1,48,8,128]{3,2,1,0:T(8,128)S(1)} %collective-permute-done.12.refs_0_, f32[1,48,8,128]{3,2,1,0:T(8,128)S(1)} %get-tuple-element.84.refs_1_, f32[1,48,8,128]{3,2,1,0:T(8,128)S(1)} %collective-permute-done.14.refs_2_, f32[1,48,8,128]{3,2,1,0:T(8,128)S(1)} %get-tuple-element.82.refs_3_, ...), custom_call_target="tpu_custom_call" | custom-call | flops 1610612736 | bytes 6291456 | tf_op jit(solution)/shard_map/lateral/pallas_call | solution.py:94
  261.3 7.2 %lateral.6 = (f32[4096,128]{1,0:T(8,128)S(1)}, f32[4096,128]{1,0:T(8,128)S(1)}) custom-call(f32[1,32,8,128]{3,2,1,0:T(8,128)S(1)} %get-tuple-element.92.refs_0_, f32[1,32,8,128]{3,2,1,0:T(8,128)S(1)} %get-tuple-element.72.refs_1_, f32[1,32,8,128]{3,2,1,0:T(8,128)S(1)} %get-tuple-element.91.refs_2_, f32[1,32,8,128]{3,2,1,0:T(8,128)S(1)} %get-tuple-element.71.refs_3_, ...), custom_call_target="tpu_custom_call" | custom-call | flops 2147483648 | bytes 8388608 | tf_op jit(solution)/shard_map/lateral/pallas_call | solution.py:94
  268.6 27.9 %middle.3 = (f32[8,48,8,128]{3,2,1,0:T(8,128)S(1)}, f32[8,48,8,128]{3,2,1,0:T(8,128)S(1)}) custom-call(f32[4096,128]{1,0:T(8,128)S(1)} %get-tuple-element.23.sb, f32[6144,128]{1,0:T(8,128)S(1)} %lateral.7.so, f32[4096,128]{1,0:T(8,128)S(1)} %get-tuple-element.24.sa, f32[2048,128]{1,0:T(8,128)} %bitcast.17.mb, f32[6144,128]{1,0:T(8,128)S(1)} %bitcast.112, ...), custom_call_target="tpu_custom_call" | custom-call | flops 8000000000 | bytes 15728640 | tf_op jit(solution)/shard_map/middle/pallas_call | solution.py:144
  297.0 3.0 collective-permute-done.25
  300.4 3.6 collective-permute-start.26
  303.9 12.3 %collective-permute-done.27 = f32[2,48,8,128]{3,2,1,0:T(8,128)S(1)} collective-permute-done((f32[2,48,8,128]{3,2,1,0:T(8,128)S(1)}, f32[2,48,8,128]{3,2,1,0:T(8,128)S(1)}, u32[]{:S(2)}, u32[]{:S(2)}) %collective-permute-start.27) | collective-permute-done | bytes 393248 | tf_op jit(solution)/shard_map/ppermute | solution.py:182
  316.2 2.0 collective-permute-start.28
  318.8 9.2 %collective-permute-done.28 = f32[1,48,8,128]{3,2,1,0:T(8,128)S(1)} collective-permute-done((f32[1,48,8,128]{3,2,1,0:T(8,128)S(1)}, f32[1,48,8,128]{3,2,1,0:T(8,128)S(1)}, u32[]{:S(2)}, u32[]{:S(2)}) %collective-permute-start.28) | collective-permute-done | bytes 196640 | tf_op jit(solution)/shard_map/ppermute | solution.py:182
  328.2 7.0 %collective-permute-done.29 = f32[1,48,8,128]{3,2,1,0:T(8,128)S(1)} collective-permute-done((f32[1,48,8,128]{3,2,1,0:T(8,128)S(1)}, f32[1,48,8,128]{3,2,1,0:T(8,128)S(1)}, u32[]{:S(2)}, u32[]{:S(2)}) %collective-permute-start.29) | collective-permute-done | bytes 196640 | tf_op jit(solution)/shard_map/ppermute | solution.py:186
  335.4 7.2 %collective-permute-start.30 = (f32[2,48,8,128]{3,2,1,0:T(8,128)S(1)}, f32[2,48,8,128]{3,2,1,0:T(8,128)S(1)}, u32[]{:S(2)}, u32[]{:S(2)}) collective-permute-start(f32[2,48,8,128]{3,2,1,0:T(8,128)S(1)} %fusion.2.refs_6_), channel_id=1, source_target_pairs={{0,64},{32,96},{64,128},{96,160},{128,192},{160,224},{192,0},{224,... | collective-permute-start | bytes 1179656 | tf_op jit(solution)/shard_map/ppermute | solution.py:182
  342.6 15.4 %collective-permute-done.30 = f32[2,48,8,128]{3,2,1,0:T(8,128)S(1)} collective-permute-done((f32[2,48,8,128]{3,2,1,0:T(8,128)S(1)}, f32[2,48,8,128]{3,2,1,0:T(8,128)S(1)}, u32[]{:S(2)}, u32[]{:S(2)}) %collective-permute-start.30) | collective-permute-done | bytes 393248 | tf_op jit(solution)/shard_map/ppermute | solution.py:182
  358.0 3.4 collective-permute-start.31
  362.0 2.3 collective-permute-start.35
  365.0 2.0 collective-permute-done.31.refs_0_
  366.9 9.1 %collective-permute-done.33.refs_2_ = f32[1,48,8,128]{3,2,1,0:T(8,128)S(1)} collective-permute-done((f32[1,48,8,128]{3,2,1,0:T(8,128)S(1)}, f32[1,48,8,128]{3,2,1,0:T(8,128)S(1)}, u32[]{:S(2)}, u32[]{:S(2)}) %collective-permute-start.33) | collective-permute-done | bytes 196640 | tf_op jit(solution)/shard_map/ppermute | solution.py:186
  378.4 2.6 place.1
  (177 shorter events, 58.9 us)
Async XLA Ops:
  0.0 32.7 %copy-start.19 = (f32[1,128,128]{2,1,0:T(8,128)S(1)}, f32[1,128,128]{2,1,0:T(8,128)}, u32[]{:S(2)}) copy-start(f32[1,128,128]{2,1,0:T(8,128)} %param.8) | copy-start | bytes 196612
  0.0 33.4 %copy-start.12 = (f32[1,128,128]{2,1,0:T(8,128)S(1)}, f32[1,128,128]{2,1,0:T(8,128)}, u32[]{:S(2)}) copy-start(f32[1,128,128]{2,1,0:T(8,128)} %param.7) | copy-start | bytes 196612
  0.0 34.0 %copy-start.20 = (f32[1,33]{1,0:T(1,128)S(1)}, f32[1,33]{1,0:T(1,128)}, u32[]{:S(2)}) copy-start(f32[1,33]{1,0:T(1,128)} %param.9) | copy-start | bytes 400
  1.8 82.8 %collective-permute-start = (f32[32,64,128]{2,1,0:T(8,128)S(1)}, f32[32,64,128]{2,1,0:T(8,128)S(1)}, u32[]{:S(2)}, u32[]{:S(2)}) collective-permute-start(f32[32,64,128]{2,1,0:T(8,128)S(1)} %get-tuple-element.30), channel_id=1, source_target_pairs={{0,1},{1,2},{2,3},{3,4},{4,5},{5,6},{6,7},{7,8},{8,9},{9,10},{10,1... | collective-permute-start | bytes 3145736 | tf_op jit(solution)/shard_map/ppermute | solution.py:191
  4.9 79.7 %collective-permute-start.1 = (f32[32,64,128]{2,1,0:T(8,128)S(1)}, f32[32,64,128]{2,1,0:T(8,128)}, u32[]{:S(2)}, u32[]{:S(2)}) collective-permute-start(f32[32,64,128]{2,1,0:T(8,128)S(1)} %get-tuple-element.29), channel_id=1, source_target_pairs={{1,0},{2,1},{3,2},{4,3},{5,4},{6,5},{7,6},{8,7},{9,8},{10,9},{11,1... | collective-permute-start | bytes 3145736 | tf_op jit(solution)/shard_map/ppermute | solution.py:196
  85.5 16.5 %copy-start = (f32[48,128,128]{2,1,0:T(8,128)S(1)}, f32[48,128,128]{2,1,0:T(8,128)}, u32[]{:S(2)}) copy-start(f32[48,128,128]{2,1,0:T(8,128)} %refs_0_.1) | copy-start | bytes 9437188
  85.5 21.9 %collective-permute-start.2 = (f32[32,64,128]{2,1,0:T(8,128)}, f32[32,64,128]{2,1,0:T(8,128)}, u32[]{:S(2)}, u32[]{:S(2)}) collective-permute-start(f32[32,64,128]{2,1,0:T(8,128)} %copy-done.10), channel_id=1, source_target_pairs={{0,32},{32,0},{64,96},{96,64},{128,160},{160,128},{192,224},{224,1... | collective-permute-start | bytes 3145736 | tf_op jit(solution)/shard_map/ppermute | solution.py:178
  86.7 20.7 %collective-permute-start.3 = (f32[32,64,128]{2,1,0:T(8,128)}, f32[32,64,128]{2,1,0:T(8,128)}, u32[]{:S(2)}, u32[]{:S(2)}) collective-permute-start(f32[32,64,128]{2,1,0:T(8,128)} %collective-permute-done.1.refs_2_), channel_id=1, source_target_pairs={{0,32},{32,0},{64,96},{96,64},{128,160},{160,128},{192,224},{224,1... | collective-permute-start | bytes 3145736 | tf_op jit(solution)/shard_map/ppermute | solution.py:178
  89.9 30.3 %collective-permute-start.4 = (f32[16,128,128]{2,1,0:T(8,128)}, f32[16,128,128]{2,1,0:T(8,128)}, u32[]{:S(2)}, u32[]{:S(2)}) collective-permute-start(f32[16,128,128]{2,1,0:T(8,128)} %get-tuple-element.28), channel_id=1, source_target_pairs={{0,1},{1,2},{2,3},{3,4},{4,5},{5,6},{6,7},{7,8},{8,9},{9,10},{10,1... | collective-permute-start | bytes 3145736 | tf_op jit(solution)/shard_map/ppermute | solution.py:191
  91.8 29.3 %collective-permute-start.5 = (f32[16,128,128]{2,1,0:T(8,128)}, f32[16,128,128]{2,1,0:T(8,128)}, u32[]{:S(2)}, u32[]{:S(2)}) collective-permute-start(f32[16,128,128]{2,1,0:T(8,128)} %get-tuple-element.27), channel_id=1, source_target_pairs={{1,0},{2,1},{3,2},{4,3},{5,4},{6,5},{7,6},{8,7},{9,8},{10,9},{11,1... | collective-permute-start | bytes 3145736 | tf_op jit(solution)/shard_map/ppermute | solution.py:196
  102.0 19.1 %copy-start.3 = (bf16[256,256]{1,0:T(8,128)(2,1)}, bf16[256,256]{1,0:T(8,128)(2,1)S(1)}, u32[]{:S(2)}) copy-start(bf16[256,256]{1,0:T(8,128)(2,1)S(1)} %maximum_maximum_fusion.4.right_ref) | copy-start | bytes 393220
  107.4 13.8 %copy-start.1 = (f32[1,48,128,128]{3,2,1,0:T(8,128)S(1)}, f32[1,48,128,128]{3,2,1,0:T(8,128)}, u32[]{:S(2)}) copy-start(f32[1,48,128,128]{3,2,1,0:T(8,128)} %param.6) | copy-start | bytes 9437188
  107.4 13.7 %copy-start.6 = (bf16[160,224]{1,0:T(8,128)(2,1)S(1)}, bf16[160,224]{1,0:T(8,128)(2,1)}, u32[]{:S(2)}) copy-start(bf16[160,224]{1,0:T(8,128)(2,1)} %maximum_maximum_fusion.6.tf_ref) | copy-start | bytes 215044
  107.4 13.7 %copy-start.8 = (bf16[96,160]{1,0:T(8,128)(2,1)S(1)}, bf16[96,160]{1,0:T(8,128)(2,1)}, u32[]{:S(2)}) copy-start(bf16[96,160]{1,0:T(8,128)(2,1)} %maximum_maximum_fusion.7.ta_ref) | copy-start | bytes 92164
  149.1 5.1 %collective-permute-start.6 = (f32[8,48,8,128]{3,2,1,0:T(8,128)S(1)}, f32[8,48,8,128]{3,2,1,0:T(8,128)S(1)}, u32[]{:S(2)}, u32[]{:S(2)}) collective-permute-start(f32[8,48,8,128]{3,2,1,0:T(8,128)S(1)} %get-tuple-element.22), channel_id=1, source_target_pairs={{0,32},{32,0},{64,96},{96,64},{128,160},{160,128},{192,224},{224,1... | collective-permute-start | bytes 4718600 | tf_op jit(solution)/shard_map/ppermute | solution.py:178
  154.4 18.3 %collective-permute-start.8 = (f32[2,48,8,128]{3,2,1,0:T(8,128)S(1)}, f32[2,48,8,128]{3,2,1,0:T(8,128)S(1)}, u32[]{:S(2)}, u32[]{:S(2)}) collective-permute-start(f32[2,48,8,128]{3,2,1,0:T(8,128)S(1)} %get-tuple-element.49), channel_id=1, source_target_pairs={{0,64},{32,96},{64,128},{96,160},{128,192},{160,224},{192,0},{224,... | collective-permute-start | bytes 1179656 | tf_op jit(solution)/shard_map/ppermute | solution.py:182
  157.5 18.5 %collective-permute-start.7 = (f32[2,48,8,128]{3,2,1,0:T(8,128)S(1)}, f32[2,48,8,128]{3,2,1,0:T(8,128)S(1)}, u32[]{:S(2)}, u32[]{:S(2)}) collective-permute-start(f32[2,48,8,128]{3,2,1,0:T(8,128)S(1)} %get-tuple-element.50), channel_id=1, source_target_pairs={{0,192},{32,224},{64,0},{96,32},{128,64},{160,96},{192,128},{224,1... | collective-permute-start | bytes 1179656 | tf_op jit(solution)/shard_map/ppermute | solution.py:186
  172.8 10.3 %collective-permute-start.9 = (f32[1,48,8,128]{3,2,1,0:T(8,128)S(1)}, f32[1,48,8,128]{3,2,1,0:T(8,128)S(1)}, u32[]{:S(2)}, u32[]{:S(2)}) collective-permute-start(f32[1,48,8,128]{3,2,1,0:T(8,128)S(1)} %slice_add_fusion.6), channel_id=1, source_target_pairs={{0,64},{32,96},{64,128},{96,160},{128,192},{160,224},{192,0},{224,... | collective-permute-start | bytes 589832 | tf_op jit(solution)/shard_map/ppermute | solution.py:182
  183.2 14.7 %copy-start.17 = (f32[1,48,8,128]{3,2,1,0:T(8,128)}, f32[1,48,8,128]{3,2,1,0:T(8,128)S(1)}, u32[]{:S(2)}) copy-start(f32[1,48,8,128]{3,2,1,0:T(8,128)S(1)} %get-tuple-element.35) | copy-start | bytes 589828
  183.2 9.7 %collective-permute-start.10 = (f32[1,48,8,128]{3,2,1,0:T(8,128)S(1)}, f32[1,48,8,128]{3,2,1,0:T(8,128)S(1)}, u32[]{:S(2)}, u32[]{:S(2)}) collective-permute-start(f32[1,48,8,128]{3,2,1,0:T(8,128)S(1)} %get-tuple-element.36), channel_id=1, source_target_pairs={{0,192},{32,224},{64,0},{96,32},{128,64},{160,96},{192,128},{224,1... | collective-permute-start | bytes 589832 | tf_op jit(solution)/shard_map/ppermute | solution.py:186
  193.0 20.4 %collective-permute-start.11 = (f32[2,48,8,128]{3,2,1,0:T(8,128)S(1)}, f32[2,48,8,128]{3,2,1,0:T(8,128)S(1)}, u32[]{:S(2)}, u32[]{:S(2)}) collective-permute-start(f32[2,48,8,128]{3,2,1,0:T(8,128)S(1)} %maximum_multiply_fusion.refs_6_), channel_id=1, source_target_pairs={{0,64},{32,96},{64,128},{96,160},{128,192},{160,224},{192,0},{224,... | collective-permute-start | bytes 1179656 | tf_op jit(solution)/shard_map/ppermute | solution.py:182
  194.8 18.9 %collective-permute-start.13 = (f32[2,48,8,128]{3,2,1,0:T(8,128)S(1)}, f32[2,48,8,128]{3,2,1,0:T(8,128)S(1)}, u32[]{:S(2)}, u32[]{:S(2)}) collective-permute-start(f32[2,48,8,128]{3,2,1,0:T(8,128)S(1)} %maximum_multiply_fusion.refs_6_), channel_id=1, source_target_pairs={{0,192},{32,224},{64,0},{96,32},{128,64},{160,96},{192,128},{224,1... | collective-permute-start | bytes 1179656 | tf_op jit(solution)/shard_map/ppermute | solution.py:186
  213.4 13.6 %collective-permute-start.12 = (f32[1,48,8,128]{3,2,1,0:T(8,128)S(1)}, f32[1,48,8,128]{3,2,1,0:T(8,128)S(1)}, u32[]{:S(2)}, u32[]{:S(2)}) collective-permute-start(f32[1,48,8,128]{3,2,1,0:T(8,128)S(1)} %get-tuple-element.82.refs_3_), channel_id=1, source_target_pairs={{0,64},{32,96},{64,128},{96,160},{128,192},{160,224},{192,0},{224,... | collective-permute-start | bytes 589832 | tf_op jit(solution)/shard_map/ppermute | solution.py:182
  213.7 13.3 %collective-permute-start.14 = (f32[1,48,8,128]{3,2,1,0:T(8,128)S(1)}, f32[1,48,8,128]{3,2,1,0:T(8,128)S(1)}, u32[]{:S(2)}, u32[]{:S(2)}) collective-permute-start(f32[1,48,8,128]{3,2,1,0:T(8,128)S(1)} %get-tuple-element.84.refs_1_), channel_id=1, source_target_pairs={{0,192},{32,224},{64,0},{96,32},{128,64},{160,96},{192,128},{224,1... | collective-permute-start | bytes 589832 | tf_op jit(solution)/shard_map/ppermute | solution.py:186
  217.5 36.6 %collective-permute-start.16 = (f32[4,32,8,128]{3,2,1,0:T(8,128)S(1)}, f32[4,32,8,128]{3,2,1,0:T(8,128)S(1)}, u32[]{:S(2)}, u32[]{:S(2)}) collective-permute-start(f32[4,32,8,128]{3,2,1,0:T(8,128)S(1)} %get-tuple-element.60), channel_id=1, source_target_pairs={{0,1},{1,2},{2,3},{3,4},{4,5},{5,6},{6,7},{7,8},{8,9},{9,10},{10,1... | collective-permute-start | bytes 1572872 | tf_op jit(solution)/shard_map/ppermute | solution.py:191
  219.7 34.4 %collective-permute-start.21 = (f32[4,32,8,128]{3,2,1,0:T(8,128)S(1)}, f32[4,32,8,128]{3,2,1,0:T(8,128)S(1)}, u32[]{:S(2)}, u32[]{:S(2)}) collective-permute-start(f32[4,32,8,128]{3,2,1,0:T(8,128)S(1)} %get-tuple-element.59), channel_id=1, source_target_pairs={{1,0},{2,1},{3,2},{4,3},{5,4},{6,5},{7,6},{8,7},{9,8},{10,9},{11,1... | collective-permute-start | bytes 1572872 | tf_op jit(solution)/shard_map/ppermute | solution.py:196
  227.1 14.4 %collective-permute-start.15 = (f32[2,32,8,128]{3,2,1,0:T(8,128)S(1)}, f32[2,32,8,128]{3,2,1,0:T(8,128)S(1)}, u32[]{:S(2)}, u32[]{:S(2)}) collective-permute-start(f32[2,32,8,128]{3,2,1,0:T(8,128)S(1)} %get-tuple-element.88), channel_id=1, source_target_pairs={{0,1},{1,2},{2,3},{3,4},{4,5},{5,6},{6,7},{7,8},{8,9},{9,10},{10,1... | collective-permute-start | bytes 786440 | tf_op jit(solution)/shard_map/ppermute | solution.py:191
  229.1 17.2 %collective-permute-start.18 = (f32[2,32,8,128]{3,2,1,0:T(8,128)S(1)}, f32[2,32,8,128]{3,2,1,0:T(8,128)S(1)}, u32[]{:S(2)}, u32[]{:S(2)}) collective-permute-start(f32[2,32,8,128]{3,2,1,0:T(8,128)S(1)} %get-tuple-element.87), channel_id=1, source_target_pairs={{1,0},{2,1},{3,2},{4,3},{5,4},{6,5},{7,6},{8,7},{9,8},{10,9},{11,1... | collective-permute-start | bytes 786440 | tf_op jit(solution)/shard_map/ppermute | solution.py:196
  236.7 13.7 %collective-permute-start.17 = (f32[2,32,8,128]{3,2,1,0:T(8,128)S(1)}, f32[2,32,8,128]{3,2,1,0:T(8,128)S(1)}, u32[]{:S(2)}, u32[]{:S(2)}) collective-permute-start(f32[2,32,8,128]{3,2,1,0:T(8,128)S(1)} %get-tuple-element.86), channel_id=1, source_target_pairs={{0,1},{1,2},{2,3},{3,4},{4,5},{5,6},{6,7},{7,8},{8,9},{9,10},{10,1... | collective-permute-start | bytes 786440 | tf_op jit(solution)/shard_map/ppermute | solution.py:191
  241.5 11.0 %collective-permute-start.20 = (f32[2,32,8,128]{3,2,1,0:T(8,128)S(1)}, f32[2,32,8,128]{3,2,1,0:T(8,128)S(1)}, u32[]{:S(2)}, u32[]{:S(2)}) collective-permute-start(f32[2,32,8,128]{3,2,1,0:T(8,128)S(1)} %get-tuple-element.85), channel_id=1, source_target_pairs={{1,0},{2,1},{3,2},{4,3},{5,4},{6,5},{7,6},{8,7},{9,8},{10,9},{11,1... | collective-permute-start | bytes 786440 | tf_op jit(solution)/shard_map/ppermute | solution.py:196
  246.3 9.3 %collective-permute-start.24 = (f32[6,48,8,128]{3,2,1,0:T(8,128)S(1)}, f32[6,48,8,128]{3,2,1,0:T(8,128)S(1)}, u32[]{:S(2)}, u32[]{:S(2)}) collective-permute-start(f32[6,48,8,128]{3,2,1,0:T(8,128)S(1)} %pad_maximum_fusion.1), channel_id=1, source_target_pairs={{0,32},{32,0},{64,96},{96,64},{128,160},{160,128},{192,224},{224,1... | collective-permute-start | bytes 3538952 | tf_op jit(solution)/shard_map/ppermute | solution.py:178
  250.4 4.0 %collective-permute-start.23 = (f32[2,48,8,128]{3,2,1,0:T(8,128)S(1)}, f32[2,48,8,128]{3,2,1,0:T(8,128)S(1)}, u32[]{:S(2)}, u32[]{:S(2)}) collective-permute-start(f32[2,48,8,128]{3,2,1,0:T(8,128)S(1)} %constant_dynamic-update-slice_fusion.16), channel_id=1, source_target_pairs={{0,32},{32,0},{64,96},{96,64},{128,160},{160,128},{192,224},{224,1... | collective-permute-start | bytes 1179656 | tf_op jit(solution)/shard_map/ppermute | solution.py:178
  252.5 3.1 collective-permute-start.19
  254.2 6.9 %collective-permute-start.22 = (f32[12,32,8,128]{3,2,1,0:T(8,128)S(1)}, f32[12,32,8,128]{3,2,1,0:T(8,128)S(1)}, u32[]{:S(2)}, u32[]{:S(2)}) collective-permute-start(f32[12,32,8,128]{3,2,1,0:T(8,128)S(1)} %pad_maximum_fusion), channel_id=1, source_target_pairs={{0,32},{32,0},{64,96},{96,64},{128,160},{160,128},{192,224},{224,1... | collective-permute-start | bytes 4718600 | tf_op jit(solution)/shard_map/ppermute | solution.py:178
  296.5 3.5 collective-permute-start.25
  300.2 35.0 %copy-start.14 = (f32[1,48,8,128]{3,2,1,0:T(8,128)S(1)}, f32[1,48,8,128]{3,2,1,0:T(8,128)}, u32[]{:S(2)}) copy-start(f32[1,48,8,128]{3,2,1,0:T(8,128)} %copy-done.13) | copy-start | bytes 589828
  300.3 35.0 %copy-start.16 = (f32[1,48,8,128]{3,2,1,0:T(8,128)S(1)}, f32[1,48,8,128]{3,2,1,0:T(8,128)}, u32[]{:S(2)}) copy-start(f32[1,48,8,128]{3,2,1,0:T(8,128)} %copy-done.15) | copy-start | bytes 589828
  300.3 35.0 %copy-start.18 = (f32[1,48,8,128]{3,2,1,0:T(8,128)S(1)}, f32[1,48,8,128]{3,2,1,0:T(8,128)}, u32[]{:S(2)}) copy-start(f32[1,48,8,128]{3,2,1,0:T(8,128)} %copy-done.17) | copy-start | bytes 589828
  300.3 15.9 %collective-permute-start.27 = (f32[2,48,8,128]{3,2,1,0:T(8,128)S(1)}, f32[2,48,8,128]{3,2,1,0:T(8,128)S(1)}, u32[]{:S(2)}, u32[]{:S(2)}) collective-permute-start(f32[2,48,8,128]{3,2,1,0:T(8,128)S(1)} %get-tuple-element.37), channel_id=1, source_target_pairs={{0,64},{32,96},{64,128},{96,160},{128,192},{160,224},{192,0},{224,... | collective-permute-start | bytes 1179656 | tf_op jit(solution)/shard_map/ppermute | solution.py:182
  300.4 18.5 %collective-permute-start.26 = (f32[2,48,8,128]{3,2,1,0:T(8,128)S(1)}, f32[2,48,8,128]{3,2,1,0:T(8,128)S(1)}, u32[]{:S(2)}, u32[]{:S(2)}) collective-permute-start(f32[2,48,8,128]{3,2,1,0:T(8,128)S(1)} %get-tuple-element.38), channel_id=1, source_target_pairs={{0,192},{32,224},{64,0},{96,32},{128,64},{160,96},{192,128},{224,1... | collective-permute-start | bytes 1179656 | tf_op jit(solution)/shard_map/ppermute | solution.py:186
  316.2 11.8 %collective-permute-start.28 = (f32[1,48,8,128]{3,2,1,0:T(8,128)S(1)}, f32[1,48,8,128]{3,2,1,0:T(8,128)S(1)}, u32[]{:S(2)}, u32[]{:S(2)}) collective-permute-start(f32[1,48,8,128]{3,2,1,0:T(8,128)S(1)} %slice_add_fusion.2), channel_id=1, source_target_pairs={{0,64},{32,96},{64,128},{96,160},{128,192},{160,224},{192,0},{224,... | collective-permute-start | bytes 589832 | tf_op jit(solution)/shard_map/ppermute | solution.py:182
  328.1 7.0 %collective-permute-start.29 = (f32[1,48,8,128]{3,2,1,0:T(8,128)S(1)}, f32[1,48,8,128]{3,2,1,0:T(8,128)S(1)}, u32[]{:S(2)}, u32[]{:S(2)}) collective-permute-start(f32[1,48,8,128]{3,2,1,0:T(8,128)S(1)} %get-tuple-element.34), channel_id=1, source_target_pairs={{0,192},{32,224},{64,0},{96,32},{128,64},{160,96},{192,128},{224,1... | collective-permute-start | bytes 589832 | tf_op jit(solution)/shard_map/ppermute | solution.py:186
  335.4 22.7 %collective-permute-start.30 = (f32[2,48,8,128]{3,2,1,0:T(8,128)S(1)}, f32[2,48,8,128]{3,2,1,0:T(8,128)S(1)}, u32[]{:S(2)}, u32[]{:S(2)}) collective-permute-start(f32[2,48,8,128]{3,2,1,0:T(8,128)S(1)} %fusion.2.refs_6_), channel_id=1, source_target_pairs={{0,64},{32,96},{64,128},{96,160},{128,192},{160,224},{192,0},{224,... | collective-permute-start | bytes 1179656 | tf_op jit(solution)/shard_map/ppermute | solution.py:182
  342.6 19.4 %collective-permute-start.32 = (f32[2,48,8,128]{3,2,1,0:T(8,128)S(1)}, f32[2,48,8,128]{3,2,1,0:T(8,128)S(1)}, u32[]{:S(2)}, u32[]{:S(2)}) collective-permute-start(f32[2,48,8,128]{3,2,1,0:T(8,128)S(1)} %fusion.2.refs_6_), channel_id=1, source_target_pairs={{0,192},{32,224},{64,0},{96,32},{128,64},{160,96},{192,128},{224,1... | collective-permute-start | bytes 1179656 | tf_op jit(solution)/shard_map/ppermute | solution.py:186
  358.0 8.9 %collective-permute-start.31 = (f32[1,48,8,128]{3,2,1,0:T(8,128)S(1)}, f32[1,48,8,128]{3,2,1,0:T(8,128)S(1)}, u32[]{:S(2)}, u32[]{:S(2)}) collective-permute-start(f32[1,48,8,128]{3,2,1,0:T(8,128)S(1)} %get-tuple-element.76.refs_3_), channel_id=1, source_target_pairs={{0,64},{32,96},{64,128},{96,160},{128,192},{160,224},{192,0},{224,... | collective-permute-start | bytes 589832 | tf_op jit(solution)/shard_map/ppermute | solution.py:182
  362.0 16.3 %collective-permute-start.35 = (f32[6,48,8,128]{3,2,1,0:T(8,128)S(1)}, f32[6,48,8,128]{3,2,1,0:T(8,128)S(1)}, u32[]{:S(2)}, u32[]{:S(2)}) collective-permute-start(f32[6,48,8,128]{3,2,1,0:T(8,128)S(1)} %pad_maximum_fusion.2), channel_id=1, source_target_pairs={{0,32},{32,0},{64,96},{96,64},{128,160},{160,128},{192,224},{224,1... | collective-permute-start | bytes 3538952 | tf_op jit(solution)/shard_map/ppermute | solution.py:178
  364.3 11.7 %collective-permute-start.33 = (f32[1,48,8,128]{3,2,1,0:T(8,128)S(1)}, f32[1,48,8,128]{3,2,1,0:T(8,128)S(1)}, u32[]{:S(2)}, u32[]{:S(2)}) collective-permute-start(f32[1,48,8,128]{3,2,1,0:T(8,128)S(1)} %get-tuple-element.78.refs_1_), channel_id=1, source_target_pairs={{0,192},{32,224},{64,0},{96,32},{128,64},{160,96},{192,128},{224,1... | collective-permute-start | bytes 589832 | tf_op jit(solution)/shard_map/ppermute | solution.py:186
  376.1 2.2 collective-permute-start.34
  (9 other events, 63.5 us)

commit v2 on v1

--- a/solution.py
+++ b/solution.py
@@ -13,26 +13,13 @@
 F32 = jnp.float32
 BF16 = jnp.bfloat16
 MIB = 1024 * 1024
+PITCH = 132
+STEP = 16
 
 
 def split(x):
     hi = x.astype(BF16)
     return hi, (x - hi.astype(F32)).astype(BF16)
-
-
-def split_matrix(m):
-    hi = lax.reduce_precision(m, 8, 7)
-    return hi.astype(BF16), lax.reduce_precision(m - hi, 8, 7).astype(BF16)
-
-
-def left_operand(m):
-    hi, lo = split_matrix(m)
-    return jnp.concatenate([jnp.concatenate([hi, hi], 1), jnp.concatenate([lo, lo], 1)], 0)
-
-
-def right_operand(m):
-    hi, lo = split_matrix(m)
-    return jnp.concatenate([jnp.concatenate([hi, lo], 1), jnp.concatenate([hi, lo], 1)], 0)
 
 
 def left_product(operand, x):
@@ -50,8 +37,10 @@
 
 
 def two_sided(planes, left, right):
-    both = left_product(left, jnp.concatenate(planes, 1))
-    rows = jnp.concatenate([both[:, :N], both[:, N:]], 0)
+    sides = [
+        left_product(left, jnp.concatenate(planes[i : i + 2], 1)) for i in range(0, len(planes), 2)
+    ]
+    rows = jnp.concatenate([part for s in sides for part in (s[:, :N], s[:, N:])], 0)
     return right_product(rows, right)
 
 
@@ -75,12 +64,12 @@
         region = ins[at : at + count]
         at += count
 
-        @pl.loop(0, planes // 4)
+        @pl.loop(0, planes // STEP)
         def _(i, region=region, out=out):
-            for j in range(2):
-                z = 4 * i + 2 * j
-                res = two_sided([region_plane(region, z), region_plane(region, z + 1)], left, right)
-                out[pl.ds(pl.multiple_of(z * N, 2 * N), 2 * N), :] = res
+            zs = [STEP * i + j for j in range(STEP)]
+            res = two_sided([region_plane(region, z) for z in zs], left, right)
+            for j, z in enumerate(zs):
+                out[pl.ds(z * PITCH, N), :] = res[j * N : j * N + N]
 
 
 def lateral(regions, left, right):
@@ -93,10 +82,10 @@
     planes = sum(p for _, p in counts)
     return pl.pallas_call(
         lambda *refs: lateral_kernel(counts, *refs),
-        out_shape=[jax.ShapeDtypeStruct((p * N, N), F32) for _, p in counts],
+        out_shape=[jax.ShapeDtypeStruct((p * PITCH, N), F32) for _, p in counts],
         in_specs=[pl.BlockSpec(memory_space=pltpu.VMEM)] * (len(ins) + 2),
         out_specs=[pl.BlockSpec(memory_space=pltpu.VMEM)] * len(counts),
-        compiler_params=pltpu.CompilerParams(vmem_limit_bytes=20 * MIB),
+        compiler_params=pltpu.CompilerParams(vmem_limit_bytes=24 * MIB),
         cost_estimate=pl.CostEstimate(flops=planes * 16 * N**3, bytes_accessed=planes * 8 * N * N, transcendentals=0),
         name="lateral",
     )(*ins, left, right)
@@ -106,51 +95,137 @@
     tf = tf_ref[...]
     ta = ta_ref[...]
 
-    def rows(refs, a):
-        return jnp.concatenate([r[pl.ds(a, r.shape[0] // N, stride=N), :] for r in refs], 0)
-
-    def pair(refs, a):
-        return jnp.concatenate([rows(refs, a), rows(refs, a + 1)], 1)
-
-    @pl.loop(0, N // 4)
+    def smooth(a):
+        return jnp.concatenate([r[pl.ds(a, r.shape[0] // PITCH, stride=PITCH), :] for r in (sb, so, sa)], 0)
+
+    def recorded(a):
+        return jnp.concatenate([r[a] for r in (mb, mo, ma)], 0)
+
+    @pl.loop(0, N // STEP)
     def _(i):
-        for j in range(2):
-            a = 4 * i + 2 * j
-            blurred = left_product(tf, pair((sb, so, sa), a))
-            recorded = pair((mb, mo, ma), a)
-            ratio = jnp.where(recorded > 0, recorded / blurred, 0.0)
+        firsts = [STEP * i + j for j in range(0, STEP, 2)]
+        blurred = [left_product(tf, jnp.concatenate([smooth(a), smooth(a + 1)], 1)) for a in firsts]
+        ratios = []
+        for a, blur in zip(firsts, blurred):
+            rec = jnp.concatenate([recorded(a), recorded(a + 1)], 1)
+            ratios.append(jnp.where(rec > 0, rec / blur, 0.0))
+        for a, ratio in zip(firsts, ratios):
             res = left_product(ta, ratio)
-            back[pl.ds(a, SLAB, stride=N), :] = res[:, :N]
-            back[pl.ds(a + 1, SLAB, stride=N), :] = res[:, N:]
+            back[pl.ds(a, SLAB, stride=PITCH), :] = res[:, :N]
+            back[pl.ds(a + 1, SLAB, stride=PITCH), :] = res[:, N:]
 
     left = left_ref[...]
     right = right_ref[...]
 
-    @pl.loop(0, SLAB // 4)
+    @pl.loop(0, SLAB // STEP)
     def _(i):
-        for j in range(2):
-            z = 4 * i + 2 * j
-            at = pl.multiple_of(z * N, 2 * N)
-            logs = jnp.log(two_sided([back[pl.ds(at, N), :], back[pl.ds(at + N, N), :]], left, right))
-            for k in range(2):
-                for p in range(8):
-                    own[p, z + k] = logs[k * N + 8 * p : k * N + 8 * p + 8]
-                    other[p, z + k] = logs[k * N + 64 + 8 * p : k * N + 64 + 8 * p + 8]
+        zs = [STEP * i + j for j in range(STEP)]
+        logs = jnp.log(two_sided([back[pl.ds(z * PITCH, N), :] for z in zs], left, right))
+        for j, z in enumerate(zs):
+            for p in range(8):
+                own[p, z] = logs[j * N + 8 * p : j * N + 8 * p + 8]
+                other[p, z] = logs[j * N + 64 + 8 * p : j * N + 64 + 8 * p + 8]
 
 
 def middle(smooth, recorded, tf, ta, left, right):
-    ins = [*smooth, *[r.reshape(-1, N) for r in recorded], tf, ta, left, right]
+    ins = [*smooth, *recorded, tf, ta, left, right]
     half = jax.ShapeDtypeStruct((8, SLAB, 8, N), F32)
     return pl.pallas_call(
         middle_kernel,
         out_shape=[half, half],
         in_specs=[pl.BlockSpec(memory_space=pltpu.VMEM)] * len(ins),
         out_specs=[pl.BlockSpec(memory_space=pltpu.VMEM)] * 2,
-        scratch_shapes=[pltpu.VMEM((SLAB * N, N), F32)],
-        compiler_params=pltpu.CompilerParams(vmem_limit_bytes=28 * MIB),
+        scratch_shapes=[pltpu.VMEM((SLAB * PITCH, N), F32)],
+        compiler_params=pltpu.CompilerParams(vmem_limit_bytes=32 * MIB),
         cost_estimate=pl.CostEstimate(flops=8 * 10**9, bytes_accessed=15 * MIB, transcendentals=SLAB * N * N),
         name="middle",
     )(*ins)
+
+
+def operand_rows(m):
+    hi, lo = split(m)
+    return jnp.concatenate([hi, lo], 0)
+
+
+def twice(m, axis):
+    return jnp.concatenate([m, m], axis)
+
+
+def operand_cols(m):
+    hi, lo = split(twice(m, 0))
+    return jnp.concatenate([hi, lo], 1)
+
+
+def prep_kernel(
+    starts, taps, mx_ref, my_ref, rec,
+    tf, ta, x_all, x_halves, x_pieces, adj_x, fwd_y, adj_y, rec_t, rec_first, rec_last, xt_ref,
+):
+    def toeplitz(rows, cols, flip):
+        i = lax.broadcasted_iota(jnp.int32, (rows, 2 * cols), 0)
+        j = lax.broadcasted_iota(jnp.int32, (rows, 2 * cols), 1)
+        diag = jnp.where(j >= cols, j - cols, j) - i
+        out = jnp.zeros((rows, 2 * cols), F32)
+        for k in range(DEPTH):
+            out = jnp.where(diag == k, taps[0, DEPTH - 1 - k if flip else k], out)
+        return out
+
+    tf[...] = operand_rows(toeplitz(SLAB + 2 * HALF, SLAB + 2 * FAR, False))
+    ta[...] = operand_rows(toeplitz(SLAB, SLAB + 2 * HALF, True))
+    mx = mx_ref[...]
+    my = my_ref[...]
+    x_all[...] = operand_rows(twice(mx, 1))
+    fwd_y[...] = operand_cols(my.T)
+    adj_y[...] = operand_cols(my)
+    xt_ref[...] = mx.T
+
+    def row_blocks(rows):
+        return jnp.concatenate([xt_ref[pl.ds(pl.multiple_of(r, 8), 8), :] for r in rows], 0)
+
+    pieces = row_blocks([starts[p] for p in range(16)])
+    adj_x[...] = operand_rows(twice(pieces, 1))
+    x_pieces[...] = operand_rows(twice(pieces.T, 1))
+    core = starts[16]
+    halves = row_blocks([core * 64 + 8 * p for p in range(8)] + [64 - core * 64 + 8 * p for p in range(8)])
+    x_halves[...] = operand_rows(twice(halves.T, 1))
+
+    @pl.loop(0, N // 8)
+    def _(i):
+        at = pl.multiple_of(8 * i, 8)
+        for zb in range(0, SLAB, 8):
+            block = jnp.stack([rec[z, pl.ds(at, 8), :] for z in range(zb, zb + 8)], 0)
+            block = jnp.swapaxes(block, 0, 1)
+            for j in range(8):
+                rec_t[at + j, zb : zb + 8, :] = block[j]
+                if zb < HALF:
+                    rec_first[at + j, zb : zb + 8, :] = block[j]
+                if zb >= SLAB - HALF:
+                    rec_last[at + j, zb - SLAB + HALF : zb - SLAB + HALF + 8, :] = block[j]
+
+
+def prep(starts, taps, mx, my, rec):
+    full = SLAB + 2 * HALF
+    wide = SLAB + 2 * FAR
+    square = jax.ShapeDtypeStruct((2 * N, 2 * N), BF16)
+    edge = jax.ShapeDtypeStruct((N, HALF, N), F32)
+    outs = [
+        jax.ShapeDtypeStruct((2 * full, 2 * wide), BF16),
+        jax.ShapeDtypeStruct((2 * SLAB, 2 * full), BF16),
+        *[square] * 6,
+        jax.ShapeDtypeStruct((N, SLAB, N), F32),
+        edge,
+        edge,
+    ]
+    vmem = pl.BlockSpec(memory_space=pltpu.VMEM)
+    smem = pl.BlockSpec(memory_space=pltpu.SMEM)
+    return pl.pallas_call(
+        prep_kernel,
+        out_shape=outs,
+        in_specs=[smem, smem, vmem, vmem, vmem],
+        out_specs=[vmem] * len(outs),
+        scratch_shapes=[pltpu.VMEM((N, N), F32)],
+        compiler_params=pltpu.CompilerParams(vmem_limit_bytes=20 * MIB),
+        name="prep",
+    )(starts, taps, mx, my, rec)
 
 
 def place_kernel(starts, *refs):
@@ -200,10 +275,13 @@
     total = own + to_core(other)
     from_prev = to_next(total[0:2])
     from_next = to_prev(total[2:4])
+    from_prev, from_next = lax.optimization_barrier((from_prev, from_next))
     fwd_next = total[4:5] + from_prev[0:1]
     fwd_prev = total[5:6] + from_next[0:1]
+    fwd_next, fwd_prev = lax.optimization_barrier((fwd_next, fwd_prev))
     last_a = to_next(fwd_next)
     last_b = to_prev(fwd_prev)
+    last_a, last_b = lax.optimization_barrier((last_a, last_b))
     a = total[6:7] + from_next[1:2] + last_a
     b = total[7:8] + from_prev[1:2] + last_b
     return jnp.concatenate([a, b], 0)
@@ -216,43 +294,31 @@
     recorded = measured[0]
     mx = lateral_x[0]
     my = lateral_y[0]
-    taps = depth_taps[0]
+
+    nxt, prv, opp = (chip + 1) % 4, (chip + 3) % 4, (chip + 2) % 4
+    order = jnp.stack([2 * opp, 2 * nxt + 1, 2 * opp + 1, 2 * prv, 2 * nxt, 2 * prv + 1, 2 * chip, 2 * chip + 1])
+    starts = jnp.concatenate([core * 64 + 8 * order, (1 - core) * 64 + 8 * order, core[None]]).astype(jnp.int32)
 
     half = lax.dynamic_slice_in_dim(estimate, core * 64, 64, axis=1)
     before = up(half[SLAB - FAR :])
     after = down(half[:FAR])
-    before, after, recorded = lax.optimization_barrier((before, after, recorded))
-    rec_before = up(recorded[SLAB - HALF :])
-    rec_after = down(recorded[:HALF])
+    tf, ta, x_all, x_halves, x_fwd, adj_x, fwd_y, adj_y, rec_own, rec_first, rec_last = prep(
+        starts, depth_taps, mx, my, recorded
+    )
+    before, after, rec_first, rec_last = lax.optimization_barrier((before, after, rec_first, rec_last))
+    rec_before = up(rec_last)
+    rec_after = down(rec_first)
     before2, after2 = to_core(before), to_core(after)
 
-    nxt, prv, opp = (chip + 1) % 4, (chip + 3) % 4, (chip + 2) % 4
-    order = jnp.stack([2 * opp, 2 * nxt + 1, 2 * opp + 1, 2 * prv, 2 * nxt, 2 * prv + 1, 2 * chip, 2 * chip + 1])
-    starts = jnp.concatenate([core * 64 + 8 * order, (1 - core) * 64 + 8 * order]).astype(jnp.int32)
-    xt = mx.T
-    xt_pieces = jnp.concatenate([lax.dynamic_slice_in_dim(xt, starts[p], 8, axis=0) for p in range(16)], 0)
-    x_pieces = xt_pieces.T
-    x_halves = jnp.roll(mx, core * 64, axis=1)
-
-    diag = jnp.arange(112)[None, :] - jnp.arange(80)[:, None]
-    shift = jnp.arange(DEPTH)[:, None, None]
-    toeplitz = jnp.sum(jnp.where(diag[None] == shift, taps[:, None, None], 0.0), 0)
-    adjoint = jnp.sum(jnp.where(diag[None, :SLAB, :80] == shift, taps[::-1][:, None, None], 0.0), 0)
-    tf = left_operand(toeplitz)
-    ta = left_operand(adjoint)
-    fwd_y = right_operand(my.T)
-    adj_y = right_operand(my)
-    adj_x = left_operand(xt_pieces)
-
     def middle_of(smooth):
-        return middle(smooth, (rec_before, recorded, rec_after), tf, ta, adj_x, adj_y)
+        return middle(smooth, (rec_before, rec_own, rec_after), tf, ta, adj_x, adj_y)
 
     mine = jnp.stack(
         [lax.dynamic_slice_in_dim(estimate, starts[6 + k], 8, axis=1) for k in range(2)], 0
     )
 
-    (smooth_own,) = lateral([[estimate]], left_operand(mx), fwd_y)
-    smooth_b, smooth_a = lateral([[before, before2], [after, after2]], left_operand(x_halves), fwd_y)
+    (smooth_own,) = lateral([[estimate]], x_all, fwd_y)
+    smooth_b, smooth_a = lateral([[before, before2], [after, after2]], x_halves, fwd_y)
     own, other = middle_of((smooth_b, smooth_own, smooth_a))
     mine = mine * jnp.exp(reduce_chunk(other, own) / 8.0)
 
@@ -270,8 +336,6 @@
     ends2 = to_core(ends)
     tail = jnp.concatenate([b2, a2], 0)
     tail2 = to_core(tail)
-
-    x_fwd = left_operand(x_pieces)
 
     def in_order(near, opp_c):
         mine, prv, nxt = near[0:2], near[2:4], near[4:6]

time: 383 us -> 266 us (0.69)
  the two profiles are of different devices: /device:TPU:33 before, /device:TPU:15 now
where the time goes in v2:
time: 266 us; the launch traced here: 265 us
  waiting for transfers between devices  135 us (51%)
  starting transfers between devices  84.5 us (32%)
  Pallas kernels  30 us (11%)
  local copies, waits for them, and re-layouts  6.87 us (3%)
  between operations  4.94 us (2%)
  other arithmetic  3.31 us (1%)
    ppermute x8, waiting for transfers between devices, to_next(): return lax.ppermute(x, 'view', [(i, (i + 2) % 8) for i in range(8)])  62 us
    ppermute x5, waiting for transfers between devices, up(): return lax.ppermute(x, 'gz', [(i, i + 1) for i in range(n - 1)])  32.8 us
    ppermute x10, starting transfers between devices, to_core(): return lax.ppermute(x, 'view', [(i, i ^ 1) for i in range(8)])  25.2 us
    ppermute x8, starting transfers between devices, to_prev(): return lax.ppermute(x, 'view', [(i, (i - 2) % 8) for i in range(8)])  22.7 us
    ppermute x8, waiting for transfers between devices, to_prev(): return lax.ppermute(x, 'view', [(i, (i - 2) % 8) for i in range(8)])  19.9 us
    ppermute x5, starting transfers between devices, down(): return lax.ppermute(x, 'gz', [(i + 1, i) for i in range(n - 1)])  14.2 us
    pallas_call x2, Pallas kernels, middle(): pl.pallas_call(middle_kernel, out_shape=[half, half], in_specs=[pl.BlockS...  13.5 us
    ppermute x5, starting transfers between devices, up(): return lax.ppermute(x, 'gz', [(i, i + 1) for i in range(n - 1)])  12.9 us
  transfers between devices with their start and end apart: 36, of which 20 were waited for; matrix products, arithmetic and copies ran while one was open for 1% of the time, Pallas kernels for 4%

profile of v2, /device:TPU:15, one launch (start us, length us, event | category | flops | bytes accessed | tf_op | source)
XLA Modules:
  0.0 265.0 jit_solution(1909162756310093226)
XLA Ops:
  0.0 3.1 %constant_dynamic-slice_fusion.1 = (f32[32,64,128]{2,1,0:T(8,128)}, f32[32,64,128]{2,1,0:T(8,128)}) fusion(f32[48,128,128]{2,1,0:T(8,128)} %refs_0_.1, s32[]{:T(128)S(6)} %select_n.29, s32[]{:T(128)S(6)} %add.127), kind=kLoop, calls=%fused_computation.30 | loop fusion | bytes 4194312 | tf_op jit(solution)/shard_map/slice | solution.py:304
  3.2 3.1 %collective-permute-start = (f32[32,64,128]{2,1,0:T(8,128)}, f32[32,64,128]{2,1,0:T(8,128)}, u32[]{:S(2)}, u32[]{:S(2)}) collective-permute-start(f32[32,64,128]{2,1,0:T(8,128)} %get-tuple-element.76), channel_id=1, source_target_pairs={{0,1},{1,2},{2,3},{3,4},{4,5},{5,6},{6,7},{7,8},{8,9},{9,10},{10,1... | collective-permute-start | bytes 3145736 | tf_op jit(solution)/shard_map/ppermute | solution.py:266
  6.3 2.2 collective-permute-start.1
  8.7 1.9 copy-done.1
  12.3 17.0 %collective-permute-done.refs_0_ = f32[32,64,128]{2,1,0:T(8,128)} collective-permute-done((f32[32,64,128]{2,1,0:T(8,128)}, f32[32,64,128]{2,1,0:T(8,128)}, u32[]{:S(2)}, u32[]{:S(2)}) %collective-permute-start) | collective-permute-done | bytes 1048608 | tf_op jit(solution)/shard_map/ppermute | solution.py:266
  29.3 4.9 %collective-permute-done.1.refs_2_ = f32[32,64,128]{2,1,0:T(8,128)} collective-permute-done((f32[32,64,128]{2,1,0:T(8,128)}, f32[32,64,128]{2,1,0:T(8,128)}, u32[]{:S(2)}, u32[]{:S(2)}) %collective-permute-start.1) | collective-permute-done | bytes 1048608 | tf_op jit(solution)/shard_map/ppermute | solution.py:271
  34.3 1.9 collective-permute-start.2
  36.2 1.9 collective-permute-start.4
  38.1 3.4 %collective-permute-start.5 = (f32[128,16,128]{2,1,0:T(8,128)S(1)}, f32[128,16,128]{2,1,0:T(8,128)S(1)}, u32[]{:S(2)}, u32[]{:S(2)}) collective-permute-start(f32[128,16,128]{2,1,0:T(8,128)S(1)} %get-tuple-element.51), channel_id=1, source_target_pairs={{1,0},{2,1},{3,2},{4,3},{5,4},{6,5},{7,6},{8,7},{9,8},{10,9},{11,1... | collective-permute-start | bytes 3145736 | tf_op jit(solution)/shard_map/ppermute | solution.py:271
  41.5 2.2 lateral.5.so
  43.7 4.6 %lateral.4 = (f32[4224,128]{1,0:T(8,128)S(1)}, f32[4224,128]{1,0:T(8,128)S(1)}) custom-call(f32[32,64,128]{2,1,0:T(8,128)} %collective-permute-done.refs_0_, f32[32,64,128]{2,1,0:T(8,128)S(1)} %collective-permute-done.2.refs_1_, f32[32,64,128]{2,1,0:T(8,128)} %collective-permute-done.1.refs_2_, f32[32,64,128]{2,1,0:T(8,128)S(1)} %collective-permute-done.3.refs_3_, ...), custom_call_target="tpu_custom_call" | custom-call | flops 2147483648 | bytes 8388608 | tf_op jit(solution)/shard_map/lateral/pallas_call | solution.py:83
  48.3 13.9 %collective-permute-done.4.mb = f32[128,16,128]{2,1,0:T(8,128)S(1)} collective-permute-done((f32[128,16,128]{2,1,0:T(8,128)S(1)}, f32[128,16,128]{2,1,0:T(8,128)S(1)}, u32[]{:S(2)}, u32[]{:S(2)}) %collective-permute-start.4) | collective-permute-done | bytes 1048608 | tf_op jit(solution)/shard_map/ppermute | solution.py:266
  62.3 4.0 %collective-permute-done.5.ma = f32[128,16,128]{2,1,0:T(8,128)S(1)} collective-permute-done((f32[128,16,128]{2,1,0:T(8,128)S(1)}, f32[128,16,128]{2,1,0:T(8,128)S(1)}, u32[]{:S(2)}, u32[]{:S(2)}) %collective-permute-start.5) | collective-permute-done | bytes 1048608 | tf_op jit(solution)/shard_map/ppermute | solution.py:271
  66.3 6.7 %middle.2 = (f32[8,48,8,128]{3,2,1,0:T(8,128)S(1)}, f32[8,48,8,128]{3,2,1,0:T(8,128)S(1)}) custom-call(f32[4224,128]{1,0:T(8,128)S(1)} %get-tuple-element.46.sb, f32[6336,128]{1,0:T(8,128)S(1)} %lateral.5.so, f32[4224,128]{1,0:T(8,128)S(1)} %get-tuple-element.48.sa, f32[128,16,128]{2,1,0:T(8,128)S(1)} %collective-permute-done.4.mb, ...), custom_call_target="tpu_custom_call" | custom-call | flops 8000000000 | bytes 15728640 | tf_op jit(solution)/shard_map/middle/pallas_call | solution.py:133
  74.5 3.0 %collective-permute-done.6 = f32[8,48,8,128]{3,2,1,0:T(8,128)S(1)} collective-permute-done((f32[8,48,8,128]{3,2,1,0:T(8,128)S(1)}, f32[8,48,8,128]{3,2,1,0:T(8,128)S(1)}, u32[]{:S(2)}, u32[]{:S(2)}) %collective-permute-start.6) | collective-permute-done | bytes 1572896 | tf_op jit(solution)/shard_map/ppermute | solution.py:253
  77.8 3.1 %collective-permute-start.7 = (f32[2,48,8,128]{3,2,1,0:T(8,128)S(1)}, f32[2,48,8,128]{3,2,1,0:T(8,128)S(1)}, u32[]{:S(2)}, u32[]{:S(2)}) collective-permute-start(f32[2,48,8,128]{3,2,1,0:T(8,128)S(1)} %get-tuple-element.100), channel_id=1, source_target_pairs={{0,64},{32,96},{64,128},{96,160},{128,192},{160,224},{192,0},{224,... | collective-permute-start | bytes 1179656 | tf_op jit(solution)/shard_map/ppermute | solution.py:257
  80.9 3.1 %collective-permute-start.8 = (f32[2,48,8,128]{3,2,1,0:T(8,128)S(1)}, f32[2,48,8,128]{3,2,1,0:T(8,128)S(1)}, u32[]{:S(2)}, u32[]{:S(2)}) collective-permute-start(f32[2,48,8,128]{3,2,1,0:T(8,128)S(1)} %get-tuple-element.99), channel_id=1, source_target_pairs={{0,192},{32,224},{64,0},{96,32},{128,64},{160,96},{192,128},{224,1... | collective-permute-start | bytes 1179656 | tf_op jit(solution)/shard_map/ppermute | solution.py:261
  84.0 12.1 %collective-permute-done.7 = f32[2,48,8,128]{3,2,1,0:T(8,128)S(1)} collective-permute-done((f32[2,48,8,128]{3,2,1,0:T(8,128)S(1)}, f32[2,48,8,128]{3,2,1,0:T(8,128)S(1)}, u32[]{:S(2)}, u32[]{:S(2)}) %collective-permute-start.7) | collective-permute-done | bytes 393248 | tf_op jit(solution)/shard_map/ppermute | solution.py:257
  96.1 6.6 %collective-permute-done.8 = f32[2,48,8,128]{3,2,1,0:T(8,128)S(1)} collective-permute-done((f32[2,48,8,128]{3,2,1,0:T(8,128)S(1)}, f32[2,48,8,128]{3,2,1,0:T(8,128)S(1)}, u32[]{:S(2)}, u32[]{:S(2)}) %collective-permute-start.8) | collective-permute-done | bytes 393248 | tf_op jit(solution)/shard_map/ppermute | solution.py:261
  103.5 3.3 %collective-permute-start.9 = (f32[1,48,8,128]{3,2,1,0:T(8,128)}, f32[1,48,8,128]{3,2,1,0:T(8,128)}, u32[]{:S(2)}, u32[]{:S(2)}) collective-permute-start(f32[1,48,8,128]{3,2,1,0:T(8,128)} %get-tuple-element.60), channel_id=1, source_target_pairs={{0,64},{32,96},{64,128},{96,160},{128,192},{160,224},{192,0},{224,... | collective-permute-start | bytes 589832 | tf_op jit(solution)/shard_map/ppermute | solution.py:257
  112.0 4.1 %collective-permute-done.9 = f32[1,48,8,128]{3,2,1,0:T(8,128)} collective-permute-done((f32[1,48,8,128]{3,2,1,0:T(8,128)}, f32[1,48,8,128]{3,2,1,0:T(8,128)}, u32[]{:S(2)}, u32[]{:S(2)}) %collective-permute-start.9) | collective-permute-done | bytes 196640 | tf_op jit(solution)/shard_map/ppermute | solution.py:257
  117.6 2.3 collective-permute-start.11
  121.7 10.8 %collective-permute-done.11 = f32[2,48,8,128]{3,2,1,0:T(8,128)S(1)} collective-permute-done((f32[2,48,8,128]{3,2,1,0:T(8,128)S(1)}, f32[2,48,8,128]{3,2,1,0:T(8,128)S(1)}, u32[]{:S(2)}, u32[]{:S(2)}) %collective-permute-start.11) | collective-permute-done | bytes 393248 | tf_op jit(solution)/shard_map/ppermute | solution.py:257
  132.9 3.6 %collective-permute-start.14 = (f32[1,48,8,128]{3,2,1,0:T(8,128)S(1)}, f32[1,48,8,128]{3,2,1,0:T(8,128)S(1)}, u32[]{:S(2)}, u32[]{:S(2)}) collective-permute-start(f32[1,48,8,128]{3,2,1,0:T(8,128)S(1)} %get-tuple-element.134.refs_1_), channel_id=1, source_target_pairs={{0,192},{32,224},{64,0},{96,32},{128,64},{160,96},{192,128},{224,1... | collective-permute-start | bytes 589832 | tf_op jit(solution)/shard_map/ppermute | solution.py:261
  136.7 1.9 collective-permute-start.16
  138.6 3.4 %collective-permute-start.21 = (f32[4,32,8,128]{3,2,1,0:T(8,128)S(1)}, f32[4,32,8,128]{3,2,1,0:T(8,128)S(1)}, u32[]{:S(2)}, u32[]{:S(2)}) collective-permute-start(f32[4,32,8,128]{3,2,1,0:T(8,128)S(1)} %get-tuple-element.109), channel_id=1, source_target_pairs={{1,0},{2,1},{3,2},{4,3},{5,4},{6,5},{7,6},{8,7},{9,8},{10,9},{11,1... | collective-permute-start | bytes 1572872 | tf_op jit(solution)/shard_map/ppermute | solution.py:271
  142.0 2.7 %collective-permute-done.14.refs_2_ = f32[1,48,8,128]{3,2,1,0:T(8,128)S(1)} collective-permute-done((f32[1,48,8,128]{3,2,1,0:T(8,128)S(1)}, f32[1,48,8,128]{3,2,1,0:T(8,128)S(1)}, u32[]{:S(2)}, u32[]{:S(2)}) %collective-permute-start.14) | collective-permute-done | bytes 196640 | tf_op jit(solution)/shard_map/ppermute | solution.py:261
  144.7 1.9 collective-permute-start.15
  146.6 3.4 %collective-permute-start.18 = (f32[2,32,8,128]{3,2,1,0:T(8,128)S(1)}, f32[2,32,8,128]{3,2,1,0:T(8,128)S(1)}, u32[]{:S(2)}, u32[]{:S(2)}) collective-permute-start(f32[2,32,8,128]{3,2,1,0:T(8,128)S(1)} %get-tuple-element.137), channel_id=1, source_target_pairs={{1,0},{2,1},{3,2},{4,3},{5,4},{6,5},{7,6},{8,7},{9,8},{10,9},{11,1... | collective-permute-start | bytes 786440 | tf_op jit(solution)/shard_map/ppermute | solution.py:271
  150.1 4.0 %collective-permute-start.17 = (f32[2,32,8,128]{3,2,1,0:T(8,128)S(1)}, f32[2,32,8,128]{3,2,1,0:T(8,128)S(1)}, u32[]{:S(2)}, u32[]{:S(2)}) collective-permute-start(f32[2,32,8,128]{3,2,1,0:T(8,128)S(1)} %get-tuple-element.136), channel_id=1, source_target_pairs={{0,1},{1,2},{2,3},{3,4},{4,5},{5,6},{6,7},{7,8},{8,9},{9,10},{10,1... | collective-permute-start | bytes 786440 | tf_op jit(solution)/shard_map/ppermute | solution.py:266
  156.0 1.9 collective-permute-start.20
  157.9 2.1 collective-permute-done.18
  160.1 2.6 collective-permute-start.24
  165.2 5.7 %collective-permute-start.19 = (f32[4,32,8,128]{3,2,1,0:T(8,128)S(1)}, f32[4,32,8,128]{3,2,1,0:T(8,128)S(1)}, u32[]{:S(2)}, u32[]{:S(2)}) collective-permute-start(f32[4,32,8,128]{3,2,1,0:T(8,128)S(1)} %pad_maximum_fusion.3), channel_id=1, source_target_pairs={{0,32},{32,0},{64,96},{96,64},{128,160},{160,128},{192,224},{224,1... | collective-permute-start | bytes 1572872 | tf_op jit(solution)/shard_map/ppermute | solution.py:253
  172.7 2.3 lateral.7.so
  175.2 3.1 %lateral.6 = (f32[4224,128]{1,0:T(8,128)S(1)}, f32[4224,128]{1,0:T(8,128)S(1)}) custom-call(f32[1,32,8,128]{3,2,1,0:T(8,128)S(1)} %get-tuple-element.142.refs_0_, f32[1,32,8,128]{3,2,1,0:T(8,128)S(1)} %get-tuple-element.122.refs_1_, f32[1,32,8,128]{3,2,1,0:T(8,128)S(1)} %get-tuple-element.141.refs_2_, f32[1,32,8,128]{3,2,1,0:T(8,128)S(1)} %get-tuple-element.121.refs_3_, ...), custom_call_target="tpu_custom_call" | custom-call | flops 2147483648 | bytes 8388608 | tf_op jit(solution)/shard_map/lateral/pallas_call | solution.py:83
  178.3 6.7 %middle.3 = (f32[8,48,8,128]{3,2,1,0:T(8,128)S(1)}, f32[8,48,8,128]{3,2,1,0:T(8,128)S(1)}) custom-call(f32[4224,128]{1,0:T(8,128)S(1)} %get-tuple-element.65.sb, f32[6336,128]{1,0:T(8,128)S(1)} %lateral.7.so, f32[4224,128]{1,0:T(8,128)S(1)} %get-tuple-element.66.sa, f32[128,16,128]{2,1,0:T(8,128)S(1)} %copy-done.8, f32[128,48,128]{2,1,0:T(8,128)S(1)} %copy-done.6, ...), custom_call_target="tpu_custom_call" | custom-call | flops 8000000000 | bytes 15728640 | tf_op jit(solution)/shard_map/middle/pallas_call | solution.py:133
  185.5 3.0 %collective-permute-done.25 = f32[8,48,8,128]{3,2,1,0:T(8,128)S(1)} collective-permute-done((f32[8,48,8,128]{3,2,1,0:T(8,128)S(1)}, f32[8,48,8,128]{3,2,1,0:T(8,128)S(1)}, u32[]{:S(2)}, u32[]{:S(2)}) %collective-permute-start.25) | collective-permute-done | bytes 1572896 | tf_op jit(solution)/shard_map/ppermute | solution.py:253
  188.9 3.6 %collective-permute-start.27 = (f32[2,48,8,128]{3,2,1,0:T(8,128)S(1)}, f32[2,48,8,128]{3,2,1,0:T(8,128)S(1)}, u32[]{:S(2)}, u32[]{:S(2)}) collective-permute-start(f32[2,48,8,128]{3,2,1,0:T(8,128)S(1)} %get-tuple-element.83), channel_id=1, source_target_pairs={{0,192},{32,224},{64,0},{96,32},{128,64},{160,96},{192,128},{224,1... | collective-permute-start | bytes 1179656 | tf_op jit(solution)/shard_map/ppermute | solution.py:261
  192.4 17.3 %collective-permute-done.26 = f32[2,48,8,128]{3,2,1,0:T(8,128)S(1)} collective-permute-done((f32[2,48,8,128]{3,2,1,0:T(8,128)S(1)}, f32[2,48,8,128]{3,2,1,0:T(8,128)S(1)}, u32[]{:S(2)}, u32[]{:S(2)}) %collective-permute-start.26) | collective-permute-done | bytes 393248 | tf_op jit(solution)/shard_map/ppermute | solution.py:257
  209.8 3.6 %collective-permute-start.29 = (f32[1,48,8,128]{3,2,1,0:T(8,128)S(1)}, f32[1,48,8,128]{3,2,1,0:T(8,128)S(1)}, u32[]{:S(2)}, u32[]{:S(2)}) collective-permute-start(f32[1,48,8,128]{3,2,1,0:T(8,128)S(1)} %get-tuple-element.72), channel_id=1, source_target_pairs={{0,192},{32,224},{64,0},{96,32},{128,64},{160,96},{192,128},{224,1... | collective-permute-start | bytes 589832 | tf_op jit(solution)/shard_map/ppermute | solution.py:261
  213.4 9.2 %collective-permute-done.28 = f32[1,48,8,128]{3,2,1,0:T(8,128)S(1)} collective-permute-done((f32[1,48,8,128]{3,2,1,0:T(8,128)S(1)}, f32[1,48,8,128]{3,2,1,0:T(8,128)S(1)}, u32[]{:S(2)}, u32[]{:S(2)}) %collective-permute-start.28) | collective-permute-done | bytes 196640 | tf_op jit(solution)/shard_map/ppermute | solution.py:257
  223.1 3.6 %collective-permute-start.32 = (f32[2,48,8,128]{3,2,1,0:T(8,128)S(1)}, f32[2,48,8,128]{3,2,1,0:T(8,128)S(1)}, u32[]{:S(2)}, u32[]{:S(2)}) collective-permute-start(f32[2,48,8,128]{3,2,1,0:T(8,128)S(1)} %fusion.2.refs_6_), channel_id=1, source_target_pairs={{0,192},{32,224},{64,0},{96,32},{128,64},{160,96},{192,128},{224,1... | collective-permute-start | bytes 1179656 | tf_op jit(solution)/shard_map/ppermute | solution.py:261
  226.6 8.5 %collective-permute-done.30 = f32[2,48,8,128]{3,2,1,0:T(8,128)S(1)} collective-permute-done((f32[2,48,8,128]{3,2,1,0:T(8,128)S(1)}, f32[2,48,8,128]{3,2,1,0:T(8,128)S(1)}, u32[]{:S(2)}, u32[]{:S(2)}) %collective-permute-start.30) | collective-permute-done | bytes 393248 | tf_op jit(solution)/shard_map/ppermute | solution.py:257
  235.4 10.9 %collective-permute-start.35 = (f32[6,48,8,128]{3,2,1,0:T(8,128)S(1)}, f32[6,48,8,128]{3,2,1,0:T(8,128)S(1)}, u32[]{:S(2)}, u32[]{:S(2)}) collective-permute-start(f32[6,48,8,128]{3,2,1,0:T(8,128)S(1)} %pad_maximum_fusion.2), channel_id=1, source_target_pairs={{0,32},{32,0},{64,96},{96,64},{128,160},{160,128},{192,224},{224,1... | collective-permute-start | bytes 3538952 | tf_op jit(solution)/shard_map/ppermute | solution.py:253
  246.3 3.3 %collective-permute-start.33 = (f32[1,48,8,128]{3,2,1,0:T(8,128)S(1)}, f32[1,48,8,128]{3,2,1,0:T(8,128)S(1)}, u32[]{:S(2)}, u32[]{:S(2)}) collective-permute-start(f32[1,48,8,128]{3,2,1,0:T(8,128)S(1)} %get-tuple-element.128.refs_1_), channel_id=1, source_target_pairs={{0,192},{32,224},{64,0},{96,32},{128,64},{160,96},{192,128},{224,1... | collective-permute-start | bytes 589832 | tf_op jit(solution)/shard_map/ppermute | solution.py:261
  249.6 10.6 %collective-permute-done.33.refs_2_ = f32[1,48,8,128]{3,2,1,0:T(8,128)S(1)} collective-permute-done((f32[1,48,8,128]{3,2,1,0:T(8,128)S(1)}, f32[1,48,8,128]{3,2,1,0:T(8,128)S(1)}, u32[]{:S(2)}, u32[]{:S(2)}) %collective-permute-start.33) | collective-permute-done | bytes 196640 | tf_op jit(solution)/shard_map/ppermute | solution.py:261
  262.4 2.6 place.1
  (121 shorter events, 19.3 us)
Async XLA Ops:
  0.0 8.7 %copy-start.2 = (f32[1,128,128]{2,1,0:T(8,128)S(1)}, f32[1,128,128]{2,1,0:T(8,128)}, u32[]{:S(2)}) copy-start(f32[1,128,128]{2,1,0:T(8,128)} %param.7) | copy-start | bytes 196612
  0.0 8.7 %copy-start.3 = (f32[1,128,128]{2,1,0:T(8,128)S(1)}, f32[1,128,128]{2,1,0:T(8,128)}, u32[]{:S(2)}) copy-start(f32[1,128,128]{2,1,0:T(8,128)} %param.8) | copy-start | bytes 196612
  0.0 8.7 %copy-start.4 = (f32[1,33]{1,0:T(1,128)S(1)}, f32[1,33]{1,0:T(1,128)}, u32[]{:S(2)}) copy-start(f32[1,33]{1,0:T(1,128)} %taps.1) | copy-start | bytes 400
  3.2 26.2 %collective-permute-start = (f32[32,64,128]{2,1,0:T(8,128)}, f32[32,64,128]{2,1,0:T(8,128)}, u32[]{:S(2)}, u32[]{:S(2)}) collective-permute-start(f32[32,64,128]{2,1,0:T(8,128)} %get-tuple-element.76), channel_id=1, source_target_pairs={{0,1},{1,2},{2,3},{3,4},{4,5},{5,6},{6,7},{7,8},{8,9},{9,10},{10,1... | collective-permute-start | bytes 3145736 | tf_op jit(solution)/shard_map/ppermute | solution.py:266
  6.3 28.0 %collective-permute-start.1 = (f32[32,64,128]{2,1,0:T(8,128)}, f32[32,64,128]{2,1,0:T(8,128)}, u32[]{:S(2)}, u32[]{:S(2)}) collective-permute-start(f32[32,64,128]{2,1,0:T(8,128)} %get-tuple-element.75), channel_id=1, source_target_pairs={{1,0},{2,1},{3,2},{4,3},{5,4},{6,5},{7,6},{8,7},{9,8},{10,9},{11,1... | collective-permute-start | bytes 3145736 | tf_op jit(solution)/shard_map/ppermute | solution.py:271
  10.6 30.9 %copy-start = (f32[48,128,128]{2,1,0:T(8,128)S(1)}, f32[48,128,128]{2,1,0:T(8,128)}, u32[]{:S(2)}) copy-start(f32[48,128,128]{2,1,0:T(8,128)} %refs_0_.1) | copy-start | bytes 9437188
  12.3 54.0 %copy-start.5 = (f32[128,48,128]{2,1,0:T(8,128)}, f32[128,48,128]{2,1,0:T(8,128)S(1)}, u32[]{:S(2)}) copy-start(f32[128,48,128]{2,1,0:T(8,128)S(1)} %get-tuple-element.50.mo) | copy-start | bytes 9437188
  12.3 54.0 %copy-start.11 = (bf16[256,256]{1,0:T(8,128)(2,1)}, bf16[256,256]{1,0:T(8,128)(2,1)S(1)}, u32[]{:S(2)}) copy-start(bf16[256,256]{1,0:T(8,128)(2,1)S(1)} %get-tuple-element.54.left_ref) | copy-start | bytes 393220
  12.3 54.0 %copy-start.13 = (bf16[256,256]{1,0:T(8,128)(2,1)}, bf16[256,256]{1,0:T(8,128)(2,1)S(1)}, u32[]{:S(2)}) copy-start(bf16[256,256]{1,0:T(8,128)(2,1)S(1)} %get-tuple-element.55.right_ref) | copy-start | bytes 393220
  12.3 54.0 %copy-start.15 = (bf16[160,224]{1,0:T(8,128)(2,1)}, bf16[160,224]{1,0:T(8,128)(2,1)S(1)}, u32[]{:S(2)}) copy-start(bf16[160,224]{1,0:T(8,128)(2,1)S(1)} %get-tuple-element.52.tf_ref) | copy-start | bytes 215044
  12.3 54.0 %copy-start.17 = (bf16[96,160]{1,0:T(8,128)(2,1)}, bf16[96,160]{1,0:T(8,128)(2,1)S(1)}, u32[]{:S(2)}) copy-start(bf16[96,160]{1,0:T(8,128)(2,1)S(1)} %get-tuple-element.53.ta_ref) | copy-start | bytes 92164
  34.3 9.5 %collective-permute-start.2 = (f32[32,64,128]{2,1,0:T(8,128)}, f32[32,64,128]{2,1,0:T(8,128)S(1)}, u32[]{:S(2)}, u32[]{:S(2)}) collective-permute-start(f32[32,64,128]{2,1,0:T(8,128)} %collective-permute-done.refs_0_), channel_id=1, source_target_pairs={{0,32},{32,0},{64,96},{96,64},{128,160},{160,128},{192,224},{224,1... | collective-permute-start | bytes 3145736 | tf_op jit(solution)/shard_map/ppermute | solution.py:253
  36.2 7.6 %collective-permute-start.3 = (f32[32,64,128]{2,1,0:T(8,128)}, f32[32,64,128]{2,1,0:T(8,128)S(1)}, u32[]{:S(2)}, u32[]{:S(2)}) collective-permute-start(f32[32,64,128]{2,1,0:T(8,128)} %collective-permute-done.1.refs_2_), channel_id=1, source_target_pairs={{0,32},{32,0},{64,96},{96,64},{128,160},{160,128},{192,224},{224,1... | collective-permute-start | bytes 3145736 | tf_op jit(solution)/shard_map/ppermute | solution.py:253
  36.2 26.1 %collective-permute-start.4 = (f32[128,16,128]{2,1,0:T(8,128)S(1)}, f32[128,16,128]{2,1,0:T(8,128)S(1)}, u32[]{:S(2)}, u32[]{:S(2)}) collective-permute-start(f32[128,16,128]{2,1,0:T(8,128)S(1)} %get-tuple-element.49), channel_id=1, source_target_pairs={{0,1},{1,2},{2,3},{3,4},{4,5},{5,6},{6,7},{7,8},{8,9},{9,10},{10,1... | collective-permute-start | bytes 3145736 | tf_op jit(solution)/shard_map/ppermute | solution.py:266
  38.1 28.2 %collective-permute-start.5 = (f32[128,16,128]{2,1,0:T(8,128)S(1)}, f32[128,16,128]{2,1,0:T(8,128)S(1)}, u32[]{:S(2)}, u32[]{:S(2)}) collective-permute-start(f32[128,16,128]{2,1,0:T(8,128)S(1)} %get-tuple-element.51), channel_id=1, source_target_pairs={{1,0},{2,1},{3,2},{4,3},{5,4},{6,5},{7,6},{8,7},{9,8},{10,9},{11,1... | collective-permute-start | bytes 3145736 | tf_op jit(solution)/shard_map/ppermute | solution.py:271
  62.3 10.8 %copy-start.7 = (f32[128,16,128]{2,1,0:T(8,128)}, f32[128,16,128]{2,1,0:T(8,128)S(1)}, u32[]{:S(2)}) copy-start(f32[128,16,128]{2,1,0:T(8,128)S(1)} %collective-permute-done.4.mb) | copy-start | bytes 3145732
  73.1 4.5 %collective-permute-start.6 = (f32[8,48,8,128]{3,2,1,0:T(8,128)S(1)}, f32[8,48,8,128]{3,2,1,0:T(8,128)S(1)}, u32[]{:S(2)}, u32[]{:S(2)}) collective-permute-start(f32[8,48,8,128]{3,2,1,0:T(8,128)S(1)} %get-tuple-element.57), channel_id=1, source_target_pairs={{0,32},{32,0},{64,96},{96,64},{128,160},{160,128},{192,224},{224,1... | collective-permute-start | bytes 4718600 | tf_op jit(solution)/shard_map/ppermute | solution.py:253
  77.7 24.9 %copy-start.19 = (f32[8,48,8,128]{3,2,1,0:T(8,128)}, f32[8,48,8,128]{3,2,1,0:T(8,128)S(1)}, u32[]{:S(2)}) copy-start(f32[8,48,8,128]{3,2,1,0:T(8,128)S(1)} %add.111) | copy-start | bytes 4718596
  77.8 18.2 %collective-permute-start.7 = (f32[2,48,8,128]{3,2,1,0:T(8,128)S(1)}, f32[2,48,8,128]{3,2,1,0:T(8,128)S(1)}, u32[]{:S(2)}, u32[]{:S(2)}) collective-permute-start(f32[2,48,8,128]{3,2,1,0:T(8,128)S(1)} %get-tuple-element.100), channel_id=1, source_target_pairs={{0,64},{32,96},{64,128},{96,160},{128,192},{160,224},{192,0},{224,... | collective-permute-start | bytes 1179656 | tf_op jit(solution)/shard_map/ppermute | solution.py:257
  80.9 21.8 %collective-permute-start.8 = (f32[2,48,8,128]{3,2,1,0:T(8,128)S(1)}, f32[2,48,8,128]{3,2,1,0:T(8,128)S(1)}, u32[]{:S(2)}, u32[]{:S(2)}) collective-permute-start(f32[2,48,8,128]{3,2,1,0:T(8,128)S(1)} %get-tuple-element.99), channel_id=1, source_target_pairs={{0,192},{32,224},{64,0},{96,32},{128,64},{160,96},{192,128},{224,1... | collective-permute-start | bytes 1179656 | tf_op jit(solution)/shard_map/ppermute | solution.py:261
  96.1 7.5 %copy-start.20 = (f32[2,48,8,128]{3,2,1,0:T(8,128)}, f32[2,48,8,128]{3,2,1,0:T(8,128)S(1)}, u32[]{:S(2)}) copy-start(f32[2,48,8,128]{3,2,1,0:T(8,128)S(1)} %collective-permute-done.7) | copy-start | bytes 1179652
  103.5 12.6 %collective-permute-start.9 = (f32[1,48,8,128]{3,2,1,0:T(8,128)}, f32[1,48,8,128]{3,2,1,0:T(8,128)}, u32[]{:S(2)}, u32[]{:S(2)}) collective-permute-start(f32[1,48,8,128]{3,2,1,0:T(8,128)} %get-tuple-element.60), channel_id=1, source_target_pairs={{0,64},{32,96},{64,128},{96,160},{128,192},{160,224},{192,0},{224,... | collective-permute-start | bytes 589832 | tf_op jit(solution)/shard_map/ppermute | solution.py:257
  106.9 9.2 %collective-permute-start.10 = (f32[1,48,8,128]{3,2,1,0:T(8,128)}, f32[1,48,8,128]{3,2,1,0:T(8,128)}, u32[]{:S(2)}, u32[]{:S(2)}) collective-permute-start(f32[1,48,8,128]{3,2,1,0:T(8,128)} %get-tuple-element.61), channel_id=1, source_target_pairs={{0,192},{32,224},{64,0},{96,32},{128,64},{160,96},{192,128},{224,1... | collective-permute-start | bytes 589832 | tf_op jit(solution)/shard_map/ppermute | solution.py:261
  117.6 14.9 %collective-permute-start.11 = (f32[2,48,8,128]{3,2,1,0:T(8,128)S(1)}, f32[2,48,8,128]{3,2,1,0:T(8,128)S(1)}, u32[]{:S(2)}, u32[]{:S(2)}) collective-permute-start(f32[2,48,8,128]{3,2,1,0:T(8,128)S(1)} %maximum_multiply_fusion.refs_6_), channel_id=1, source_target_pairs={{0,64},{32,96},{64,128},{96,160},{128,192},{160,224},{192,0},{224,... | collective-permute-start | bytes 1179656 | tf_op jit(solution)/shard_map/ppermute | solution.py:257
  119.9 12.9 %collective-permute-start.13 = (f32[2,48,8,128]{3,2,1,0:T(8,128)S(1)}, f32[2,48,8,128]{3,2,1,0:T(8,128)S(1)}, u32[]{:S(2)}, u32[]{:S(2)}) collective-permute-start(f32[2,48,8,128]{3,2,1,0:T(8,128)S(1)} %maximum_multiply_fusion.refs_6_), channel_id=1, source_target_pairs={{0,192},{32,224},{64,0},{96,32},{128,64},{160,96},{192,128},{224,1... | collective-permute-start | bytes 1179656 | tf_op jit(solution)/shard_map/ppermute | solution.py:261
  132.6 9.4 %collective-permute-start.12 = (f32[1,48,8,128]{3,2,1,0:T(8,128)S(1)}, f32[1,48,8,128]{3,2,1,0:T(8,128)S(1)}, u32[]{:S(2)}, u32[]{:S(2)}) collective-permute-start(f32[1,48,8,128]{3,2,1,0:T(8,128)S(1)} %get-tuple-element.132.refs_3_), channel_id=1, source_target_pairs={{0,64},{32,96},{64,128},{96,160},{128,192},{160,224},{192,0},{224,... | collective-permute-start | bytes 589832 | tf_op jit(solution)/shard_map/ppermute | solution.py:257
  132.9 11.8 %collective-permute-start.14 = (f32[1,48,8,128]{3,2,1,0:T(8,128)S(1)}, f32[1,48,8,128]{3,2,1,0:T(8,128)S(1)}, u32[]{:S(2)}, u32[]{:S(2)}) collective-permute-start(f32[1,48,8,128]{3,2,1,0:T(8,128)S(1)} %get-tuple-element.134.refs_1_), channel_id=1, source_target_pairs={{0,192},{32,224},{64,0},{96,32},{128,64},{160,96},{192,128},{224,1... | collective-permute-start | bytes 589832 | tf_op jit(solution)/shard_map/ppermute | solution.py:261
  136.7 34.3 %collective-permute-start.16 = (f32[4,32,8,128]{3,2,1,0:T(8,128)S(1)}, f32[4,32,8,128]{3,2,1,0:T(8,128)S(1)}, u32[]{:S(2)}, u32[]{:S(2)}) collective-permute-start(f32[4,32,8,128]{3,2,1,0:T(8,128)S(1)} %get-tuple-element.110), channel_id=1, source_target_pairs={{0,1},{1,2},{2,3},{3,4},{4,5},{5,6},{6,7},{7,8},{8,9},{9,10},{10,1... | collective-permute-start | bytes 1572872 | tf_op jit(solution)/shard_map/ppermute | solution.py:266
  138.6 32.4 %collective-permute-start.21 = (f32[4,32,8,128]{3,2,1,0:T(8,128)S(1)}, f32[4,32,8,128]{3,2,1,0:T(8,128)S(1)}, u32[]{:S(2)}, u32[]{:S(2)}) collective-permute-start(f32[4,32,8,128]{3,2,1,0:T(8,128)S(1)} %get-tuple-element.109), channel_id=1, source_target_pairs={{1,0},{2,1},{3,2},{4,3},{5,4},{6,5},{7,6},{8,7},{9,8},{10,9},{11,1... | collective-permute-start | bytes 1572872 | tf_op jit(solution)/shard_map/ppermute | solution.py:271
  144.7 11.3 %collective-permute-start.15 = (f32[2,32,8,128]{3,2,1,0:T(8,128)S(1)}, f32[2,32,8,128]{3,2,1,0:T(8,128)S(1)}, u32[]{:S(2)}, u32[]{:S(2)}) collective-permute-start(f32[2,32,8,128]{3,2,1,0:T(8,128)S(1)} %get-tuple-element.138), channel_id=1, source_target_pairs={{0,1},{1,2},{2,3},{3,4},{4,5},{5,6},{6,7},{7,8},{8,9},{9,10},{10,1... | collective-permute-start | bytes 786440 | tf_op jit(solution)/shard_map/ppermute | solution.py:266
  146.6 13.4 %collective-permute-start.18 = (f32[2,32,8,128]{3,2,1,0:T(8,128)S(1)}, f32[2,32,8,128]{3,2,1,0:T(8,128)S(1)}, u32[]{:S(2)}, u32[]{:S(2)}) collective-permute-start(f32[2,32,8,128]{3,2,1,0:T(8,128)S(1)} %get-tuple-element.137), channel_id=1, source_target_pairs={{1,0},{2,1},{3,2},{4,3},{5,4},{6,5},{7,6},{8,7},{9,8},{10,9},{11,1... | collective-permute-start | bytes 786440 | tf_op jit(solution)/shard_map/ppermute | solution.py:271
  150.1 12.6 %collective-permute-start.17 = (f32[2,32,8,128]{3,2,1,0:T(8,128)S(1)}, f32[2,32,8,128]{3,2,1,0:T(8,128)S(1)}, u32[]{:S(2)}, u32[]{:S(2)}) collective-permute-start(f32[2,32,8,128]{3,2,1,0:T(8,128)S(1)} %get-tuple-element.136), channel_id=1, source_target_pairs={{0,1},{1,2},{2,3},{3,4},{4,5},{5,6},{6,7},{7,8},{8,9},{9,10},{10,1... | collective-permute-start | bytes 786440 | tf_op jit(solution)/shard_map/ppermute | solution.py:266
  156.0 9.2 %collective-permute-start.20 = (f32[2,32,8,128]{3,2,1,0:T(8,128)S(1)}, f32[2,32,8,128]{3,2,1,0:T(8,128)S(1)}, u32[]{:S(2)}, u32[]{:S(2)}) collective-permute-start(f32[2,32,8,128]{3,2,1,0:T(8,128)S(1)} %get-tuple-element.135), channel_id=1, source_target_pairs={{1,0},{2,1},{3,2},{4,3},{5,4},{6,5},{7,6},{8,7},{9,8},{10,9},{11,1... | collective-permute-start | bytes 786440 | tf_op jit(solution)/shard_map/ppermute | solution.py:271
  160.1 12.5 %collective-permute-start.24 = (f32[6,48,8,128]{3,2,1,0:T(8,128)S(1)}, f32[6,48,8,128]{3,2,1,0:T(8,128)S(1)}, u32[]{:S(2)}, u32[]{:S(2)}) collective-permute-start(f32[6,48,8,128]{3,2,1,0:T(8,128)S(1)} %pad_maximum_fusion.1), channel_id=1, source_target_pairs={{0,32},{32,0},{64,96},{96,64},{128,160},{160,128},{192,224},{224,1... | collective-permute-start | bytes 3538952 | tf_op jit(solution)/shard_map/ppermute | solution.py:253
  162.7 8.6 %collective-permute-start.23 = (f32[2,48,8,128]{3,2,1,0:T(8,128)S(1)}, f32[2,48,8,128]{3,2,1,0:T(8,128)S(1)}, u32[]{:S(2)}, u32[]{:S(2)}) collective-permute-start(f32[2,48,8,128]{3,2,1,0:T(8,128)S(1)} %constant_dynamic-update-slice_fusion), channel_id=1, source_target_pairs={{0,32},{32,0},{64,96},{96,64},{128,160},{160,128},{192,224},{224,1... | collective-permute-start | bytes 1179656 | tf_op jit(solution)/shard_map/ppermute | solution.py:253
  165.2 7.3 %collective-permute-start.19 = (f32[4,32,8,128]{3,2,1,0:T(8,128)S(1)}, f32[4,32,8,128]{3,2,1,0:T(8,128)S(1)}, u32[]{:S(2)}, u32[]{:S(2)}) collective-permute-start(f32[4,32,8,128]{3,2,1,0:T(8,128)S(1)} %pad_maximum_fusion.3), channel_id=1, source_target_pairs={{0,32},{32,0},{64,96},{96,64},{128,160},{160,128},{192,224},{224,1... | collective-permute-start | bytes 1572872 | tf_op jit(solution)/shard_map/ppermute | solution.py:253
  171.1 3.9 %collective-permute-start.22 = (f32[12,32,8,128]{3,2,1,0:T(8,128)S(1)}, f32[12,32,8,128]{3,2,1,0:T(8,128)S(1)}, u32[]{:S(2)}, u32[]{:S(2)}) collective-permute-start(f32[12,32,8,128]{3,2,1,0:T(8,128)S(1)} %pad_maximum_fusion), channel_id=1, source_target_pairs={{0,32},{32,0},{64,96},{96,64},{128,160},{160,128},{192,224},{224,1... | collective-permute-start | bytes 4718600 | tf_op jit(solution)/shard_map/ppermute | solution.py:253
  185.0 3.5 %collective-permute-start.25 = (f32[8,48,8,128]{3,2,1,0:T(8,128)S(1)}, f32[8,48,8,128]{3,2,1,0:T(8,128)S(1)}, u32[]{:S(2)}, u32[]{:S(2)}) collective-permute-start(f32[8,48,8,128]{3,2,1,0:T(8,128)S(1)} %get-tuple-element.68), channel_id=1, source_target_pairs={{0,32},{32,0},{64,96},{96,64},{128,160},{160,128},{192,224},{224,1... | collective-permute-start | bytes 4718600 | tf_op jit(solution)/shard_map/ppermute | solution.py:253
  188.8 20.9 %collective-permute-start.26 = (f32[2,48,8,128]{3,2,1,0:T(8,128)S(1)}, f32[2,48,8,128]{3,2,1,0:T(8,128)S(1)}, u32[]{:S(2)}, u32[]{:S(2)}) collective-permute-start(f32[2,48,8,128]{3,2,1,0:T(8,128)S(1)} %get-tuple-element.84), channel_id=1, source_target_pairs={{0,64},{32,96},{64,128},{96,160},{128,192},{160,224},{192,0},{224,... | collective-permute-start | bytes 1179656 | tf_op jit(solution)/shard_map/ppermute | solution.py:257
  188.9 20.9 %collective-permute-start.27 = (f32[2,48,8,128]{3,2,1,0:T(8,128)S(1)}, f32[2,48,8,128]{3,2,1,0:T(8,128)S(1)}, u32[]{:S(2)}, u32[]{:S(2)}) collective-permute-start(f32[2,48,8,128]{3,2,1,0:T(8,128)S(1)} %get-tuple-element.83), channel_id=1, source_target_pairs={{0,192},{32,224},{64,0},{96,32},{128,64},{160,96},{192,128},{224,1... | collective-permute-start | bytes 1179656 | tf_op jit(solution)/shard_map/ppermute | solution.py:261
  209.8 12.8 %collective-permute-start.28 = (f32[1,48,8,128]{3,2,1,0:T(8,128)S(1)}, f32[1,48,8,128]{3,2,1,0:T(8,128)S(1)}, u32[]{:S(2)}, u32[]{:S(2)}) collective-permute-start(f32[1,48,8,128]{3,2,1,0:T(8,128)S(1)} %get-tuple-element.71), channel_id=1, source_target_pairs={{0,64},{32,96},{64,128},{96,160},{128,192},{160,224},{192,0},{224,... | collective-permute-start | bytes 589832 | tf_op jit(solution)/shard_map/ppermute | solution.py:257
  209.8 12.7 %collective-permute-start.29 = (f32[1,48,8,128]{3,2,1,0:T(8,128)S(1)}, f32[1,48,8,128]{3,2,1,0:T(8,128)S(1)}, u32[]{:S(2)}, u32[]{:S(2)}) collective-permute-start(f32[1,48,8,128]{3,2,1,0:T(8,128)S(1)} %get-tuple-element.72), channel_id=1, source_target_pairs={{0,192},{32,224},{64,0},{96,32},{128,64},{160,96},{192,128},{224,1... | collective-permute-start | bytes 589832 | tf_op jit(solution)/shard_map/ppermute | solution.py:261
  222.8 12.4 %collective-permute-start.30 = (f32[2,48,8,128]{3,2,1,0:T(8,128)S(1)}, f32[2,48,8,128]{3,2,1,0:T(8,128)S(1)}, u32[]{:S(2)}, u32[]{:S(2)}) collective-permute-start(f32[2,48,8,128]{3,2,1,0:T(8,128)S(1)} %fusion.2.refs_6_), channel_id=1, source_target_pairs={{0,64},{32,96},{64,128},{96,160},{128,192},{160,224},{192,0},{224,... | collective-permute-start | bytes 1179656 | tf_op jit(solution)/shard_map/ppermute | solution.py:257
  223.1 12.2 %collective-permute-start.32 = (f32[2,48,8,128]{3,2,1,0:T(8,128)S(1)}, f32[2,48,8,128]{3,2,1,0:T(8,128)S(1)}, u32[]{:S(2)}, u32[]{:S(2)}) collective-permute-start(f32[2,48,8,128]{3,2,1,0:T(8,128)S(1)} %fusion.2.refs_6_), channel_id=1, source_target_pairs={{0,192},{32,224},{64,0},{96,32},{128,64},{160,96},{192,128},{224,1... | collective-permute-start | bytes 1179656 | tf_op jit(solution)/shard_map/ppermute | solution.py:261
  235.2 14.4 %collective-permute-start.31 = (f32[1,48,8,128]{3,2,1,0:T(8,128)S(1)}, f32[1,48,8,128]{3,2,1,0:T(8,128)S(1)}, u32[]{:S(2)}, u32[]{:S(2)}) collective-permute-start(f32[1,48,8,128]{3,2,1,0:T(8,128)S(1)} %get-tuple-element.126.refs_3_), channel_id=1, source_target_pairs={{0,64},{32,96},{64,128},{96,160},{128,192},{160,224},{192,0},{224,... | collective-permute-start | bytes 589832 | tf_op jit(solution)/shard_map/ppermute | solution.py:257
  235.4 26.9 %collective-permute-start.35 = (f32[6,48,8,128]{3,2,1,0:T(8,128)S(1)}, f32[6,48,8,128]{3,2,1,0:T(8,128)S(1)}, u32[]{:S(2)}, u32[]{:S(2)}) collective-permute-start(f32[6,48,8,128]{3,2,1,0:T(8,128)S(1)} %pad_maximum_fusion.2), channel_id=1, source_target_pairs={{0,32},{32,0},{64,96},{96,64},{128,160},{160,128},{192,224},{224,1... | collective-permute-start | bytes 3538952 | tf_op jit(solution)/shard_map/ppermute | solution.py:253
  246.3 13.9 %collective-permute-start.33 = (f32[1,48,8,128]{3,2,1,0:T(8,128)S(1)}, f32[1,48,8,128]{3,2,1,0:T(8,128)S(1)}, u32[]{:S(2)}, u32[]{:S(2)}) collective-permute-start(f32[1,48,8,128]{3,2,1,0:T(8,128)S(1)} %get-tuple-element.128.refs_1_), channel_id=1, source_target_pairs={{0,192},{32,224},{64,0},{96,32},{128,64},{160,96},{192,128},{224,1... | collective-permute-start | bytes 589832 | tf_op jit(solution)/shard_map/ppermute | solution.py:261
  260.3 2.0 collective-permute-start.34
  (10 other events, 31.5 us)

commit v3 on v2

--- a/solution.py
+++ b/solution.py
@@ -91,29 +91,24 @@
     )(*ins, left, right)
 
 
-def middle_kernel(sb, so, sa, mb, mo, ma, tf_ref, ta_ref, left_ref, right_ref, own, other, back):
-    tf = tf_ref[...]
-    ta = ta_ref[...]
-
-    def smooth(a):
-        return jnp.concatenate([r[pl.ds(a, r.shape[0] // PITCH, stride=PITCH), :] for r in (sb, so, sa)], 0)
-
-    def recorded(a):
-        return jnp.concatenate([r[a] for r in (mb, mo, ma)], 0)
-
-    @pl.loop(0, N // STEP)
-    def _(i):
-        firsts = [STEP * i + j for j in range(0, STEP, 2)]
-        blurred = [left_product(tf, jnp.concatenate([smooth(a), smooth(a + 1)], 1)) for a in firsts]
-        ratios = []
-        for a, blur in zip(firsts, blurred):
-            rec = jnp.concatenate([recorded(a), recorded(a + 1)], 1)
-            ratios.append(jnp.where(rec > 0, rec / blur, 0.0))
-        for a, ratio in zip(firsts, ratios):
-            res = left_product(ta, ratio)
-            back[pl.ds(a, SLAB, stride=PITCH), :] = res[:, :N]
-            back[pl.ds(a + 1, SLAB, stride=PITCH), :] = res[:, N:]
-
+def strided(refs, a):
+    return jnp.concatenate([r[pl.ds(a, r.shape[0] // PITCH, stride=PITCH), :] for r in refs], 0)
+
+
+def at_row(refs, a):
+    return jnp.concatenate([r[a] for r in refs], 0)
+
+
+def pair(pick, refs, a):
+    return jnp.concatenate([pick(refs, a), pick(refs, a + 1)], 1)
+
+
+def store_back(back, a, res):
+    back[pl.ds(a, SLAB, stride=PITCH), :] = res[:, :N]
+    back[pl.ds(a + 1, SLAB, stride=PITCH), :] = res[:, N:]
+
+
+def logs_out(back, left_ref, right_ref, own, other):
     left = left_ref[...]
     right = right_ref[...]
 
@@ -127,19 +122,80 @@
                 other[p, z] = logs[j * N + 64 + 8 * p : j * N + 64 + 8 * p + 8]
 
 
+def ratio_kernel(sb, so, sa, rec, tf_ref, out, first, last):
+    tf = tf_ref[...]
+
+    @pl.loop(0, N // STEP)
+    def _(i):
+        firsts = [STEP * i + j for j in range(0, STEP, 2)]
+        blurred = [left_product(tf, pair(strided, (sb, so, sa), a)) for a in firsts]
+        for a, blur in zip(firsts, blurred):
+            both = pair(at_row, (rec,), a) / blur
+            for k in range(2):
+                ratio = both[:, k * N : k * N + N]
+                out[a + k] = ratio
+                first[a + k] = ratio[:HALF]
+                last[a + k] = ratio[SLAB - HALF :]
+
+
+def adjoint_kernel(rb, ro, ra, ta_ref, left_ref, right_ref, own, other, back):
+    ta = ta_ref[...]
+
+    @pl.loop(0, N // STEP)
+    def _(i):
+        for a in [STEP * i + j for j in range(0, STEP, 2)]:
+            store_back(back, a, left_product(ta, pair(at_row, (rb, ro, ra), a)))
+
+    logs_out(back, left_ref, right_ref, own, other)
+
+
+def middle_kernel(sb, so, sa, mb, mo, ma, tf_ref, ta_ref, left_ref, right_ref, own, other, back):
+    tf = tf_ref[...]
+    ta = ta_ref[...]
+
+    @pl.loop(0, N // STEP)
+    def _(i):
+        firsts = [STEP * i + j for j in range(0, STEP, 2)]
+        blurred = [left_product(tf, pair(strided, (sb, so, sa), a)) for a in firsts]
+        ratios = []
+        for a, blur in zip(firsts, blurred):
+            rec = pair(at_row, (mb, mo, ma), a)
+            ratios.append(jnp.where(rec > 0, rec / blur, 0.0))
+        for a, ratio in zip(firsts, ratios):
+            store_back(back, a, left_product(ta, ratio))
+
+    logs_out(back, left_ref, right_ref, own, other)
+
+
+def kernel_call(kernel, ins, outs, scratch, flops, name):
+    return pl.pallas_call(
+        kernel,
+        out_shape=outs,
+        in_specs=[pl.BlockSpec(memory_space=pltpu.VMEM)] * len(ins),
+        out_specs=[pl.BlockSpec(memory_space=pltpu.VMEM)] * len(outs),
+        scratch_shapes=scratch,
+        compiler_params=pltpu.CompilerParams(vmem_limit_bytes=32 * MIB),
+        cost_estimate=pl.CostEstimate(flops=flops, bytes_accessed=15 * MIB, transcendentals=SLAB * N * N),
+        name=name,
+    )(*ins)
+
+
+def ratio_of(smooth, recorded, tf):
+    edge = jax.ShapeDtypeStruct((N, HALF, N), F32)
+    outs = [jax.ShapeDtypeStruct((N, SLAB, N), F32), edge, edge]
+    return kernel_call(ratio_kernel, (*smooth, recorded, tf), outs, [], 3 * 10**9, "ratio")
+
+
+def adjoint(ratios, ta, left, right):
+    half = jax.ShapeDtypeStruct((8, SLAB, 8, N), F32)
+    back = [pltpu.VMEM((SLAB * PITCH, N), F32)]
+    return kernel_call(adjoint_kernel, (*ratios, ta, left, right), [half, half], back, 5 * 10**9, "adjoint")
+
+
 def middle(smooth, recorded, tf, ta, left, right):
-    ins = [*smooth, *recorded, tf, ta, left, right]
     half = jax.ShapeDtypeStruct((8, SLAB, 8, N), F32)
-    return pl.pallas_call(
-        middle_kernel,
-        out_shape=[half, half],
-        in_specs=[pl.BlockSpec(memory_space=pltpu.VMEM)] * len(ins),
-        out_specs=[pl.BlockSpec(memory_space=pltpu.VMEM)] * 2,
-        scratch_shapes=[pltpu.VMEM((SLAB * PITCH, N), F32)],
-        compiler_params=pltpu.CompilerParams(vmem_limit_bytes=32 * MIB),
-        cost_estimate=pl.CostEstimate(flops=8 * 10**9, bytes_accessed=15 * MIB, transcendentals=SLAB * N * N),
-        name="middle",
-    )(*ins)
+    back = [pltpu.VMEM((SLAB * PITCH, N), F32)]
+    return kernel_call(middle_kernel, (*smooth, *recorded, tf, ta, left, right), [half, half], back, 8 * 10**9, "middle")
 
 
 def operand_rows(m):
@@ -158,7 +214,7 @@
 
 def prep_kernel(
     starts, taps, mx_ref, my_ref, rec,
-    tf, ta, x_all, x_halves, x_pieces, adj_x, fwd_y, adj_y, rec_t, rec_first, rec_last, xt_ref,
+    tf, ts, ta, x_all, x_halves, x_pieces, adj_x, fwd_y, adj_y, rec_t, rec_first, rec_last, xt_ref,
 ):
     def toeplitz(rows, cols, flip):
         i = lax.broadcasted_iota(jnp.int32, (rows, 2 * cols), 0)
@@ -170,6 +226,7 @@
         return out
 
     tf[...] = operand_rows(toeplitz(SLAB + 2 * HALF, SLAB + 2 * FAR, False))
+    ts[...] = operand_rows(toeplitz(SLAB, SLAB + 2 * HALF, False))
     ta[...] = operand_rows(toeplitz(SLAB, SLAB + 2 * HALF, True))
     mx = mx_ref[...]
     my = my_ref[...]
@@ -209,6 +266,7 @@
     edge = jax.ShapeDtypeStruct((N, HALF, N), F32)
     outs = [
         jax.ShapeDtypeStruct((2 * full, 2 * wide), BF16),
+        jax.ShapeDtypeStruct((2 * SLAB, 2 * full), BF16),
         jax.ShapeDtypeStruct((2 * SLAB, 2 * full), BF16),
         *[square] * 6,
         jax.ShapeDtypeStruct((N, SLAB, N), F32),
@@ -271,20 +329,21 @@
     return lax.ppermute(x, "gz", [(i + 1, i) for i in range(n - 1)])
 
 
-def reduce_chunk(other, own):
+def reduce_chunk(other, own, beside=None):
     total = own + to_core(other)
     from_prev = to_next(total[0:2])
     from_next = to_prev(total[2:4])
+    extra = beside(total) if beside else ()
     from_prev, from_next = lax.optimization_barrier((from_prev, from_next))
     fwd_next = total[4:5] + from_prev[0:1]
     fwd_prev = total[5:6] + from_next[0:1]
     fwd_next, fwd_prev = lax.optimization_barrier((fwd_next, fwd_prev))
     last_a = to_next(fwd_next)
     last_b = to_prev(fwd_prev)
-    last_a, last_b = lax.optimization_barrier((last_a, last_b))
+    last_a, last_b, *extra = lax.optimization_barrier((last_a, last_b, *extra))
     a = total[6:7] + from_next[1:2] + last_a
     b = total[7:8] + from_prev[1:2] + last_b
-    return jnp.concatenate([a, b], 0)
+    return jnp.concatenate([a, b], 0), extra
 
 
 def on_device(estimate, measured, lateral_x, lateral_y, depth_taps):
@@ -299,36 +358,37 @@
     order = jnp.stack([2 * opp, 2 * nxt + 1, 2 * opp + 1, 2 * prv, 2 * nxt, 2 * prv + 1, 2 * chip, 2 * chip + 1])
     starts = jnp.concatenate([core * 64 + 8 * order, (1 - core) * 64 + 8 * order, core[None]]).astype(jnp.int32)
 
-    half = lax.dynamic_slice_in_dim(estimate, core * 64, 64, axis=1)
-    before = up(half[SLAB - FAR :])
-    after = down(half[:FAR])
-    tf, ta, x_all, x_halves, x_fwd, adj_x, fwd_y, adj_y, rec_own, rec_first, rec_last = prep(
+    before = up(lax.dynamic_slice(estimate, (SLAB - HALF, core * 64, 0), (HALF, 64, N)))
+    after = down(lax.dynamic_slice(estimate, (0, core * 64, 0), (HALF, 64, N)))
+    tf, ts, ta, x_all, x_halves, x_fwd, adj_x, fwd_y, adj_y, rec_own, rec_first, rec_last = prep(
         starts, depth_taps, mx, my, recorded
     )
-    before, after, rec_first, rec_last = lax.optimization_barrier((before, after, rec_first, rec_last))
-    rec_before = up(rec_last)
-    rec_after = down(rec_first)
+    (smooth_own,) = lateral([[estimate]], x_all, fwd_y)
+    before, after = lax.optimization_barrier((before, after))
     before2, after2 = to_core(before), to_core(after)
-
-    def middle_of(smooth):
-        return middle(smooth, (rec_before, rec_own, rec_after), tf, ta, adj_x, adj_y)
-
-    mine = jnp.stack(
-        [lax.dynamic_slice_in_dim(estimate, starts[6 + k], 8, axis=1) for k in range(2)], 0
-    )
-
-    (smooth_own,) = lateral([[estimate]], x_all, fwd_y)
     smooth_b, smooth_a = lateral([[before, before2], [after, after2]], x_halves, fwd_y)
-    own, other = middle_of((smooth_b, smooth_own, smooth_a))
-    mine = mine * jnp.exp(reduce_chunk(other, own) / 8.0)
+    ratio, ratio_first, ratio_last = ratio_of((smooth_b, smooth_own, smooth_a), rec_own, ts)
+    ratio_b = up(ratio_last)
+    ratio_a = down(ratio_first)
+    mine = jnp.stack([lax.dynamic_slice_in_dim(estimate, starts[6 + k], 8, axis=1) for k in range(2)], 0)
+    own, other = adjoint((ratio_b, ratio, ratio_a), ta, adj_x, adj_y)
+
+    def recorded_halo(total):
+        last, first, _ = lax.optimization_barrier((rec_last, rec_first, total))
+        return up(last), down(first)
+
+    log_sum, (rec_before, rec_after) = reduce_chunk(other, own, recorded_halo)
+    mine = mine * jnp.exp(log_sum / 8.0)
 
     prev_c, next_c = to_next(mine), to_prev(mine)
     b0, a0 = up(mine[:, SLAB - FAR :]), down(mine[:, :FAR])
+    prev_c, next_c, b0, a0 = lax.optimization_barrier((prev_c, next_c, b0, a0))
     opp_a, opp_b = to_next(prev_c[0:1]), to_prev(next_c[1:2])
     sides = jnp.concatenate([prev_c, next_c], 0)
     b1, a1 = up(sides[:, SLAB - FAR :]), down(sides[:, :FAR])
     near = jnp.concatenate([mine, sides], 0)
     near2 = to_core(near)
+    opp_a, opp_b, near2 = lax.optimization_barrier((opp_a, opp_b, near2))
     opp_c = jnp.concatenate([opp_a, opp_b], 0)
     b2, a2 = up(opp_c[:, SLAB - FAR :]), down(opp_c[:, :FAR])
     opp2 = to_core(opp_c)
@@ -350,9 +410,11 @@
         x_fwd,
         fwd_y,
     )
-    own, other = middle_of((smooth_b, smooth_own, smooth_a))
-    mine = mine * jnp.exp(reduce_chunk(other, own) / 8.0)
-    prev_c, next_c = to_next(mine), to_prev(mine)
+    smooth = (smooth_b, smooth_own, smooth_a)
+    own, other = middle(smooth, (rec_before, rec_own, rec_after), tf, ta, adj_x, adj_y)
+    log_sum, _ = reduce_chunk(other, own)
+    mine = mine * jnp.exp(log_sum / 8.0)
+    prev_c, next_c = lax.optimization_barrier((to_next(mine), to_prev(mine)))
     near = jnp.concatenate([mine, prev_c, next_c], 0)
     near2 = to_core(near)
     opp_c = jnp.concatenate([to_next(prev_c[0:1]), to_prev(next_c[1:2])], 0)

time: 266 us -> 308 us (1.16)
  the two profiles are of different devices: /device:TPU:15 before, /device:TPU:33 now
where the time goes in v3:
time: 308 us; the launch traced here: 306 us
  waiting for transfers between devices  156 us (51%)
  starting transfers between devices  105 us (34%)
  Pallas kernels  31.2 us (10%)
  local copies, waits for them, and re-layouts  5.67 us (2%)
  between operations  4.42 us (1%)
  other arithmetic  3.42 us (1%)
    ppermute x6, waiting for transfers between devices, up(): return lax.ppermute(x, 'gz', [(i, i + 1) for i in range(n - 1)])  59.7 us
    ppermute x8, waiting for transfers between devices, to_prev(): return lax.ppermute(x, 'view', [(i, (i - 2) % 8) for i in range(8)])  52.6 us
    ppermute x6, starting transfers between devices, down(): return lax.ppermute(x, 'gz', [(i + 1, i) for i in range(n - 1)])  46.6 us
    ppermute x8, waiting for transfers between devices, to_next(): return lax.ppermute(x, 'view', [(i, (i + 2) % 8) for i in range(8)])  33.9 us
    ppermute x8, starting transfers between devices, to_prev(): return lax.ppermute(x, 'view', [(i, (i - 2) % 8) for i in range(8)])  19.3 us
    pallas_call x3, Pallas kernels, kernel_call(): pl.pallas_call(kernel, out_shape=outs, in_specs=[pl.BlockSpec(memory_spac...  14.9 us
    ppermute x10, starting transfers between devices, to_core(): return lax.ppermute(x, 'view', [(i, i ^ 1) for i in range(8)])  14.8 us
    ppermute x6, starting transfers between devices, up(): return lax.ppermute(x, 'gz', [(i, i + 1) for i in range(n - 1)])  12.7 us
  transfers between devices with their start and end apart: 38, of which 22 were waited for; matrix products, arithmetic and copies ran while one was open for 1% of the time, Pallas kernels for 2%

profile of v3, /device:TPU:33, one launch (start us, length us, event | category | flops | bytes accessed | tf_op | source)
XLA Modules:
  0.0 306.4 jit_solution(6951311901734155313)
XLA Ops:
  1.4 3.1 %collective-permute-start = (f32[16,64,128]{2,1,0:T(8,128)S(1)}, f32[16,64,128]{2,1,0:T(8,128)}, u32[]{:S(2)}, u32[]{:S(2)}) collective-permute-start(f32[16,64,128]{2,1,0:T(8,128)S(1)} %get-tuple-element.106), channel_id=1, source_target_pairs={{0,1},{1,2},{2,3},{3,4},{4,5},{5,6},{6,7},{7,8},{8,9},{9,10},{10,1... | collective-permute-start | bytes 1572872 | tf_op jit(solution)/shard_map/ppermute | solution.py:324
  4.5 6.4 %collective-permute-start.1 = (f32[16,64,128]{2,1,0:T(8,128)S(1)}, f32[16,64,128]{2,1,0:T(8,128)}, u32[]{:S(2)}, u32[]{:S(2)}) collective-permute-start(f32[16,64,128]{2,1,0:T(8,128)S(1)} %get-tuple-element.105), channel_id=1, source_target_pairs={{1,0},{2,1},{3,2},{4,3},{5,4},{6,5},{7,6},{8,7},{9,8},{10,9},{11,1... | collective-permute-start | bytes 1572872 | tf_op jit(solution)/shard_map/ppermute | solution.py:329
  10.9 9.5 %collective-permute-done.refs_0_ = f32[16,64,128]{2,1,0:T(8,128)} collective-permute-done((f32[16,64,128]{2,1,0:T(8,128)S(1)}, f32[16,64,128]{2,1,0:T(8,128)}, u32[]{:S(2)}, u32[]{:S(2)}) %collective-permute-start) | collective-permute-done | bytes 524320 | tf_op jit(solution)/shard_map/ppermute | solution.py:324
  23.2 1.9 copy-done.1
  25.1 3.1 %prep.1 = (bf16[160,224]{1,0:T(8,128)(2,1)S(1)}, bf16[96,160]{1,0:T(8,128)(2,1)S(1)}, bf16[96,160]{1,0:T(8,128)(2,1)S(1)}, bf16[256,256]{1,0:T(8,128)(2,1)S(1)},...) custom-call(s32[17]{0:T(128)S(1)} %pad_add_fusion.starts, ...), custom_call_target="tpu_custom_call" | custom-call | tf_op jit(solution)/shard_map/prep/pallas_call | solution.py:278
  28.9 2.2 lateral.5.so
  31.2 3.0 lateral.4
  34.1 2.2 ratio.1
  36.3 1.9 collective-permute-start.4
  38.3 8.4 %collective-permute-start.5 = (f32[128,16,128]{2,1,0:T(8,128)S(1)}, f32[128,16,128]{2,1,0:T(8,128)S(1)}, u32[]{:S(2)}, u32[]{:S(2)}) collective-permute-start(f32[128,16,128]{2,1,0:T(8,128)S(1)} %get-tuple-element.66), channel_id=1, source_target_pairs={{1,0},{2,1},{3,2},{4,3},{5,4},{6,5},{7,6},{8,7},{9,8},{10,9},{11,1... | collective-permute-start | bytes 3145736 | tf_op jit(solution)/shard_map/ppermute | solution.py:329
  46.7 21.1 %collective-permute-done.4.rb = f32[128,16,128]{2,1,0:T(8,128)S(1)} collective-permute-done((f32[128,16,128]{2,1,0:T(8,128)S(1)}, f32[128,16,128]{2,1,0:T(8,128)S(1)}, u32[]{:S(2)}, u32[]{:S(2)}) %collective-permute-start.4) | collective-permute-done | bytes 1048608 | tf_op jit(solution)/shard_map/ppermute | solution.py:324
  68.7 4.4 %adjoint.1 = (f32[8,48,8,128]{3,2,1,0:T(8,128)S(1)}, f32[8,48,8,128]{3,2,1,0:T(8,128)S(1)}) custom-call(f32[128,16,128]{2,1,0:T(8,128)S(1)} %collective-permute-done.4.rb, f32[128,48,128]{2,1,0:T(8,128)S(1)} %get-tuple-element.65.ro, f32[128,16,128]{2,1,0:T(8,128)S(1)} %collective-permute-done.5.ra, bf16[96,160]{1,0:T(8,128)(2,1)S(1)} %get-tuple-element.67.ta_ref, ...), custom_call_target="tpu_custom_call" | custom-call | flops 5000000000 | bytes 15728640 | tf_op jit(solution)/shard_map/adjoint/pallas_call | solution.py:171
  74.6 3.0 collective-permute-done.6
  77.9 1.9 collective-permute-start.11
  79.8 8.3 %collective-permute-start.12 = (f32[128,16,128]{2,1,0:T(8,128)}, f32[128,16,128]{2,1,0:T(8,128)}, u32[]{:S(2)}, u32[]{:S(2)}) collective-permute-start(f32[128,16,128]{2,1,0:T(8,128)} %get-tuple-element.79), channel_id=1, source_target_pairs={{1,0},{2,1},{3,2},{4,3},{5,4},{6,5},{7,6},{8,7},{9,8},{10,9},{11,1... | collective-permute-start | bytes 3145736 | tf_op jit(solution)/shard_map/ppermute | solution.py:329
  88.2 3.1 %collective-permute-start.7 = (f32[2,48,8,128]{3,2,1,0:T(8,128)S(1)}, f32[2,48,8,128]{3,2,1,0:T(8,128)S(1)}, u32[]{:S(2)}, u32[]{:S(2)}) collective-permute-start(f32[2,48,8,128]{3,2,1,0:T(8,128)S(1)} %get-tuple-element.130), channel_id=1, source_target_pairs={{0,64},{32,96},{64,128},{96,160},{128,192},{160,224},{192,0},{224,... | collective-permute-start | bytes 1179656 | tf_op jit(solution)/shard_map/ppermute | solution.py:315
  91.3 2.2 collective-permute-start.8
  93.5 9.6 %collective-permute-done.7 = f32[2,48,8,128]{3,2,1,0:T(8,128)S(1)} collective-permute-done((f32[2,48,8,128]{3,2,1,0:T(8,128)S(1)}, f32[2,48,8,128]{3,2,1,0:T(8,128)S(1)}, u32[]{:S(2)}, u32[]{:S(2)}) %collective-permute-start.7) | collective-permute-done | bytes 393248 | tf_op jit(solution)/shard_map/ppermute | solution.py:315
  103.1 38.9 %collective-permute-done.8 = f32[2,48,8,128]{3,2,1,0:T(8,128)S(1)} collective-permute-done((f32[2,48,8,128]{3,2,1,0:T(8,128)S(1)}, f32[2,48,8,128]{3,2,1,0:T(8,128)S(1)}, u32[]{:S(2)}, u32[]{:S(2)}) %collective-permute-start.8) | collective-permute-done | bytes 393248 | tf_op jit(solution)/shard_map/ppermute | solution.py:319
  142.9 3.6 %collective-permute-start.10 = (f32[1,48,8,128]{3,2,1,0:T(8,128)}, f32[1,48,8,128]{3,2,1,0:T(8,128)}, u32[]{:S(2)}, u32[]{:S(2)}) collective-permute-start(f32[1,48,8,128]{3,2,1,0:T(8,128)} %get-tuple-element.75), channel_id=1, source_target_pairs={{0,192},{32,224},{64,0},{96,32},{128,64},{160,96},{192,128},{224,1... | collective-permute-start | bytes 589832 | tf_op jit(solution)/shard_map/ppermute | solution.py:319
  151.0 4.6 %collective-permute-done.9 = f32[1,48,8,128]{3,2,1,0:T(8,128)} collective-permute-done((f32[1,48,8,128]{3,2,1,0:T(8,128)}, f32[1,48,8,128]{3,2,1,0:T(8,128)}, u32[]{:S(2)}, u32[]{:S(2)}) %collective-permute-start.9) | collective-permute-done | bytes 196640 | tf_op jit(solution)/shard_map/ppermute | solution.py:315
  157.1 3.6 %collective-permute-start.14 = (f32[2,48,8,128]{3,2,1,0:T(8,128)S(1)}, f32[2,48,8,128]{3,2,1,0:T(8,128)S(1)}, u32[]{:S(2)}, u32[]{:S(2)}) collective-permute-start(f32[2,48,8,128]{3,2,1,0:T(8,128)S(1)} %maximum_multiply_fusion.refs_6_), channel_id=1, source_target_pairs={{0,192},{32,224},{64,0},{96,32},{128,64},{160,96},{192,128},{224,1... | collective-permute-start | bytes 1179656 | tf_op jit(solution)/shard_map/ppermute | solution.py:319
  160.7 1.9 collective-permute-start.15
  162.7 7.6 %collective-permute-start.16 = (f32[2,32,8,128]{3,2,1,0:T(8,128)S(1)}, f32[2,32,8,128]{3,2,1,0:T(8,128)S(1)}, u32[]{:S(2)}, u32[]{:S(2)}) collective-permute-start(f32[2,32,8,128]{3,2,1,0:T(8,128)S(1)} %get-tuple-element.167), channel_id=1, source_target_pairs={{1,0},{2,1},{3,2},{4,3},{5,4},{6,5},{7,6},{8,7},{9,8},{10,9},{11,1... | collective-permute-start | bytes 786440 | tf_op jit(solution)/shard_map/ppermute | solution.py:329
  170.3 2.5 collective-permute-done.15.refs_6_
  173.7 3.5 %collective-permute-start.19 = (f32[6,48,8,128]{3,2,1,0:T(8,128)S(1)}, f32[6,48,8,128]{3,2,1,0:T(8,128)S(1)}, u32[]{:S(2)}, u32[]{:S(2)}) collective-permute-start(f32[6,48,8,128]{3,2,1,0:T(8,128)S(1)} %pad_maximum_fusion.1), channel_id=1, source_target_pairs={{0,32},{32,0},{64,96},{96,64},{128,160},{160,128},{192,224},{224,1... | collective-permute-start | bytes 3538952 | tf_op jit(solution)/shard_map/ppermute | solution.py:311
  177.3 1.9 collective-permute-start.21
  179.2 8.3 %collective-permute-start.24 = (f32[4,32,8,128]{3,2,1,0:T(8,128)S(1)}, f32[4,32,8,128]{3,2,1,0:T(8,128)S(1)}, u32[]{:S(2)}, u32[]{:S(2)}) collective-permute-start(f32[4,32,8,128]{3,2,1,0:T(8,128)S(1)} %get-tuple-element.139), channel_id=1, source_target_pairs={{1,0},{2,1},{3,2},{4,3},{5,4},{6,5},{7,6},{8,7},{9,8},{10,9},{11,1... | collective-permute-start | bytes 1572872 | tf_op jit(solution)/shard_map/ppermute | solution.py:329
  187.7 3.6 %collective-permute-start.18 = (f32[1,48,8,128]{3,2,1,0:T(8,128)S(1)}, f32[1,48,8,128]{3,2,1,0:T(8,128)S(1)}, u32[]{:S(2)}, u32[]{:S(2)}) collective-permute-start(f32[1,48,8,128]{3,2,1,0:T(8,128)S(1)} %get-tuple-element.164.refs_1_), channel_id=1, source_target_pairs={{0,192},{32,224},{64,0},{96,32},{128,64},{160,96},{192,128},{224,1... | collective-permute-start | bytes 589832 | tf_op jit(solution)/shard_map/ppermute | solution.py:319
  191.3 17.1 %collective-permute-done.21 = f32[4,32,8,128]{3,2,1,0:T(8,128)S(1)} collective-permute-done((f32[4,32,8,128]{3,2,1,0:T(8,128)S(1)}, f32[4,32,8,128]{3,2,1,0:T(8,128)S(1)}, u32[]{:S(2)}, u32[]{:S(2)}) %collective-permute-start.21) | collective-permute-done | bytes 524320 | tf_op jit(solution)/shard_map/ppermute | solution.py:324
  209.4 6.3 %collective-permute-done.18.refs_2_ = f32[1,48,8,128]{3,2,1,0:T(8,128)S(1)} collective-permute-done((f32[1,48,8,128]{3,2,1,0:T(8,128)S(1)}, f32[1,48,8,128]{3,2,1,0:T(8,128)S(1)}, u32[]{:S(2)}, u32[]{:S(2)}) %collective-permute-start.18) | collective-permute-done | bytes 196640 | tf_op jit(solution)/shard_map/ppermute | solution.py:319
  215.8 1.9 collective-permute-start.20
  217.7 7.6 %collective-permute-start.22 = (f32[2,32,8,128]{3,2,1,0:T(8,128)S(1)}, f32[2,32,8,128]{3,2,1,0:T(8,128)S(1)}, u32[]{:S(2)}, u32[]{:S(2)}) collective-permute-start(f32[2,32,8,128]{3,2,1,0:T(8,128)S(1)} %get-tuple-element.165), channel_id=1, source_target_pairs={{1,0},{2,1},{3,2},{4,3},{5,4},{6,5},{7,6},{8,7},{9,8},{10,9},{11,1... | collective-permute-start | bytes 786440 | tf_op jit(solution)/shard_map/ppermute | solution.py:329
  226.9 9.5 %collective-permute-done.20 = f32[2,32,8,128]{3,2,1,0:T(8,128)S(1)} collective-permute-done((f32[2,32,8,128]{3,2,1,0:T(8,128)S(1)}, f32[2,32,8,128]{3,2,1,0:T(8,128)S(1)}, u32[]{:S(2)}, u32[]{:S(2)}) %collective-permute-start.20) | collective-permute-done | bytes 262176 | tf_op jit(solution)/shard_map/ppermute | solution.py:324
  237.2 2.3 lateral.7.so
  239.7 3.1 lateral.6
  242.8 8.3 %middle.1 = (f32[8,48,8,128]{3,2,1,0:T(8,128)S(1)}, f32[8,48,8,128]{3,2,1,0:T(8,128)S(1)}) custom-call(f32[4224,128]{1,0:T(8,128)S(1)} %get-tuple-element.89.sb, f32[6336,128]{1,0:T(8,128)S(1)} %lateral.7.so, f32[4224,128]{1,0:T(8,128)S(1)} %get-tuple-element.91.sa, f32[128,16,128]{2,1,0:T(8,128)} %collective-permute-done.11.mb, ...), custom_call_target="tpu_custom_call" | custom-call | flops 8000000000 | bytes 15728640 | tf_op jit(solution)/shard_map/middle/pallas_call | solution.py:171
  251.2 3.4 %collective-permute-done.27 = f32[8,48,8,128]{3,2,1,0:T(8,128)S(1)} collective-permute-done((f32[8,48,8,128]{3,2,1,0:T(8,128)S(1)}, f32[8,48,8,128]{3,2,1,0:T(8,128)S(1)}, u32[]{:S(2)}, u32[]{:S(2)}) %collective-permute-start.27) | collective-permute-done | bytes 1572896 | tf_op jit(solution)/shard_map/ppermute | solution.py:311
  254.8 2.1 collective-permute-start.28
  258.5 9.1 %collective-permute-done.28 = f32[2,48,8,128]{3,2,1,0:T(8,128)S(1)} collective-permute-done((f32[2,48,8,128]{3,2,1,0:T(8,128)S(1)}, f32[2,48,8,128]{3,2,1,0:T(8,128)S(1)}, u32[]{:S(2)}, u32[]{:S(2)}) %collective-permute-start.28) | collective-permute-done | bytes 393248 | tf_op jit(solution)/shard_map/ppermute | solution.py:315
  269.8 2.0 collective-permute-start.31
  271.8 3.7 %collective-permute-done.30 = f32[1,48,8,128]{3,2,1,0:T(8,128)S(1)} collective-permute-done((f32[1,48,8,128]{3,2,1,0:T(8,128)S(1)}, f32[1,48,8,128]{3,2,1,0:T(8,128)S(1)}, u32[]{:S(2)}, u32[]{:S(2)}) %collective-permute-start.30) | collective-permute-done | bytes 196640 | tf_op jit(solution)/shard_map/ppermute | solution.py:315
  276.1 3.2 %collective-permute-start.32 = (f32[2,48,8,128]{3,2,1,0:T(8,128)S(1)}, f32[2,48,8,128]{3,2,1,0:T(8,128)S(1)}, u32[]{:S(2)}, u32[]{:S(2)}) collective-permute-start(f32[2,48,8,128]{3,2,1,0:T(8,128)S(1)} %fusion.2.refs_6_), channel_id=1, source_target_pairs={{0,64},{32,96},{64,128},{96,160},{128,192},{160,224},{192,0},{224,... | collective-permute-start | bytes 1179656 | tf_op jit(solution)/shard_map/ppermute | solution.py:315
  279.9 7.0 %collective-permute-done.32 = f32[2,48,8,128]{3,2,1,0:T(8,128)S(1)} collective-permute-done((f32[2,48,8,128]{3,2,1,0:T(8,128)S(1)}, f32[2,48,8,128]{3,2,1,0:T(8,128)S(1)}, u32[]{:S(2)}, u32[]{:S(2)}) %collective-permute-start.32) | collective-permute-done | bytes 393248 | tf_op jit(solution)/shard_map/ppermute | solution.py:315
  289.8 4.0 %collective-permute-start.37 = (f32[6,48,8,128]{3,2,1,0:T(8,128)S(1)}, f32[6,48,8,128]{3,2,1,0:T(8,128)S(1)}, u32[]{:S(2)}, u32[]{:S(2)}) collective-permute-start(f32[6,48,8,128]{3,2,1,0:T(8,128)S(1)} %pad_maximum_fusion.2), channel_id=1, source_target_pairs={{0,32},{32,0},{64,96},{96,64},{128,160},{160,128},{192,224},{224,1... | collective-permute-start | bytes 3538952 | tf_op jit(solution)/shard_map/ppermute | solution.py:311
  293.8 2.2 collective-permute-start.35
  296.0 5.3 %collective-permute-done.35.refs_2_ = f32[1,48,8,128]{3,2,1,0:T(8,128)S(1)} collective-permute-done((f32[1,48,8,128]{3,2,1,0:T(8,128)S(1)}, f32[1,48,8,128]{3,2,1,0:T(8,128)S(1)}, u32[]{:S(2)}, u32[]{:S(2)}) %collective-permute-start.35) | collective-permute-done | bytes 196640 | tf_op jit(solution)/shard_map/ppermute | solution.py:319
  303.7 2.6 place.1
  (118 shorter events, 26.0 us)
Async XLA Ops:
  0.0 23.2 %copy-start.4 = (f32[1,33]{1,0:T(1,128)S(1)}, f32[1,33]{1,0:T(1,128)}, u32[]{:S(2)}) copy-start(f32[1,33]{1,0:T(1,128)} %taps.1) | copy-start | bytes 400
  0.0 23.2 %copy-start.2 = (f32[1,128,128]{2,1,0:T(8,128)S(1)}, f32[1,128,128]{2,1,0:T(8,128)}, u32[]{:S(2)}) copy-start(f32[1,128,128]{2,1,0:T(8,128)} %param.7) | copy-start | bytes 196612
  0.0 23.2 %copy-start.3 = (f32[1,128,128]{2,1,0:T(8,128)S(1)}, f32[1,128,128]{2,1,0:T(8,128)}, u32[]{:S(2)}) copy-start(f32[1,128,128]{2,1,0:T(8,128)} %param.8) | copy-start | bytes 196612
  1.4 19.0 %collective-permute-start = (f32[16,64,128]{2,1,0:T(8,128)S(1)}, f32[16,64,128]{2,1,0:T(8,128)}, u32[]{:S(2)}, u32[]{:S(2)}) collective-permute-start(f32[16,64,128]{2,1,0:T(8,128)S(1)} %get-tuple-element.106), channel_id=1, source_target_pairs={{0,1},{1,2},{2,3},{3,4},{4,5},{5,6},{6,7},{7,8},{8,9},{9,10},{10,1... | collective-permute-start | bytes 1572872 | tf_op jit(solution)/shard_map/ppermute | solution.py:324
  4.5 16.6 %collective-permute-start.1 = (f32[16,64,128]{2,1,0:T(8,128)S(1)}, f32[16,64,128]{2,1,0:T(8,128)}, u32[]{:S(2)}, u32[]{:S(2)}) collective-permute-start(f32[16,64,128]{2,1,0:T(8,128)S(1)} %get-tuple-element.105), channel_id=1, source_target_pairs={{1,0},{2,1},{3,2},{4,3},{5,4},{6,5},{7,6},{8,7},{9,8},{10,9},{11,1... | collective-permute-start | bytes 1572872 | tf_op jit(solution)/shard_map/ppermute | solution.py:329
  21.2 10.0 %collective-permute-start.2 = (f32[16,64,128]{2,1,0:T(8,128)}, f32[16,64,128]{2,1,0:T(8,128)}, u32[]{:S(2)}, u32[]{:S(2)}) collective-permute-start(f32[16,64,128]{2,1,0:T(8,128)} %collective-permute-done.refs_0_), channel_id=1, source_target_pairs={{0,32},{32,0},{64,96},{96,64},{128,160},{160,128},{192,224},{224,1... | collective-permute-start | bytes 1572872 | tf_op jit(solution)/shard_map/ppermute | solution.py:311
  23.0 8.1 %collective-permute-start.3 = (f32[16,64,128]{2,1,0:T(8,128)}, f32[16,64,128]{2,1,0:T(8,128)}, u32[]{:S(2)}, u32[]{:S(2)}) collective-permute-start(f32[16,64,128]{2,1,0:T(8,128)} %collective-permute-done.1.refs_2_), channel_id=1, source_target_pairs={{0,32},{32,0},{64,96},{96,64},{128,160},{160,128},{192,224},{224,1... | collective-permute-start | bytes 1572872 | tf_op jit(solution)/shard_map/ppermute | solution.py:311
  25.1 3.8 %copy-start = (f32[48,128,128]{2,1,0:T(8,128)S(1)}, f32[48,128,128]{2,1,0:T(8,128)}, u32[]{:S(2)}) copy-start(f32[48,128,128]{2,1,0:T(8,128)} %refs_0_.1) | copy-start | bytes 9437188
  28.9 5.3 %copy-start.5 = (f32[128,48,128]{2,1,0:T(8,128)}, f32[128,48,128]{2,1,0:T(8,128)S(1)}, u32[]{:S(2)}) copy-start(f32[128,48,128]{2,1,0:T(8,128)S(1)} %get-tuple-element.62.rec.mo) | copy-start | bytes 9437188
  28.9 39.8 %copy-start.7 = (bf16[256,256]{1,0:T(8,128)(2,1)}, bf16[256,256]{1,0:T(8,128)(2,1)S(1)}, u32[]{:S(2)}) copy-start(bf16[256,256]{1,0:T(8,128)(2,1)S(1)} %get-tuple-element.68.left_ref) | copy-start | bytes 393220
  28.9 39.8 %copy-start.9 = (bf16[256,256]{1,0:T(8,128)(2,1)}, bf16[256,256]{1,0:T(8,128)(2,1)S(1)}, u32[]{:S(2)}) copy-start(bf16[256,256]{1,0:T(8,128)(2,1)S(1)} %get-tuple-element.69.right_ref) | copy-start | bytes 393220
  28.9 39.8 %copy-start.13 = (bf16[96,160]{1,0:T(8,128)(2,1)}, bf16[96,160]{1,0:T(8,128)(2,1)S(1)}, u32[]{:S(2)}) copy-start(bf16[96,160]{1,0:T(8,128)(2,1)S(1)} %get-tuple-element.67.ta_ref) | copy-start | bytes 92164
  36.3 31.5 %collective-permute-start.4 = (f32[128,16,128]{2,1,0:T(8,128)S(1)}, f32[128,16,128]{2,1,0:T(8,128)S(1)}, u32[]{:S(2)}, u32[]{:S(2)}) collective-permute-start(f32[128,16,128]{2,1,0:T(8,128)S(1)} %get-tuple-element.64), channel_id=1, source_target_pairs={{0,1},{1,2},{2,3},{3,4},{4,5},{5,6},{6,7},{7,8},{8,9},{9,10},{10,1... | collective-permute-start | bytes 3145736 | tf_op jit(solution)/shard_map/ppermute | solution.py:324
  38.3 30.4 %collective-permute-start.5 = (f32[128,16,128]{2,1,0:T(8,128)S(1)}, f32[128,16,128]{2,1,0:T(8,128)S(1)}, u32[]{:S(2)}, u32[]{:S(2)}) collective-permute-start(f32[128,16,128]{2,1,0:T(8,128)S(1)} %get-tuple-element.66), channel_id=1, source_target_pairs={{1,0},{2,1},{3,2},{4,3},{5,4},{6,5},{7,6},{8,7},{9,8},{10,9},{11,1... | collective-permute-start | bytes 3145736 | tf_op jit(solution)/shard_map/ppermute | solution.py:329
  73.2 4.5 %collective-permute-start.6 = (f32[8,48,8,128]{3,2,1,0:T(8,128)S(1)}, f32[8,48,8,128]{3,2,1,0:T(8,128)S(1)}, u32[]{:S(2)}, u32[]{:S(2)}) collective-permute-start(f32[8,48,8,128]{3,2,1,0:T(8,128)S(1)} %get-tuple-element.71), channel_id=1, source_target_pairs={{0,32},{32,0},{64,96},{96,64},{128,160},{160,128},{192,224},{224,1... | collective-permute-start | bytes 4718600 | tf_op jit(solution)/shard_map/ppermute | solution.py:311
  77.9 64.1 %copy-start.15 = (f32[8,48,8,128]{3,2,1,0:T(8,128)}, f32[8,48,8,128]{3,2,1,0:T(8,128)S(1)}, u32[]{:S(2)}) copy-start(f32[8,48,8,128]{3,2,1,0:T(8,128)S(1)} %add.112) | copy-start | bytes 4718596
  77.9 77.7 %collective-permute-start.11 = (f32[128,16,128]{2,1,0:T(8,128)}, f32[128,16,128]{2,1,0:T(8,128)}, u32[]{:S(2)}, u32[]{:S(2)}) collective-permute-start(f32[128,16,128]{2,1,0:T(8,128)} %get-tuple-element.78), channel_id=1, source_target_pairs={{0,1},{1,2},{2,3},{3,4},{4,5},{5,6},{6,7},{7,8},{8,9},{9,10},{10,1... | collective-permute-start | bytes 3145736 | tf_op jit(solution)/shard_map/ppermute | solution.py:324
  79.8 75.8 %collective-permute-start.12 = (f32[128,16,128]{2,1,0:T(8,128)}, f32[128,16,128]{2,1,0:T(8,128)}, u32[]{:S(2)}, u32[]{:S(2)}) collective-permute-start(f32[128,16,128]{2,1,0:T(8,128)} %get-tuple-element.79), channel_id=1, source_target_pairs={{1,0},{2,1},{3,2},{4,3},{5,4},{6,5},{7,6},{8,7},{9,8},{10,9},{11,1... | collective-permute-start | bytes 3145736 | tf_op jit(solution)/shard_map/ppermute | solution.py:329
  88.2 14.9 %collective-permute-start.7 = (f32[2,48,8,128]{3,2,1,0:T(8,128)S(1)}, f32[2,48,8,128]{3,2,1,0:T(8,128)S(1)}, u32[]{:S(2)}, u32[]{:S(2)}) collective-permute-start(f32[2,48,8,128]{3,2,1,0:T(8,128)S(1)} %get-tuple-element.130), channel_id=1, source_target_pairs={{0,64},{32,96},{64,128},{96,160},{128,192},{160,224},{192,0},{224,... | collective-permute-start | bytes 1179656 | tf_op jit(solution)/shard_map/ppermute | solution.py:315
  91.3 50.7 %collective-permute-start.8 = (f32[2,48,8,128]{3,2,1,0:T(8,128)S(1)}, f32[2,48,8,128]{3,2,1,0:T(8,128)S(1)}, u32[]{:S(2)}, u32[]{:S(2)}) collective-permute-start(f32[2,48,8,128]{3,2,1,0:T(8,128)S(1)} %get-tuple-element.129), channel_id=1, source_target_pairs={{0,192},{32,224},{64,0},{96,32},{128,64},{160,96},{192,128},{224,1... | collective-permute-start | bytes 1179656 | tf_op jit(solution)/shard_map/ppermute | solution.py:319
  103.1 39.8 %copy-start.16 = (f32[2,48,8,128]{3,2,1,0:T(8,128)}, f32[2,48,8,128]{3,2,1,0:T(8,128)S(1)}, u32[]{:S(2)}) copy-start(f32[2,48,8,128]{3,2,1,0:T(8,128)S(1)} %collective-permute-done.7) | copy-start | bytes 1179652
  142.9 12.7 %collective-permute-start.9 = (f32[1,48,8,128]{3,2,1,0:T(8,128)}, f32[1,48,8,128]{3,2,1,0:T(8,128)}, u32[]{:S(2)}, u32[]{:S(2)}) collective-permute-start(f32[1,48,8,128]{3,2,1,0:T(8,128)} %get-tuple-element.74), channel_id=1, source_target_pairs={{0,64},{32,96},{64,128},{96,160},{128,192},{160,224},{192,0},{224,... | collective-permute-start | bytes 589832 | tf_op jit(solution)/shard_map/ppermute | solution.py:315
  142.9 12.7 %collective-permute-start.10 = (f32[1,48,8,128]{3,2,1,0:T(8,128)}, f32[1,48,8,128]{3,2,1,0:T(8,128)}, u32[]{:S(2)}, u32[]{:S(2)}) collective-permute-start(f32[1,48,8,128]{3,2,1,0:T(8,128)} %get-tuple-element.75), channel_id=1, source_target_pairs={{0,192},{32,224},{64,0},{96,32},{128,64},{160,96},{192,128},{224,1... | collective-permute-start | bytes 589832 | tf_op jit(solution)/shard_map/ppermute | solution.py:319
  157.0 16.5 %collective-permute-start.13 = (f32[2,48,8,128]{3,2,1,0:T(8,128)S(1)}, f32[2,48,8,128]{3,2,1,0:T(8,128)S(1)}, u32[]{:S(2)}, u32[]{:S(2)}) collective-permute-start(f32[2,48,8,128]{3,2,1,0:T(8,128)S(1)} %maximum_multiply_fusion.refs_6_), channel_id=1, source_target_pairs={{0,64},{32,96},{64,128},{96,160},{128,192},{160,224},{192,0},{224,... | collective-permute-start | bytes 1179656 | tf_op jit(solution)/shard_map/ppermute | solution.py:315
  157.1 16.4 %collective-permute-start.14 = (f32[2,48,8,128]{3,2,1,0:T(8,128)S(1)}, f32[2,48,8,128]{3,2,1,0:T(8,128)S(1)}, u32[]{:S(2)}, u32[]{:S(2)}) collective-permute-start(f32[2,48,8,128]{3,2,1,0:T(8,128)S(1)} %maximum_multiply_fusion.refs_6_), channel_id=1, source_target_pairs={{0,192},{32,224},{64,0},{96,32},{128,64},{160,96},{192,128},{224,1... | collective-permute-start | bytes 1179656 | tf_op jit(solution)/shard_map/ppermute | solution.py:319
  160.7 12.0 %collective-permute-start.15 = (f32[2,32,8,128]{3,2,1,0:T(8,128)S(1)}, f32[2,32,8,128]{3,2,1,0:T(8,128)S(1)}, u32[]{:S(2)}, u32[]{:S(2)}) collective-permute-start(f32[2,32,8,128]{3,2,1,0:T(8,128)S(1)} %get-tuple-element.168), channel_id=1, source_target_pairs={{0,1},{1,2},{2,3},{3,4},{4,5},{5,6},{6,7},{7,8},{8,9},{9,10},{10,1... | collective-permute-start | bytes 786440 | tf_op jit(solution)/shard_map/ppermute | solution.py:324
  162.7 10.9 %collective-permute-start.16 = (f32[2,32,8,128]{3,2,1,0:T(8,128)S(1)}, f32[2,32,8,128]{3,2,1,0:T(8,128)S(1)}, u32[]{:S(2)}, u32[]{:S(2)}) collective-permute-start(f32[2,32,8,128]{3,2,1,0:T(8,128)S(1)} %get-tuple-element.167), channel_id=1, source_target_pairs={{1,0},{2,1},{3,2},{4,3},{5,4},{6,5},{7,6},{8,7},{9,8},{10,9},{11,1... | collective-permute-start | bytes 786440 | tf_op jit(solution)/shard_map/ppermute | solution.py:329
  173.7 42.0 %collective-permute-start.19 = (f32[6,48,8,128]{3,2,1,0:T(8,128)S(1)}, f32[6,48,8,128]{3,2,1,0:T(8,128)S(1)}, u32[]{:S(2)}, u32[]{:S(2)}) collective-permute-start(f32[6,48,8,128]{3,2,1,0:T(8,128)S(1)} %pad_maximum_fusion.1), channel_id=1, source_target_pairs={{0,32},{32,0},{64,96},{96,64},{128,160},{160,128},{192,224},{224,1... | collective-permute-start | bytes 3538952 | tf_op jit(solution)/shard_map/ppermute | solution.py:311
  177.3 31.1 %collective-permute-start.21 = (f32[4,32,8,128]{3,2,1,0:T(8,128)S(1)}, f32[4,32,8,128]{3,2,1,0:T(8,128)S(1)}, u32[]{:S(2)}, u32[]{:S(2)}) collective-permute-start(f32[4,32,8,128]{3,2,1,0:T(8,128)S(1)} %get-tuple-element.140), channel_id=1, source_target_pairs={{0,1},{1,2},{2,3},{3,4},{4,5},{5,6},{6,7},{7,8},{8,9},{9,10},{10,1... | collective-permute-start | bytes 1572872 | tf_op jit(solution)/shard_map/ppermute | solution.py:324
  179.2 29.2 %collective-permute-start.24 = (f32[4,32,8,128]{3,2,1,0:T(8,128)S(1)}, f32[4,32,8,128]{3,2,1,0:T(8,128)S(1)}, u32[]{:S(2)}, u32[]{:S(2)}) collective-permute-start(f32[4,32,8,128]{3,2,1,0:T(8,128)S(1)} %get-tuple-element.139), channel_id=1, source_target_pairs={{1,0},{2,1},{3,2},{4,3},{5,4},{6,5},{7,6},{8,7},{9,8},{10,9},{11,1... | collective-permute-start | bytes 1572872 | tf_op jit(solution)/shard_map/ppermute | solution.py:329
  187.6 21.9 %collective-permute-start.17 = (f32[1,48,8,128]{3,2,1,0:T(8,128)S(1)}, f32[1,48,8,128]{3,2,1,0:T(8,128)S(1)}, u32[]{:S(2)}, u32[]{:S(2)}) collective-permute-start(f32[1,48,8,128]{3,2,1,0:T(8,128)S(1)} %get-tuple-element.162.refs_3_), channel_id=1, source_target_pairs={{0,64},{32,96},{64,128},{96,160},{128,192},{160,224},{192,0},{224,... | collective-permute-start | bytes 589832 | tf_op jit(solution)/shard_map/ppermute | solution.py:315
  187.7 28.0 %collective-permute-start.18 = (f32[1,48,8,128]{3,2,1,0:T(8,128)S(1)}, f32[1,48,8,128]{3,2,1,0:T(8,128)S(1)}, u32[]{:S(2)}, u32[]{:S(2)}) collective-permute-start(f32[1,48,8,128]{3,2,1,0:T(8,128)S(1)} %get-tuple-element.164.refs_1_), channel_id=1, source_target_pairs={{0,192},{32,224},{64,0},{96,32},{128,64},{160,96},{192,128},{224,1... | collective-permute-start | bytes 589832 | tf_op jit(solution)/shard_map/ppermute | solution.py:319
  208.5 31.0 %collective-permute-start.25 = (f32[12,32,8,128]{3,2,1,0:T(8,128)S(1)}, f32[12,32,8,128]{3,2,1,0:T(8,128)S(1)}, u32[]{:S(2)}, u32[]{:S(2)}) collective-permute-start(f32[12,32,8,128]{3,2,1,0:T(8,128)S(1)} %pad_maximum_fusion), channel_id=1, source_target_pairs={{0,32},{32,0},{64,96},{96,64},{128,160},{160,128},{192,224},{224,1... | collective-permute-start | bytes 4718600 | tf_op jit(solution)/shard_map/ppermute | solution.py:311
  215.8 20.6 %collective-permute-start.20 = (f32[2,32,8,128]{3,2,1,0:T(8,128)S(1)}, f32[2,32,8,128]{3,2,1,0:T(8,128)S(1)}, u32[]{:S(2)}, u32[]{:S(2)}) collective-permute-start(f32[2,32,8,128]{3,2,1,0:T(8,128)S(1)} %get-tuple-element.166), channel_id=1, source_target_pairs={{0,1},{1,2},{2,3},{3,4},{4,5},{5,6},{6,7},{7,8},{8,9},{9,10},{10,1... | collective-permute-start | bytes 786440 | tf_op jit(solution)/shard_map/ppermute | solution.py:324
  217.7 18.7 %collective-permute-start.22 = (f32[2,32,8,128]{3,2,1,0:T(8,128)S(1)}, f32[2,32,8,128]{3,2,1,0:T(8,128)S(1)}, u32[]{:S(2)}, u32[]{:S(2)}) collective-permute-start(f32[2,32,8,128]{3,2,1,0:T(8,128)S(1)} %get-tuple-element.165), channel_id=1, source_target_pairs={{1,0},{2,1},{3,2},{4,3},{5,4},{6,5},{7,6},{8,7},{9,8},{10,9},{11,1... | collective-permute-start | bytes 786440 | tf_op jit(solution)/shard_map/ppermute | solution.py:329
  225.4 11.8 %collective-permute-start.26 = (f32[2,48,8,128]{3,2,1,0:T(8,128)S(1)}, f32[2,48,8,128]{3,2,1,0:T(8,128)S(1)}, u32[]{:S(2)}, u32[]{:S(2)}) collective-permute-start(f32[2,48,8,128]{3,2,1,0:T(8,128)S(1)} %constant_dynamic-update-slice_fusion), channel_id=1, source_target_pairs={{0,32},{32,0},{64,96},{96,64},{128,160},{160,128},{192,224},{224,1... | collective-permute-start | bytes 1179656 | tf_op jit(solution)/shard_map/ppermute | solution.py:311
  236.4 3.0 collective-permute-start.23
  251.1 3.5 %collective-permute-start.27 = (f32[8,48,8,128]{3,2,1,0:T(8,128)S(1)}, f32[8,48,8,128]{3,2,1,0:T(8,128)S(1)}, u32[]{:S(2)}, u32[]{:S(2)}) collective-permute-start(f32[8,48,8,128]{3,2,1,0:T(8,128)S(1)} %get-tuple-element.96), channel_id=1, source_target_pairs={{0,32},{32,0},{64,96},{96,64},{128,160},{160,128},{192,224},{224,1... | collective-permute-start | bytes 4718600 | tf_op jit(solution)/shard_map/ppermute | solution.py:311
  254.8 12.8 %collective-permute-start.28 = (f32[2,48,8,128]{3,2,1,0:T(8,128)S(1)}, f32[2,48,8,128]{3,2,1,0:T(8,128)S(1)}, u32[]{:S(2)}, u32[]{:S(2)}) collective-permute-start(f32[2,48,8,128]{3,2,1,0:T(8,128)S(1)} %get-tuple-element.114), channel_id=1, source_target_pairs={{0,64},{32,96},{64,128},{96,160},{128,192},{160,224},{192,0},{224,... | collective-permute-start | bytes 1179656 | tf_op jit(solution)/shard_map/ppermute | solution.py:315
  256.9 11.2 %collective-permute-start.29 = (f32[2,48,8,128]{3,2,1,0:T(8,128)S(1)}, f32[2,48,8,128]{3,2,1,0:T(8,128)S(1)}, u32[]{:S(2)}, u32[]{:S(2)}) collective-permute-start(f32[2,48,8,128]{3,2,1,0:T(8,128)S(1)} %get-tuple-element.113), channel_id=1, source_target_pairs={{0,192},{32,224},{64,0},{96,32},{128,64},{160,96},{192,128},{224,1... | collective-permute-start | bytes 1179656 | tf_op jit(solution)/shard_map/ppermute | solution.py:319
  268.1 7.3 %collective-permute-start.30 = (f32[1,48,8,128]{3,2,1,0:T(8,128)S(1)}, f32[1,48,8,128]{3,2,1,0:T(8,128)S(1)}, u32[]{:S(2)}, u32[]{:S(2)}) collective-permute-start(f32[1,48,8,128]{3,2,1,0:T(8,128)S(1)} %get-tuple-element.99), channel_id=1, source_target_pairs={{0,64},{32,96},{64,128},{96,160},{128,192},{160,224},{192,0},{224,... | collective-permute-start | bytes 589832 | tf_op jit(solution)/shard_map/ppermute | solution.py:315
  269.8 6.1 %collective-permute-start.31 = (f32[1,48,8,128]{3,2,1,0:T(8,128)S(1)}, f32[1,48,8,128]{3,2,1,0:T(8,128)S(1)}, u32[]{:S(2)}, u32[]{:S(2)}) collective-permute-start(f32[1,48,8,128]{3,2,1,0:T(8,128)S(1)} %get-tuple-element.100), channel_id=1, source_target_pairs={{0,192},{32,224},{64,0},{96,32},{128,64},{160,96},{192,128},{224,1... | collective-permute-start | bytes 589832 | tf_op jit(solution)/shard_map/ppermute | solution.py:319
  276.1 10.9 %collective-permute-start.32 = (f32[2,48,8,128]{3,2,1,0:T(8,128)S(1)}, f32[2,48,8,128]{3,2,1,0:T(8,128)S(1)}, u32[]{:S(2)}, u32[]{:S(2)}) collective-permute-start(f32[2,48,8,128]{3,2,1,0:T(8,128)S(1)} %fusion.2.refs_6_), channel_id=1, source_target_pairs={{0,64},{32,96},{64,128},{96,160},{128,192},{160,224},{192,0},{224,... | collective-permute-start | bytes 1179656 | tf_op jit(solution)/shard_map/ppermute | solution.py:315
  279.3 8.8 %collective-permute-start.33 = (f32[2,48,8,128]{3,2,1,0:T(8,128)S(1)}, f32[2,48,8,128]{3,2,1,0:T(8,128)S(1)}, u32[]{:S(2)}, u32[]{:S(2)}) collective-permute-start(f32[2,48,8,128]{3,2,1,0:T(8,128)S(1)} %fusion.2.refs_6_), channel_id=1, source_target_pairs={{0,192},{32,224},{64,0},{96,32},{128,64},{160,96},{192,128},{224,1... | collective-permute-start | bytes 1179656 | tf_op jit(solution)/shard_map/ppermute | solution.py:319
  288.1 7.9 %collective-permute-start.34 = (f32[1,48,8,128]{3,2,1,0:T(8,128)S(1)}, f32[1,48,8,128]{3,2,1,0:T(8,128)S(1)}, u32[]{:S(2)}, u32[]{:S(2)}) collective-permute-start(f32[1,48,8,128]{3,2,1,0:T(8,128)S(1)} %get-tuple-element.156.refs_3_), channel_id=1, source_target_pairs={{0,64},{32,96},{64,128},{96,160},{128,192},{160,224},{192,0},{224,... | collective-permute-start | bytes 589832 | tf_op jit(solution)/shard_map/ppermute | solution.py:315
  289.8 13.9 %collective-permute-start.37 = (f32[6,48,8,128]{3,2,1,0:T(8,128)S(1)}, f32[6,48,8,128]{3,2,1,0:T(8,128)S(1)}, u32[]{:S(2)}, u32[]{:S(2)}) collective-permute-start(f32[6,48,8,128]{3,2,1,0:T(8,128)S(1)} %pad_maximum_fusion.2), channel_id=1, source_target_pairs={{0,32},{32,0},{64,96},{96,64},{128,160},{160,128},{192,224},{224,1... | collective-permute-start | bytes 3538952 | tf_op jit(solution)/shard_map/ppermute | solution.py:311
  293.8 7.5 %collective-permute-start.35 = (f32[1,48,8,128]{3,2,1,0:T(8,128)S(1)}, f32[1,48,8,128]{3,2,1,0:T(8,128)S(1)}, u32[]{:S(2)}, u32[]{:S(2)}) collective-permute-start(f32[1,48,8,128]{3,2,1,0:T(8,128)S(1)} %get-tuple-element.158.refs_1_), channel_id=1, source_target_pairs={{0,192},{32,224},{64,0},{96,32},{128,64},{160,96},{192,128},{224,1... | collective-permute-start | bytes 589832 | tf_op jit(solution)/shard_map/ppermute | solution.py:319
  301.4 2.2 collective-permute-start.36
  (8 other events, 19.0 us)

commit v4 on v2

--- a/solution.py
+++ b/solution.py
@@ -85,35 +85,30 @@
         out_shape=[jax.ShapeDtypeStruct((p * PITCH, N), F32) for _, p in counts],
         in_specs=[pl.BlockSpec(memory_space=pltpu.VMEM)] * (len(ins) + 2),
         out_specs=[pl.BlockSpec(memory_space=pltpu.VMEM)] * len(counts),
-        compiler_params=pltpu.CompilerParams(vmem_limit_bytes=24 * MIB),
+        compiler_params=pltpu.CompilerParams(vmem_limit_bytes=8 * MIB),
         cost_estimate=pl.CostEstimate(flops=planes * 16 * N**3, bytes_accessed=planes * 8 * N * N, transcendentals=0),
         name="lateral",
     )(*ins, left, right)
 
 
-def middle_kernel(sb, so, sa, mb, mo, ma, tf_ref, ta_ref, left_ref, right_ref, own, other, back):
-    tf = tf_ref[...]
-    ta = ta_ref[...]
-
-    def smooth(a):
-        return jnp.concatenate([r[pl.ds(a, r.shape[0] // PITCH, stride=PITCH), :] for r in (sb, so, sa)], 0)
-
-    def recorded(a):
-        return jnp.concatenate([r[a] for r in (mb, mo, ma)], 0)
-
-    @pl.loop(0, N // STEP)
-    def _(i):
-        firsts = [STEP * i + j for j in range(0, STEP, 2)]
-        blurred = [left_product(tf, jnp.concatenate([smooth(a), smooth(a + 1)], 1)) for a in firsts]
-        ratios = []
-        for a, blur in zip(firsts, blurred):
-            rec = jnp.concatenate([recorded(a), recorded(a + 1)], 1)
-            ratios.append(jnp.where(rec > 0, rec / blur, 0.0))
-        for a, ratio in zip(firsts, ratios):
-            res = left_product(ta, ratio)
-            back[pl.ds(a, SLAB, stride=PITCH), :] = res[:, :N]
-            back[pl.ds(a + 1, SLAB, stride=PITCH), :] = res[:, N:]
-
+def strided(refs, a):
+    return jnp.concatenate([r[pl.ds(a, r.shape[0] // PITCH, stride=PITCH), :] for r in refs], 0)
+
+
+def at_row(refs, a):
+    return jnp.concatenate([r[a] for r in refs], 0)
+
+
+def pair(pick, refs, a):
+    return jnp.concatenate([pick(refs, a), pick(refs, a + 1)], 1)
+
+
+def store_back(back, a, res):
+    back[pl.ds(a, SLAB, stride=PITCH), :] = res[:, :N]
+    back[pl.ds(a + 1, SLAB, stride=PITCH), :] = res[:, N:]
+
+
+def logs_out(back, left_ref, right_ref, own, other):
     left = left_ref[...]
     right = right_ref[...]
 
@@ -127,8 +122,26 @@
                 other[p, z] = logs[j * N + 64 + 8 * p : j * N + 64 + 8 * p + 8]
 
 
+def middle_kernel(sb, so, sa, mb, mo, ma, tf_ref, ta_ref, left_ref, right_ref, own, other, back):
+    tf = tf_ref[...]
+    ta = ta_ref[...]
+
+    @pl.loop(0, N // STEP)
+    def _(i):
+        firsts = [STEP * i + j for j in range(0, STEP, 2)]
+        blurred = [left_product(tf, pair(strided, (sb, so, sa), a)) for a in firsts]
+        ratios = []
+        for a, blur in zip(firsts, blurred):
+            rec = pair(at_row, (mb, mo, ma), a)
+            ratios.append(jnp.where(rec > 0, rec / blur, 0.0))
+        for a, ratio in zip(firsts, ratios):
+            store_back(back, a, left_product(ta, ratio))
+
+    logs_out(back, left_ref, right_ref, own, other)
+
+
 def middle(smooth, recorded, tf, ta, left, right):
-    ins = [*smooth, *recorded, tf, ta, left, right]
+    ins = (*smooth, *recorded, tf, ta, left, right)
     half = jax.ShapeDtypeStruct((8, SLAB, 8, N), F32)
     return pl.pallas_call(
         middle_kernel,
@@ -136,7 +149,7 @@
         in_specs=[pl.BlockSpec(memory_space=pltpu.VMEM)] * len(ins),
         out_specs=[pl.BlockSpec(memory_space=pltpu.VMEM)] * 2,
         scratch_shapes=[pltpu.VMEM((SLAB * PITCH, N), F32)],
-        compiler_params=pltpu.CompilerParams(vmem_limit_bytes=32 * MIB),
+        compiler_params=pltpu.CompilerParams(vmem_limit_bytes=12 * MIB),
         cost_estimate=pl.CostEstimate(flops=8 * 10**9, bytes_accessed=15 * MIB, transcendentals=SLAB * N * N),
         name="middle",
     )(*ins)
@@ -156,9 +169,38 @@
     return jnp.concatenate([hi, lo], 1)
 
 
+def turn(src, dst):
+    @pl.loop(0, N // 8)
+    def _(i):
+        at = pl.multiple_of(8 * i, 8)
+        for zb in range(0, src.shape[0], 8):
+            block = jnp.stack([src[z, pl.ds(at, 8), :] for z in range(zb, zb + 8)], 0)
+            block = jnp.swapaxes(block, 0, 1)
+            for j in range(8):
+                dst[at + j, zb : zb + 8, :] = block[j]
+
+
+def turn_kernel(before, after, before_t, after_t):
+    turn(before, before_t)
+    turn(after, after_t)
+
+
+def turned(before, after):
+    vmem = pl.BlockSpec(memory_space=pltpu.VMEM)
+    edge = jax.ShapeDtypeStruct((N, HALF, N), F32)
+    return pl.pallas_call(
+        turn_kernel,
+        out_shape=[edge, edge],
+        in_specs=[vmem, vmem],
+        out_specs=[vmem, vmem],
+        compiler_params=pltpu.CompilerParams(vmem_limit_bytes=4 * MIB),
+        name="turn",
+    )(before, after)
+
+
 def prep_kernel(
     starts, taps, mx_ref, my_ref, rec,
-    tf, ta, x_all, x_halves, x_pieces, adj_x, fwd_y, adj_y, rec_t, rec_first, rec_last, xt_ref,
+    tf, ta, x_all, x_halves, x_pieces, adj_x, fwd_y, adj_y, rec_t, xt_ref,
 ):
     def toeplitz(rows, cols, flip):
         i = lax.broadcasted_iota(jnp.int32, (rows, 2 * cols), 0)
@@ -188,32 +230,18 @@
     halves = row_blocks([core * 64 + 8 * p for p in range(8)] + [64 - core * 64 + 8 * p for p in range(8)])
     x_halves[...] = operand_rows(twice(halves.T, 1))
 
-    @pl.loop(0, N // 8)
-    def _(i):
-        at = pl.multiple_of(8 * i, 8)
-        for zb in range(0, SLAB, 8):
-            block = jnp.stack([rec[z, pl.ds(at, 8), :] for z in range(zb, zb + 8)], 0)
-            block = jnp.swapaxes(block, 0, 1)
-            for j in range(8):
-                rec_t[at + j, zb : zb + 8, :] = block[j]
-                if zb < HALF:
-                    rec_first[at + j, zb : zb + 8, :] = block[j]
-                if zb >= SLAB - HALF:
-                    rec_last[at + j, zb - SLAB + HALF : zb - SLAB + HALF + 8, :] = block[j]
+    turn(rec, rec_t)
 
 
 def prep(starts, taps, mx, my, rec):
     full = SLAB + 2 * HALF
     wide = SLAB + 2 * FAR
     square = jax.ShapeDtypeStruct((2 * N, 2 * N), BF16)
-    edge = jax.ShapeDtypeStruct((N, HALF, N), F32)
     outs = [
         jax.ShapeDtypeStruct((2 * full, 2 * wide), BF16),
         jax.ShapeDtypeStruct((2 * SLAB, 2 * full), BF16),
         *[square] * 6,
         jax.ShapeDtypeStruct((N, SLAB, N), F32),
-        edge,
-        edge,
     ]
     vmem = pl.BlockSpec(memory_space=pltpu.VMEM)
     smem = pl.BlockSpec(memory_space=pltpu.SMEM)
@@ -223,7 +251,7 @@
         in_specs=[smem, smem, vmem, vmem, vmem],
         out_specs=[vmem] * len(outs),
         scratch_shapes=[pltpu.VMEM((N, N), F32)],
-        compiler_params=pltpu.CompilerParams(vmem_limit_bytes=20 * MIB),
+        compiler_params=pltpu.CompilerParams(vmem_limit_bytes=8 * MIB),
         name="prep",
     )(starts, taps, mx, my, rec)
 
@@ -244,7 +272,7 @@
         out_shape=jax.ShapeDtypeStruct((SLAB, N, N), F32),
         in_specs=[pl.BlockSpec(memory_space=pltpu.SMEM)] + [pl.BlockSpec(memory_space=pltpu.VMEM)] * len(pieces),
         out_specs=pl.BlockSpec(memory_space=pltpu.VMEM),
-        compiler_params=pltpu.CompilerParams(vmem_limit_bytes=16 * MIB),
+        compiler_params=pltpu.CompilerParams(vmem_limit_bytes=4 * MIB),
         name="place",
     )(starts, *pieces)
 
@@ -299,36 +327,32 @@
     order = jnp.stack([2 * opp, 2 * nxt + 1, 2 * opp + 1, 2 * prv, 2 * nxt, 2 * prv + 1, 2 * chip, 2 * chip + 1])
     starts = jnp.concatenate([core * 64 + 8 * order, (1 - core) * 64 + 8 * order, core[None]]).astype(jnp.int32)
 
-    half = lax.dynamic_slice_in_dim(estimate, core * 64, 64, axis=1)
-    before = up(half[SLAB - FAR :])
-    after = down(half[:FAR])
-    tf, ta, x_all, x_halves, x_fwd, adj_x, fwd_y, adj_y, rec_own, rec_first, rec_last = prep(
-        starts, depth_taps, mx, my, recorded
-    )
-    before, after, rec_first, rec_last = lax.optimization_barrier((before, after, rec_first, rec_last))
-    rec_before = up(rec_last)
-    rec_after = down(rec_first)
+    before = up(lax.dynamic_slice(estimate, (SLAB - FAR, core * 64, 0), (FAR, 64, N)))
+    after = down(lax.dynamic_slice(estimate, (0, core * 64, 0), (FAR, 64, N)))
+    rec_before = up(recorded[SLAB - HALF :])
+    rec_after = down(recorded[:HALF])
+    tf, ta, x_all, x_halves, x_fwd, adj_x, fwd_y, adj_y, rec_own = prep(starts, depth_taps, mx, my, recorded)
+    mine = lax.dynamic_slice(estimate, (0, core * 64 + chip * 16, 0), (SLAB, 16, N))
+    mine = jnp.stack([mine[:, :8], mine[:, 8:]], 0)
     before2, after2 = to_core(before), to_core(after)
-
-    def middle_of(smooth):
-        return middle(smooth, (rec_before, rec_own, rec_after), tf, ta, adj_x, adj_y)
-
-    mine = jnp.stack(
-        [lax.dynamic_slice_in_dim(estimate, starts[6 + k], 8, axis=1) for k in range(2)], 0
-    )
 
     (smooth_own,) = lateral([[estimate]], x_all, fwd_y)
     smooth_b, smooth_a = lateral([[before, before2], [after, after2]], x_halves, fwd_y)
-    own, other = middle_of((smooth_b, smooth_own, smooth_a))
+    rec_before, rec_after, smooth_b, smooth_a = lax.optimization_barrier((rec_before, rec_after, smooth_b, smooth_a))
+    smooth = (smooth_b, smooth_own, smooth_a)
+    rec_before, rec_after = turned(rec_before, rec_after)
+    own, other = middle(smooth, (rec_before, rec_own, rec_after), tf, ta, adj_x, adj_y)
     mine = mine * jnp.exp(reduce_chunk(other, own) / 8.0)
 
     prev_c, next_c = to_next(mine), to_prev(mine)
     b0, a0 = up(mine[:, SLAB - FAR :]), down(mine[:, :FAR])
+    prev_c, next_c, b0, a0 = lax.optimization_barrier((prev_c, next_c, b0, a0))
     opp_a, opp_b = to_next(prev_c[0:1]), to_prev(next_c[1:2])
     sides = jnp.concatenate([prev_c, next_c], 0)
     b1, a1 = up(sides[:, SLAB - FAR :]), down(sides[:, :FAR])
     near = jnp.concatenate([mine, sides], 0)
     near2 = to_core(near)
+    opp_a, opp_b, near2 = lax.optimization_barrier((opp_a, opp_b, near2))
     opp_c = jnp.concatenate([opp_a, opp_b], 0)
     b2, a2 = up(opp_c[:, SLAB - FAR :]), down(opp_c[:, :FAR])
     opp2 = to_core(opp_c)
@@ -350,9 +374,10 @@
         x_fwd,
         fwd_y,
     )
-    own, other = middle_of((smooth_b, smooth_own, smooth_a))
+    smooth = (smooth_b, smooth_own, smooth_a)
+    own, other = middle(smooth, (rec_before, rec_own, rec_after), tf, ta, adj_x, adj_y)
     mine = mine * jnp.exp(reduce_chunk(other, own) / 8.0)
-    prev_c, next_c = to_next(mine), to_prev(mine)
+    prev_c, next_c = lax.optimization_barrier((to_next(mine), to_prev(mine)))
     near = jnp.concatenate([mine, prev_c, next_c], 0)
     near2 = to_core(near)
     opp_c = jnp.concatenate([to_next(prev_c[0:1]), to_prev(next_c[1:2])], 0)

time: 266 us -> 273 us (1.026)
  the two profiles are of different devices: /device:TPU:15 before, /device:TPU:31 now
where the time goes in v4:
time: 273 us; the launch traced here: 272 us
  waiting for transfers between devices  143 us (52%)
  starting transfers between devices  85.7 us (31%)
  Pallas kernels  32.6 us (12%)
  local copies, waits for them, and re-layouts  6.65 us (2%)
  other arithmetic  3.41 us (1%)
    ppermute x8, waiting for transfers between devices, to_next(): return lax.ppermute(x, 'view', [(i, (i + 2) % 8) for i in range(8)])  45.7 us
    ppermute x5, waiting for transfers between devices, up(): return lax.ppermute(x, 'gz', [(i, i + 1) for i in range(n - 1)])  40 us
    ppermute x5, waiting for transfers between devices, down(): return lax.ppermute(x, 'gz', [(i + 1, i) for i in range(n - 1)])  37.1 us
    ppermute x5, starting transfers between devices, up(): return lax.ppermute(x, 'gz', [(i, i + 1) for i in range(n - 1)])  22.9 us
    ppermute x10, starting transfers between devices, to_core(): return lax.ppermute(x, 'view', [(i, i ^ 1) for i in range(8)])  18.3 us
    ppermute x8, starting transfers between devices, to_next(): return lax.ppermute(x, 'view', [(i, (i + 2) % 8) for i in range(8)])  16.4 us
    ppermute x8, starting transfers between devices, to_prev(): return lax.ppermute(x, 'view', [(i, (i - 2) % 8) for i in range(8)])  15.2 us
    pallas_call x2, Pallas kernels, middle(): pl.pallas_call(middle_kernel, out_shape=[half, half], in_specs=[pl.BlockS...  13.5 us
  transfers between devices with their start and end apart: 36, of which 24 were waited for; matrix products, arithmetic and copies ran while one was open for 1% of the time, Pallas kernels for 4%

profile of v4, /device:TPU:31, one launch (start us, length us, event | category | flops | bytes accessed | tf_op | source)
XLA Modules:
  0.0 272.4 jit_solution(10414313700191934340)
XLA Ops:
  1.8 3.1 %collective-permute-start.2 = (f32[32,64,128]{2,1,0:T(8,128)S(1)}, f32[32,64,128]{2,1,0:T(8,128)}, u32[]{:S(2)}, u32[]{:S(2)}) collective-permute-start(f32[32,64,128]{2,1,0:T(8,128)S(1)} %get-tuple-element.94), channel_id=1, source_target_pairs={{0,1},{1,2},{2,3},{3,4},{4,5},{5,6},{6,7},{7,8},{8,9},{9,10},{10,1... | collective-permute-start | bytes 3145736 | tf_op jit(solution)/shard_map/ppermute | solution.py:294
  5.0 2.3 collective-permute-start.4
  7.3 20.6 %collective-permute-done.2.refs_0_ = f32[32,64,128]{2,1,0:T(8,128)} collective-permute-done((f32[32,64,128]{2,1,0:T(8,128)S(1)}, f32[32,64,128]{2,1,0:T(8,128)}, u32[]{:S(2)}, u32[]{:S(2)}) %collective-permute-start.2) | collective-permute-done | bytes 1048608 | tf_op jit(solution)/shard_map/ppermute | solution.py:294
  29.4 5.6 %collective-permute-done.4.refs_2_ = f32[32,64,128]{2,1,0:T(8,128)} collective-permute-done((f32[32,64,128]{2,1,0:T(8,128)S(1)}, f32[32,64,128]{2,1,0:T(8,128)}, u32[]{:S(2)}, u32[]{:S(2)}) %collective-permute-start.4) | collective-permute-done | bytes 1048608 | tf_op jit(solution)/shard_map/ppermute | solution.py:299
  38.4 1.9 collective-permute-start
  40.3 3.4 %collective-permute-start.1 = (f32[16,128,128]{2,1,0:T(8,128)}, f32[16,128,128]{2,1,0:T(8,128)}, u32[]{:S(2)}, u32[]{:S(2)}) collective-permute-start(f32[16,128,128]{2,1,0:T(8,128)} %get-tuple-element.95), channel_id=1, source_target_pairs={{1,0},{2,1},{3,2},{4,3},{5,4},{6,5},{7,6},{8,7},{9,8},{10,9},{11,1... | collective-permute-start | bytes 3145736 | tf_op jit(solution)/shard_map/ppermute | solution.py:299
  47.7 2.2 lateral.5.so
  50.0 5.2 %lateral.4 = (f32[4224,128]{1,0:T(8,128)S(1)}, f32[4224,128]{1,0:T(8,128)S(1)}) custom-call(f32[32,64,128]{2,1,0:T(8,128)} %collective-permute-done.2.refs_0_, f32[32,64,128]{2,1,0:T(8,128)} %collective-permute-done.3.refs_1_, f32[32,64,128]{2,1,0:T(8,128)} %collective-permute-done.4.refs_2_, f32[32,64,128]{2,1,0:T(8,128)} %collective-permute-done.5.refs_3_, ...), custom_call_target="tpu_custom_call" | custom-call | flops 2147483648 | bytes 8388608 | tf_op jit(solution)/shard_map/lateral/pallas_call | solution.py:83
  55.2 10.2 %collective-permute-done.before = f32[16,128,128]{2,1,0:T(8,128)} collective-permute-done((f32[16,128,128]{2,1,0:T(8,128)}, f32[16,128,128]{2,1,0:T(8,128)}, u32[]{:S(2)}, u32[]{:S(2)}) %collective-permute-start) | collective-permute-done | bytes 1048608 | tf_op jit(solution)/shard_map/ppermute | solution.py:294
  65.4 6.1 %collective-permute-done.1.after = f32[16,128,128]{2,1,0:T(8,128)} collective-permute-done((f32[16,128,128]{2,1,0:T(8,128)}, f32[16,128,128]{2,1,0:T(8,128)}, u32[]{:S(2)}, u32[]{:S(2)}) %collective-permute-start.1) | collective-permute-done | bytes 1048608 | tf_op jit(solution)/shard_map/ppermute | solution.py:299
  71.5 2.1 turn.1
  73.7 6.7 %middle.2 = (f32[8,48,8,128]{3,2,1,0:T(8,128)S(1)}, f32[8,48,8,128]{3,2,1,0:T(8,128)S(1)}) custom-call(f32[4224,128]{1,0:T(8,128)S(1)} %get-tuple-element.53.sb, f32[6336,128]{1,0:T(8,128)S(1)} %lateral.5.so, f32[4224,128]{1,0:T(8,128)S(1)} %get-tuple-element.55.sa, f32[128,16,128]{2,1,0:T(8,128)S(1)} %get-tuple-element.58.mb, ...), custom_call_target="tpu_custom_call" | custom-call | flops 8000000000 | bytes 15728640 | tf_op jit(solution)/shard_map/middle/pallas_call | solution.py:146
  81.4 3.0 %collective-permute-done.6 = f32[8,48,8,128]{3,2,1,0:T(8,128)S(1)} collective-permute-done((f32[8,48,8,128]{3,2,1,0:T(8,128)S(1)}, f32[8,48,8,128]{3,2,1,0:T(8,128)S(1)}, u32[]{:S(2)}, u32[]{:S(2)}) %collective-permute-start.6) | collective-permute-done | bytes 1572896 | tf_op jit(solution)/shard_map/ppermute | solution.py:281
  84.7 3.1 %collective-permute-start.7 = (f32[2,48,8,128]{3,2,1,0:T(8,128)S(1)}, f32[2,48,8,128]{3,2,1,0:T(8,128)S(1)}, u32[]{:S(2)}, u32[]{:S(2)}) collective-permute-start(f32[2,48,8,128]{3,2,1,0:T(8,128)S(1)} %get-tuple-element.120), channel_id=1, source_target_pairs={{0,64},{32,96},{64,128},{96,160},{128,192},{160,224},{192,0},{224,... | collective-permute-start | bytes 1179656 | tf_op jit(solution)/shard_map/ppermute | solution.py:285
  87.8 2.2 collective-permute-start.8
  90.0 10.2 %collective-permute-done.7 = f32[2,48,8,128]{3,2,1,0:T(8,128)S(1)} collective-permute-done((f32[2,48,8,128]{3,2,1,0:T(8,128)S(1)}, f32[2,48,8,128]{3,2,1,0:T(8,128)S(1)}, u32[]{:S(2)}, u32[]{:S(2)}) %collective-permute-start.7) | collective-permute-done | bytes 393248 | tf_op jit(solution)/shard_map/ppermute | solution.py:285
  101.3 2.9 %collective-permute-start.9 = (f32[1,48,8,128]{3,2,1,0:T(8,128)}, f32[1,48,8,128]{3,2,1,0:T(8,128)}, u32[]{:S(2)}, u32[]{:S(2)}) collective-permute-start(f32[1,48,8,128]{3,2,1,0:T(8,128)} %get-tuple-element.69), channel_id=1, source_target_pairs={{0,64},{32,96},{64,128},{96,160},{128,192},{160,224},{192,0},{224,... | collective-permute-start | bytes 589832 | tf_op jit(solution)/shard_map/ppermute | solution.py:285
  104.9 4.6 %collective-permute-done.9 = f32[1,48,8,128]{3,2,1,0:T(8,128)} collective-permute-done((f32[1,48,8,128]{3,2,1,0:T(8,128)}, f32[1,48,8,128]{3,2,1,0:T(8,128)}, u32[]{:S(2)}, u32[]{:S(2)}) %collective-permute-start.9) | collective-permute-done | bytes 196640 | tf_op jit(solution)/shard_map/ppermute | solution.py:285
  113.2 2.2 collective-permute-start.12
  115.4 10.3 %collective-permute-start.13 = (f32[2,32,8,128]{3,2,1,0:T(8,128)S(1)}, f32[2,32,8,128]{3,2,1,0:T(8,128)S(1)}, u32[]{:S(2)}, u32[]{:S(2)}) collective-permute-start(f32[2,32,8,128]{3,2,1,0:T(8,128)S(1)} %get-tuple-element.158), channel_id=1, source_target_pairs={{0,1},{1,2},{2,3},{3,4},{4,5},{5,6},{6,7},{7,8},{8,9},{9,10},{10,1... | collective-permute-start | bytes 786440 | tf_op jit(solution)/shard_map/ppermute | solution.py:294
  125.8 1.9 collective-permute-start.14
  129.1 11.1 %collective-permute-done.14.refs_20_ = f32[2,32,8,128]{3,2,1,0:T(8,128)S(1)} collective-permute-done((f32[2,32,8,128]{3,2,1,0:T(8,128)S(1)}, f32[2,32,8,128]{3,2,1,0:T(8,128)S(1)}, u32[]{:S(2)}, u32[]{:S(2)}) %collective-permute-start.14) | collective-permute-done | bytes 262176 | tf_op jit(solution)/shard_map/ppermute | solution.py:299
  140.3 6.4 %collective-permute-start.17 = (f32[6,48,8,128]{3,2,1,0:T(8,128)S(1)}, f32[6,48,8,128]{3,2,1,0:T(8,128)S(1)}, u32[]{:S(2)}, u32[]{:S(2)}) collective-permute-start(f32[6,48,8,128]{3,2,1,0:T(8,128)S(1)} %pad_maximum_fusion.1), channel_id=1, source_target_pairs={{0,32},{32,0},{64,96},{96,64},{128,160},{160,128},{192,224},{224,1... | collective-permute-start | bytes 3538952 | tf_op jit(solution)/shard_map/ppermute | solution.py:281
  146.8 1.9 collective-permute-start.19
  148.8 3.4 %collective-permute-start.22 = (f32[4,32,8,128]{3,2,1,0:T(8,128)S(1)}, f32[4,32,8,128]{3,2,1,0:T(8,128)S(1)}, u32[]{:S(2)}, u32[]{:S(2)}) collective-permute-start(f32[4,32,8,128]{3,2,1,0:T(8,128)S(1)} %get-tuple-element.129), channel_id=1, source_target_pairs={{1,0},{2,1},{3,2},{4,3},{5,4},{6,5},{7,6},{8,7},{9,8},{10,9},{11,1... | collective-permute-start | bytes 1572872 | tf_op jit(solution)/shard_map/ppermute | solution.py:299
  153.3 2.7 collective-permute-start.16
  155.9 6.3 %collective-permute-done.19 = f32[4,32,8,128]{3,2,1,0:T(8,128)S(1)} collective-permute-done((f32[4,32,8,128]{3,2,1,0:T(8,128)S(1)}, f32[4,32,8,128]{3,2,1,0:T(8,128)S(1)}, u32[]{:S(2)}, u32[]{:S(2)}) %collective-permute-start.19) | collective-permute-done | bytes 524320 | tf_op jit(solution)/shard_map/ppermute | solution.py:294
  162.3 6.1 %collective-permute-done.22 = f32[4,32,8,128]{3,2,1,0:T(8,128)S(1)} collective-permute-done((f32[4,32,8,128]{3,2,1,0:T(8,128)S(1)}, f32[4,32,8,128]{3,2,1,0:T(8,128)S(1)}, u32[]{:S(2)}, u32[]{:S(2)}) %collective-permute-start.22) | collective-permute-done | bytes 524320 | tf_op jit(solution)/shard_map/ppermute | solution.py:299
  170.0 5.6 %collective-permute-start.18 = (f32[2,32,8,128]{3,2,1,0:T(8,128)S(1)}, f32[2,32,8,128]{3,2,1,0:T(8,128)S(1)}, u32[]{:S(2)}, u32[]{:S(2)}) collective-permute-start(f32[2,32,8,128]{3,2,1,0:T(8,128)S(1)} %get-tuple-element.156), channel_id=1, source_target_pairs={{0,1},{1,2},{2,3},{3,4},{4,5},{5,6},{6,7},{7,8},{8,9},{9,10},{10,1... | collective-permute-start | bytes 786440 | tf_op jit(solution)/shard_map/ppermute | solution.py:294
  175.6 1.9 collective-permute-start.20
  180.4 8.0 %collective-permute-done.20 = f32[2,32,8,128]{3,2,1,0:T(8,128)S(1)} collective-permute-done((f32[2,32,8,128]{3,2,1,0:T(8,128)S(1)}, f32[2,32,8,128]{3,2,1,0:T(8,128)S(1)}, u32[]{:S(2)}, u32[]{:S(2)}) %collective-permute-start.20) | collective-permute-done | bytes 262176 | tf_op jit(solution)/shard_map/ppermute | solution.py:299
  188.5 2.1 collective-permute-start.21
  190.7 2.3 lateral.7.so
  193.2 3.1 %lateral.6 = (f32[4224,128]{1,0:T(8,128)S(1)}, f32[4224,128]{1,0:T(8,128)S(1)}) custom-call(f32[1,32,8,128]{3,2,1,0:T(8,128)S(1)} %get-tuple-element.162.refs_0_, f32[1,32,8,128]{3,2,1,0:T(8,128)S(1)} %get-tuple-element.142.refs_1_, f32[1,32,8,128]{3,2,1,0:T(8,128)S(1)} %get-tuple-element.161.refs_2_, f32[1,32,8,128]{3,2,1,0:T(8,128)S(1)} %get-tuple-element.141.refs_3_, ...), custom_call_target="tpu_custom_call" | custom-call | flops 2147483648 | bytes 8388608 | tf_op jit(solution)/shard_map/lateral/pallas_call | solution.py:83
  196.4 6.8 %middle.3 = (f32[8,48,8,128]{3,2,1,0:T(8,128)S(1)}, f32[8,48,8,128]{3,2,1,0:T(8,128)S(1)}) custom-call(f32[4224,128]{1,0:T(8,128)S(1)} %get-tuple-element.80.sb, f32[6336,128]{1,0:T(8,128)S(1)} %lateral.7.so, f32[4224,128]{1,0:T(8,128)S(1)} %get-tuple-element.82.sa, f32[128,16,128]{2,1,0:T(8,128)S(1)} %copy-done.9, f32[128,48,128]{2,1,0:T(8,128)S(1)} %copy-done.7, ...), custom_call_target="tpu_custom_call" | custom-call | flops 8000000000 | bytes 15728640 | tf_op jit(solution)/shard_map/middle/pallas_call | solution.py:146
  203.3 3.4 %collective-permute-done.25 = f32[8,48,8,128]{3,2,1,0:T(8,128)S(1)} collective-permute-done((f32[8,48,8,128]{3,2,1,0:T(8,128)S(1)}, f32[8,48,8,128]{3,2,1,0:T(8,128)S(1)}, u32[]{:S(2)}, u32[]{:S(2)}) %collective-permute-start.25) | collective-permute-done | bytes 1572896 | tf_op jit(solution)/shard_map/ppermute | solution.py:281
  208.0 2.6 collective-permute-start.27
  210.5 14.5 %collective-permute-done.26 = f32[2,48,8,128]{3,2,1,0:T(8,128)S(1)} collective-permute-done((f32[2,48,8,128]{3,2,1,0:T(8,128)S(1)}, f32[2,48,8,128]{3,2,1,0:T(8,128)S(1)}, u32[]{:S(2)}, u32[]{:S(2)}) %collective-permute-start.26) | collective-permute-done | bytes 393248 | tf_op jit(solution)/shard_map/ppermute | solution.py:285
  225.0 3.0 %collective-permute-done.27 = f32[2,48,8,128]{3,2,1,0:T(8,128)S(1)} collective-permute-done((f32[2,48,8,128]{3,2,1,0:T(8,128)S(1)}, f32[2,48,8,128]{3,2,1,0:T(8,128)S(1)}, u32[]{:S(2)}, u32[]{:S(2)}) %collective-permute-start.27) | collective-permute-done | bytes 393248 | tf_op jit(solution)/shard_map/ppermute | solution.py:289
  229.6 2.7 collective-permute-start.29
  232.2 7.3 %collective-permute-done.28 = f32[1,48,8,128]{3,2,1,0:T(8,128)S(1)} collective-permute-done((f32[1,48,8,128]{3,2,1,0:T(8,128)S(1)}, f32[1,48,8,128]{3,2,1,0:T(8,128)S(1)}, u32[]{:S(2)}, u32[]{:S(2)}) %collective-permute-start.28) | collective-permute-done | bytes 196640 | tf_op jit(solution)/shard_map/ppermute | solution.py:285
  241.5 3.8 %collective-permute-start.30 = (f32[2,48,8,128]{3,2,1,0:T(8,128)S(1)}, f32[2,48,8,128]{3,2,1,0:T(8,128)S(1)}, u32[]{:S(2)}, u32[]{:S(2)}) collective-permute-start(f32[2,48,8,128]{3,2,1,0:T(8,128)S(1)} %fusion.2.refs_6_), channel_id=1, source_target_pairs={{0,64},{32,96},{64,128},{96,160},{128,192},{160,224},{192,0},{224,... | collective-permute-start | bytes 1179656 | tf_op jit(solution)/shard_map/ppermute | solution.py:285
  245.4 8.3 %collective-permute-done.30 = f32[2,48,8,128]{3,2,1,0:T(8,128)S(1)} collective-permute-done((f32[2,48,8,128]{3,2,1,0:T(8,128)S(1)}, f32[2,48,8,128]{3,2,1,0:T(8,128)S(1)}, u32[]{:S(2)}, u32[]{:S(2)}) %collective-permute-start.30) | collective-permute-done | bytes 393248 | tf_op jit(solution)/shard_map/ppermute | solution.py:285
  253.7 2.4 collective-permute-done.31
  257.7 2.1 collective-permute-start.35
  259.8 2.2 collective-permute-start.33
  262.8 4.5 %collective-permute-done.33.refs_2_ = f32[1,48,8,128]{3,2,1,0:T(8,128)S(1)} collective-permute-done((f32[1,48,8,128]{3,2,1,0:T(8,128)S(1)}, f32[1,48,8,128]{3,2,1,0:T(8,128)S(1)}, u32[]{:S(2)}, u32[]{:S(2)}) %collective-permute-start.33) | collective-permute-done | bytes 196640 | tf_op jit(solution)/shard_map/ppermute | solution.py:289
  269.7 2.6 place.1
  (124 shorter events, 34.5 us)
Async XLA Ops:
  0.0 36.9 %copy-start.1 = (f32[1,48,128,128]{3,2,1,0:T(8,128)S(1)}, f32[1,48,128,128]{3,2,1,0:T(8,128)}, u32[]{:S(2)}) copy-start(f32[1,48,128,128]{3,2,1,0:T(8,128)} %param.6) | copy-start | bytes 9437188
  1.8 26.0 %collective-permute-start.2 = (f32[32,64,128]{2,1,0:T(8,128)S(1)}, f32[32,64,128]{2,1,0:T(8,128)}, u32[]{:S(2)}, u32[]{:S(2)}) collective-permute-start(f32[32,64,128]{2,1,0:T(8,128)S(1)} %get-tuple-element.94), channel_id=1, source_target_pairs={{0,1},{1,2},{2,3},{3,4},{4,5},{5,6},{6,7},{7,8},{8,9},{9,10},{10,1... | collective-permute-start | bytes 3145736 | tf_op jit(solution)/shard_map/ppermute | solution.py:294
  5.0 39.0 %copy-start.3 = (f32[1,128,128]{2,1,0:T(8,128)S(1)}, f32[1,128,128]{2,1,0:T(8,128)}, u32[]{:S(2)}) copy-start(f32[1,128,128]{2,1,0:T(8,128)} %param.7) | copy-start | bytes 196612
  5.0 39.0 %copy-start.4 = (f32[1,128,128]{2,1,0:T(8,128)S(1)}, f32[1,128,128]{2,1,0:T(8,128)}, u32[]{:S(2)}) copy-start(f32[1,128,128]{2,1,0:T(8,128)} %param.8) | copy-start | bytes 196612
  5.0 38.9 %copy-start.5 = (f32[1,33]{1,0:T(1,128)S(1)}, f32[1,33]{1,0:T(1,128)}, u32[]{:S(2)}) copy-start(f32[1,33]{1,0:T(1,128)} %taps.1) | copy-start | bytes 400
  5.0 30.1 %collective-permute-start.4 = (f32[32,64,128]{2,1,0:T(8,128)S(1)}, f32[32,64,128]{2,1,0:T(8,128)}, u32[]{:S(2)}, u32[]{:S(2)}) collective-permute-start(f32[32,64,128]{2,1,0:T(8,128)S(1)} %get-tuple-element.93), channel_id=1, source_target_pairs={{1,0},{2,1},{3,2},{4,3},{5,4},{6,5},{7,6},{8,7},{9,8},{10,9},{11,1... | collective-permute-start | bytes 3145736 | tf_op jit(solution)/shard_map/ppermute | solution.py:299
  27.9 22.1 %collective-permute-start.3 = (f32[32,64,128]{2,1,0:T(8,128)}, f32[32,64,128]{2,1,0:T(8,128)}, u32[]{:S(2)}, u32[]{:S(2)}) collective-permute-start(f32[32,64,128]{2,1,0:T(8,128)} %collective-permute-done.2.refs_0_), channel_id=1, source_target_pairs={{0,32},{32,0},{64,96},{96,64},{128,160},{160,128},{192,224},{224,1... | collective-permute-start | bytes 3145736 | tf_op jit(solution)/shard_map/ppermute | solution.py:281
  35.1 14.9 %collective-permute-start.5 = (f32[32,64,128]{2,1,0:T(8,128)}, f32[32,64,128]{2,1,0:T(8,128)}, u32[]{:S(2)}, u32[]{:S(2)}) collective-permute-start(f32[32,64,128]{2,1,0:T(8,128)} %collective-permute-done.4.refs_2_), channel_id=1, source_target_pairs={{0,32},{32,0},{64,96},{96,64},{128,160},{160,128},{192,224},{224,1... | collective-permute-start | bytes 3145736 | tf_op jit(solution)/shard_map/ppermute | solution.py:281
  38.4 27.0 %collective-permute-start = (f32[16,128,128]{2,1,0:T(8,128)}, f32[16,128,128]{2,1,0:T(8,128)}, u32[]{:S(2)}, u32[]{:S(2)}) collective-permute-start(f32[16,128,128]{2,1,0:T(8,128)} %get-tuple-element.96), channel_id=1, source_target_pairs={{0,1},{1,2},{2,3},{3,4},{4,5},{5,6},{6,7},{7,8},{8,9},{9,10},{10,1... | collective-permute-start | bytes 3145736 | tf_op jit(solution)/shard_map/ppermute | solution.py:294
  40.3 31.2 %collective-permute-start.1 = (f32[16,128,128]{2,1,0:T(8,128)}, f32[16,128,128]{2,1,0:T(8,128)}, u32[]{:S(2)}, u32[]{:S(2)}) collective-permute-start(f32[16,128,128]{2,1,0:T(8,128)} %get-tuple-element.95), channel_id=1, source_target_pairs={{1,0},{2,1},{3,2},{4,3},{5,4},{6,5},{7,6},{8,7},{9,8},{10,9},{11,1... | collective-permute-start | bytes 3145736 | tf_op jit(solution)/shard_map/ppermute | solution.py:299
  47.5 26.2 %copy-start.6 = (f32[128,48,128]{2,1,0:T(8,128)}, f32[128,48,128]{2,1,0:T(8,128)S(1)}, u32[]{:S(2)}) copy-start(f32[128,48,128]{2,1,0:T(8,128)S(1)} %get-tuple-element.59.mo) | copy-start | bytes 9437188
  47.5 26.2 %copy-start.12 = (bf16[256,256]{1,0:T(8,128)(2,1)}, bf16[256,256]{1,0:T(8,128)(2,1)S(1)}, u32[]{:S(2)}) copy-start(bf16[256,256]{1,0:T(8,128)(2,1)S(1)} %get-tuple-element.63.left_ref) | copy-start | bytes 393220
  47.5 26.2 %copy-start.14 = (bf16[256,256]{1,0:T(8,128)(2,1)}, bf16[256,256]{1,0:T(8,128)(2,1)S(1)}, u32[]{:S(2)}) copy-start(bf16[256,256]{1,0:T(8,128)(2,1)S(1)} %get-tuple-element.64.right_ref) | copy-start | bytes 393220
  47.5 26.2 %copy-start.16 = (bf16[160,224]{1,0:T(8,128)(2,1)}, bf16[160,224]{1,0:T(8,128)(2,1)S(1)}, u32[]{:S(2)}) copy-start(bf16[160,224]{1,0:T(8,128)(2,1)S(1)} %get-tuple-element.61.tf_ref) | copy-start | bytes 215044
  47.5 26.2 %copy-start.18 = (bf16[96,160]{1,0:T(8,128)(2,1)}, bf16[96,160]{1,0:T(8,128)(2,1)S(1)}, u32[]{:S(2)}) copy-start(bf16[96,160]{1,0:T(8,128)(2,1)S(1)} %get-tuple-element.62.ta_ref) | copy-start | bytes 92164
  73.7 6.8 %copy-start.8 = (f32[128,16,128]{2,1,0:T(8,128)}, f32[128,16,128]{2,1,0:T(8,128)S(1)}, u32[]{:S(2)}) copy-start(f32[128,16,128]{2,1,0:T(8,128)S(1)} %get-tuple-element.58.mb) | copy-start | bytes 3145732
  73.7 6.8 %copy-start.10 = (f32[128,16,128]{2,1,0:T(8,128)}, f32[128,16,128]{2,1,0:T(8,128)S(1)}, u32[]{:S(2)}) copy-start(f32[128,16,128]{2,1,0:T(8,128)S(1)} %get-tuple-element.60.ma) | copy-start | bytes 3145732
  80.5 3.9 %collective-permute-start.6 = (f32[8,48,8,128]{3,2,1,0:T(8,128)S(1)}, f32[8,48,8,128]{3,2,1,0:T(8,128)S(1)}, u32[]{:S(2)}, u32[]{:S(2)}) collective-permute-start(f32[8,48,8,128]{3,2,1,0:T(8,128)S(1)} %get-tuple-element.66), channel_id=1, source_target_pairs={{0,32},{32,0},{64,96},{96,64},{128,160},{160,128},{192,224},{224,1... | collective-permute-start | bytes 4718600 | tf_op jit(solution)/shard_map/ppermute | solution.py:281
  84.6 15.6 %copy-start.20 = (f32[8,48,8,128]{3,2,1,0:T(8,128)}, f32[8,48,8,128]{3,2,1,0:T(8,128)S(1)}, u32[]{:S(2)}) copy-start(f32[8,48,8,128]{3,2,1,0:T(8,128)S(1)} %add.112) | copy-start | bytes 4718596
  84.7 15.5 %collective-permute-start.7 = (f32[2,48,8,128]{3,2,1,0:T(8,128)S(1)}, f32[2,48,8,128]{3,2,1,0:T(8,128)S(1)}, u32[]{:S(2)}, u32[]{:S(2)}) collective-permute-start(f32[2,48,8,128]{3,2,1,0:T(8,128)S(1)} %get-tuple-element.120), channel_id=1, source_target_pairs={{0,64},{32,96},{64,128},{96,160},{128,192},{160,224},{192,0},{224,... | collective-permute-start | bytes 1179656 | tf_op jit(solution)/shard_map/ppermute | solution.py:285
  87.8 12.5 %collective-permute-start.8 = (f32[2,48,8,128]{3,2,1,0:T(8,128)S(1)}, f32[2,48,8,128]{3,2,1,0:T(8,128)S(1)}, u32[]{:S(2)}, u32[]{:S(2)}) collective-permute-start(f32[2,48,8,128]{3,2,1,0:T(8,128)S(1)} %get-tuple-element.119), channel_id=1, source_target_pairs={{0,192},{32,224},{64,0},{96,32},{128,64},{160,96},{192,128},{224,1... | collective-permute-start | bytes 1179656 | tf_op jit(solution)/shard_map/ppermute | solution.py:289
  101.3 8.2 %collective-permute-start.9 = (f32[1,48,8,128]{3,2,1,0:T(8,128)}, f32[1,48,8,128]{3,2,1,0:T(8,128)}, u32[]{:S(2)}, u32[]{:S(2)}) collective-permute-start(f32[1,48,8,128]{3,2,1,0:T(8,128)} %get-tuple-element.69), channel_id=1, source_target_pairs={{0,64},{32,96},{64,128},{96,160},{128,192},{160,224},{192,0},{224,... | collective-permute-start | bytes 589832 | tf_op jit(solution)/shard_map/ppermute | solution.py:285
  104.2 6.1 %collective-permute-start.10 = (f32[1,48,8,128]{3,2,1,0:T(8,128)}, f32[1,48,8,128]{3,2,1,0:T(8,128)}, u32[]{:S(2)}, u32[]{:S(2)}) collective-permute-start(f32[1,48,8,128]{3,2,1,0:T(8,128)} %get-tuple-element.70), channel_id=1, source_target_pairs={{0,192},{32,224},{64,0},{96,32},{128,64},{160,96},{192,128},{224,1... | collective-permute-start | bytes 589832 | tf_op jit(solution)/shard_map/ppermute | solution.py:289
  111.8 28.5 %collective-permute-start.11 = (f32[2,48,8,128]{3,2,1,0:T(8,128)S(1)}, f32[2,48,8,128]{3,2,1,0:T(8,128)S(1)}, u32[]{:S(2)}, u32[]{:S(2)}) collective-permute-start(f32[2,48,8,128]{3,2,1,0:T(8,128)S(1)} %maximum_multiply_fusion.refs_6_), channel_id=1, source_target_pairs={{0,64},{32,96},{64,128},{96,160},{128,192},{160,224},{192,0},{224,... | collective-permute-start | bytes 1179656 | tf_op jit(solution)/shard_map/ppermute | solution.py:285
  113.2 27.1 %collective-permute-start.12 = (f32[2,48,8,128]{3,2,1,0:T(8,128)S(1)}, f32[2,48,8,128]{3,2,1,0:T(8,128)S(1)}, u32[]{:S(2)}, u32[]{:S(2)}) collective-permute-start(f32[2,48,8,128]{3,2,1,0:T(8,128)S(1)} %maximum_multiply_fusion.refs_6_), channel_id=1, source_target_pairs={{0,192},{32,224},{64,0},{96,32},{128,64},{160,96},{192,128},{224,1... | collective-permute-start | bytes 1179656 | tf_op jit(solution)/shard_map/ppermute | solution.py:289
  115.4 13.6 %collective-permute-start.13 = (f32[2,32,8,128]{3,2,1,0:T(8,128)S(1)}, f32[2,32,8,128]{3,2,1,0:T(8,128)S(1)}, u32[]{:S(2)}, u32[]{:S(2)}) collective-permute-start(f32[2,32,8,128]{3,2,1,0:T(8,128)S(1)} %get-tuple-element.158), channel_id=1, source_target_pairs={{0,1},{1,2},{2,3},{3,4},{4,5},{5,6},{6,7},{7,8},{8,9},{9,10},{10,1... | collective-permute-start | bytes 786440 | tf_op jit(solution)/shard_map/ppermute | solution.py:294
  125.8 14.4 %collective-permute-start.14 = (f32[2,32,8,128]{3,2,1,0:T(8,128)S(1)}, f32[2,32,8,128]{3,2,1,0:T(8,128)S(1)}, u32[]{:S(2)}, u32[]{:S(2)}) collective-permute-start(f32[2,32,8,128]{3,2,1,0:T(8,128)S(1)} %get-tuple-element.157), channel_id=1, source_target_pairs={{1,0},{2,1},{3,2},{4,3},{5,4},{6,5},{7,6},{8,7},{9,8},{10,9},{11,1... | collective-permute-start | bytes 786440 | tf_op jit(solution)/shard_map/ppermute | solution.py:299
  140.3 29.5 %collective-permute-start.17 = (f32[6,48,8,128]{3,2,1,0:T(8,128)S(1)}, f32[6,48,8,128]{3,2,1,0:T(8,128)S(1)}, u32[]{:S(2)}, u32[]{:S(2)}) collective-permute-start(f32[6,48,8,128]{3,2,1,0:T(8,128)S(1)} %pad_maximum_fusion.1), channel_id=1, source_target_pairs={{0,32},{32,0},{64,96},{96,64},{128,160},{160,128},{192,224},{224,1... | collective-permute-start | bytes 3538952 | tf_op jit(solution)/shard_map/ppermute | solution.py:281
  146.8 15.4 %collective-permute-start.19 = (f32[4,32,8,128]{3,2,1,0:T(8,128)S(1)}, f32[4,32,8,128]{3,2,1,0:T(8,128)S(1)}, u32[]{:S(2)}, u32[]{:S(2)}) collective-permute-start(f32[4,32,8,128]{3,2,1,0:T(8,128)S(1)} %get-tuple-element.130), channel_id=1, source_target_pairs={{0,1},{1,2},{2,3},{3,4},{4,5},{5,6},{6,7},{7,8},{8,9},{9,10},{10,1... | collective-permute-start | bytes 1572872 | tf_op jit(solution)/shard_map/ppermute | solution.py:294
  148.8 19.7 %collective-permute-start.22 = (f32[4,32,8,128]{3,2,1,0:T(8,128)S(1)}, f32[4,32,8,128]{3,2,1,0:T(8,128)S(1)}, u32[]{:S(2)}, u32[]{:S(2)}) collective-permute-start(f32[4,32,8,128]{3,2,1,0:T(8,128)S(1)} %get-tuple-element.129), channel_id=1, source_target_pairs={{1,0},{2,1},{3,2},{4,3},{5,4},{6,5},{7,6},{8,7},{9,8},{10,9},{11,1... | collective-permute-start | bytes 1572872 | tf_op jit(solution)/shard_map/ppermute | solution.py:299
  152.2 17.7 %collective-permute-start.15 = (f32[1,48,8,128]{3,2,1,0:T(8,128)S(1)}, f32[1,48,8,128]{3,2,1,0:T(8,128)S(1)}, u32[]{:S(2)}, u32[]{:S(2)}) collective-permute-start(f32[1,48,8,128]{3,2,1,0:T(8,128)S(1)} %get-tuple-element.152.refs_3_), channel_id=1, source_target_pairs={{0,64},{32,96},{64,128},{96,160},{128,192},{160,224},{192,0},{224,... | collective-permute-start | bytes 589832 | tf_op jit(solution)/shard_map/ppermute | solution.py:285
  153.3 16.6 %collective-permute-start.16 = (f32[1,48,8,128]{3,2,1,0:T(8,128)S(1)}, f32[1,48,8,128]{3,2,1,0:T(8,128)S(1)}, u32[]{:S(2)}, u32[]{:S(2)}) collective-permute-start(f32[1,48,8,128]{3,2,1,0:T(8,128)S(1)} %get-tuple-element.154.refs_1_), channel_id=1, source_target_pairs={{0,192},{32,224},{64,0},{96,32},{128,64},{160,96},{192,128},{224,1... | collective-permute-start | bytes 589832 | tf_op jit(solution)/shard_map/ppermute | solution.py:289
  168.5 24.5 %collective-permute-start.23 = (f32[12,32,8,128]{3,2,1,0:T(8,128)S(1)}, f32[12,32,8,128]{3,2,1,0:T(8,128)S(1)}, u32[]{:S(2)}, u32[]{:S(2)}) collective-permute-start(f32[12,32,8,128]{3,2,1,0:T(8,128)S(1)} %pad_maximum_fusion), channel_id=1, source_target_pairs={{0,32},{32,0},{64,96},{96,64},{128,160},{160,128},{192,224},{224,1... | collective-permute-start | bytes 4718600 | tf_op jit(solution)/shard_map/ppermute | solution.py:281
  170.0 10.5 %collective-permute-start.18 = (f32[2,32,8,128]{3,2,1,0:T(8,128)S(1)}, f32[2,32,8,128]{3,2,1,0:T(8,128)S(1)}, u32[]{:S(2)}, u32[]{:S(2)}) collective-permute-start(f32[2,32,8,128]{3,2,1,0:T(8,128)S(1)} %get-tuple-element.156), channel_id=1, source_target_pairs={{0,1},{1,2},{2,3},{3,4},{4,5},{5,6},{6,7},{7,8},{8,9},{9,10},{10,1... | collective-permute-start | bytes 786440 | tf_op jit(solution)/shard_map/ppermute | solution.py:294
  175.6 12.8 %collective-permute-start.20 = (f32[2,32,8,128]{3,2,1,0:T(8,128)S(1)}, f32[2,32,8,128]{3,2,1,0:T(8,128)S(1)}, u32[]{:S(2)}, u32[]{:S(2)}) collective-permute-start(f32[2,32,8,128]{3,2,1,0:T(8,128)S(1)} %get-tuple-element.155), channel_id=1, source_target_pairs={{1,0},{2,1},{3,2},{4,3},{5,4},{6,5},{7,6},{8,7},{9,8},{10,9},{11,1... | collective-permute-start | bytes 786440 | tf_op jit(solution)/shard_map/ppermute | solution.py:299
  177.6 13.0 %collective-permute-start.24 = (f32[2,48,8,128]{3,2,1,0:T(8,128)S(1)}, f32[2,48,8,128]{3,2,1,0:T(8,128)S(1)}, u32[]{:S(2)}, u32[]{:S(2)}) collective-permute-start(f32[2,48,8,128]{3,2,1,0:T(8,128)S(1)} %constant_dynamic-update-slice_fusion), channel_id=1, source_target_pairs={{0,32},{32,0},{64,96},{96,64},{128,160},{160,128},{192,224},{224,1... | collective-permute-start | bytes 1179656 | tf_op jit(solution)/shard_map/ppermute | solution.py:281
  188.5 4.5 %collective-permute-start.21 = (f32[4,32,8,128]{3,2,1,0:T(8,128)S(1)}, f32[4,32,8,128]{3,2,1,0:T(8,128)S(1)}, u32[]{:S(2)}, u32[]{:S(2)}) collective-permute-start(f32[4,32,8,128]{3,2,1,0:T(8,128)S(1)} %pad_maximum_fusion.3), channel_id=1, source_target_pairs={{0,32},{32,0},{64,96},{96,64},{128,160},{160,128},{192,224},{224,1... | collective-permute-start | bytes 1572872 | tf_op jit(solution)/shard_map/ppermute | solution.py:281
  203.1 3.5 %collective-permute-start.25 = (f32[8,48,8,128]{3,2,1,0:T(8,128)S(1)}, f32[8,48,8,128]{3,2,1,0:T(8,128)S(1)}, u32[]{:S(2)}, u32[]{:S(2)}) collective-permute-start(f32[8,48,8,128]{3,2,1,0:T(8,128)S(1)} %get-tuple-element.84), channel_id=1, source_target_pairs={{0,32},{32,0},{64,96},{96,64},{128,160},{160,128},{192,224},{224,1... | collective-permute-start | bytes 4718600 | tf_op jit(solution)/shard_map/ppermute | solution.py:281
  206.9 18.1 %collective-permute-start.26 = (f32[2,48,8,128]{3,2,1,0:T(8,128)S(1)}, f32[2,48,8,128]{3,2,1,0:T(8,128)S(1)}, u32[]{:S(2)}, u32[]{:S(2)}) collective-permute-start(f32[2,48,8,128]{3,2,1,0:T(8,128)S(1)} %get-tuple-element.104), channel_id=1, source_target_pairs={{0,64},{32,96},{64,128},{96,160},{128,192},{160,224},{192,0},{224,... | collective-permute-start | bytes 1179656 | tf_op jit(solution)/shard_map/ppermute | solution.py:285
  208.0 20.0 %collective-permute-start.27 = (f32[2,48,8,128]{3,2,1,0:T(8,128)S(1)}, f32[2,48,8,128]{3,2,1,0:T(8,128)S(1)}, u32[]{:S(2)}, u32[]{:S(2)}) collective-permute-start(f32[2,48,8,128]{3,2,1,0:T(8,128)S(1)} %get-tuple-element.103), channel_id=1, source_target_pairs={{0,192},{32,224},{64,0},{96,32},{128,64},{160,96},{192,128},{224,1... | collective-permute-start | bytes 1179656 | tf_op jit(solution)/shard_map/ppermute | solution.py:289
  228.0 11.5 %collective-permute-start.28 = (f32[1,48,8,128]{3,2,1,0:T(8,128)S(1)}, f32[1,48,8,128]{3,2,1,0:T(8,128)S(1)}, u32[]{:S(2)}, u32[]{:S(2)}) collective-permute-start(f32[1,48,8,128]{3,2,1,0:T(8,128)S(1)} %get-tuple-element.87), channel_id=1, source_target_pairs={{0,64},{32,96},{64,128},{96,160},{128,192},{160,224},{192,0},{224,... | collective-permute-start | bytes 589832 | tf_op jit(solution)/shard_map/ppermute | solution.py:285
  229.6 11.8 %collective-permute-start.29 = (f32[1,48,8,128]{3,2,1,0:T(8,128)S(1)}, f32[1,48,8,128]{3,2,1,0:T(8,128)S(1)}, u32[]{:S(2)}, u32[]{:S(2)}) collective-permute-start(f32[1,48,8,128]{3,2,1,0:T(8,128)S(1)} %get-tuple-element.88), channel_id=1, source_target_pairs={{0,192},{32,224},{64,0},{96,32},{128,64},{160,96},{192,128},{224,1... | collective-permute-start | bytes 589832 | tf_op jit(solution)/shard_map/ppermute | solution.py:289
  241.5 12.2 %collective-permute-start.30 = (f32[2,48,8,128]{3,2,1,0:T(8,128)S(1)}, f32[2,48,8,128]{3,2,1,0:T(8,128)S(1)}, u32[]{:S(2)}, u32[]{:S(2)}) collective-permute-start(f32[2,48,8,128]{3,2,1,0:T(8,128)S(1)} %fusion.2.refs_6_), channel_id=1, source_target_pairs={{0,64},{32,96},{64,128},{96,160},{128,192},{160,224},{192,0},{224,... | collective-permute-start | bytes 1179656 | tf_op jit(solution)/shard_map/ppermute | solution.py:285
  245.3 10.8 %collective-permute-start.31 = (f32[2,48,8,128]{3,2,1,0:T(8,128)S(1)}, f32[2,48,8,128]{3,2,1,0:T(8,128)S(1)}, u32[]{:S(2)}, u32[]{:S(2)}) collective-permute-start(f32[2,48,8,128]{3,2,1,0:T(8,128)S(1)} %fusion.2.refs_6_), channel_id=1, source_target_pairs={{0,192},{32,224},{64,0},{96,32},{128,64},{160,96},{192,128},{224,1... | collective-permute-start | bytes 1179656 | tf_op jit(solution)/shard_map/ppermute | solution.py:289
  256.1 6.7 %collective-permute-start.32 = (f32[1,48,8,128]{3,2,1,0:T(8,128)S(1)}, f32[1,48,8,128]{3,2,1,0:T(8,128)S(1)}, u32[]{:S(2)}, u32[]{:S(2)}) collective-permute-start(f32[1,48,8,128]{3,2,1,0:T(8,128)S(1)} %get-tuple-element.146.refs_3_), channel_id=1, source_target_pairs={{0,64},{32,96},{64,128},{96,160},{128,192},{160,224},{192,0},{224,... | collective-permute-start | bytes 589832 | tf_op jit(solution)/shard_map/ppermute | solution.py:285
  257.7 11.9 %collective-permute-start.35 = (f32[6,48,8,128]{3,2,1,0:T(8,128)S(1)}, f32[6,48,8,128]{3,2,1,0:T(8,128)S(1)}, u32[]{:S(2)}, u32[]{:S(2)}) collective-permute-start(f32[6,48,8,128]{3,2,1,0:T(8,128)S(1)} %pad_maximum_fusion.2), channel_id=1, source_target_pairs={{0,32},{32,0},{64,96},{96,64},{128,160},{160,128},{192,224},{224,1... | collective-permute-start | bytes 3538952 | tf_op jit(solution)/shard_map/ppermute | solution.py:281
  259.8 7.5 %collective-permute-start.33 = (f32[1,48,8,128]{3,2,1,0:T(8,128)S(1)}, f32[1,48,8,128]{3,2,1,0:T(8,128)S(1)}, u32[]{:S(2)}, u32[]{:S(2)}) collective-permute-start(f32[1,48,8,128]{3,2,1,0:T(8,128)S(1)} %get-tuple-element.148.refs_1_), channel_id=1, source_target_pairs={{0,192},{32,224},{64,0},{96,32},{128,64},{160,96},{192,128},{224,1... | collective-permute-start | bytes 589832 | tf_op jit(solution)/shard_map/ppermute | solution.py:289
  267.4 2.2 collective-permute-start.34
  (11 other events, 27.8 us)
